TPU v7x, 32 devices: a whole 2x2x4 slice. The times are simulated.
32 devices in a mesh: graph: 2 (over core), edge: 16 (over z, y, x).
Axes of the slice: x: 2, y: 2, z: 4, core: 2. Of those that a mesh axis runs over, the one named last changes fastest.
Arguments:
- states: bfloat16 [2, 2048, 128], P(None, ('graph', 'edge')), may hold values from -6 to 6
- edge_feats: bfloat16 [2, 16, 32768], P(None, None, ('graph', 'edge')), may hold values from -6 to 6
- source_index: int32 [2, 32768], P(None, ('graph', 'edge')), may hold values from 0 to 1023, as said below
- target_index: int32 [2, 32768], P(None, ('graph', 'edge')), may hold values from 0 to 1023, as said below
- w_edge_in: bfloat16 [16, 128], replicated, may hold values from -1.5 to 1.5
- b_edge_in: float32 [128], replicated, may hold values from -3 to 3
- w_edge_out: bfloat16 [128, 16384], replicated, may hold values from -0.01953125 to 0.01953125
- b_edge_out: float32 [16384], replicated, may hold values from -0.125 to 0.125
- w_input: bfloat16 [128, 384], replicated, may hold values from -0.5 to 0.5
- w_hidden: bfloat16 [128, 384], replicated, may hold values from -0.5 to 0.5
- b_input: float32 [384], replicated, may hold values from -3 to 3
- b_hidden: float32 [384], replicated, may hold values from -3 to 3
- cotangent: bfloat16 [2, 2048, 128], P(None, ('graph', 'edge')), may hold values from -6 to 6
Outputs:
- new_states: bfloat16 [2, 2048, 128], P(None, ('graph', 'edge'))
- state_grad: bfloat16 [2, 2048, 128], P(None, ('graph', 'edge'))
- feat_grad: bfloat16 [2, 16, 32768], P(None, None, ('graph', 'edge'))
- w_edge_in_grad: float32 [16, 128], replicated
- b_edge_in_grad: float32 [128], replicated
- w_edge_out_grad: float32 [128, 16384], replicated
- b_edge_out_grad: float32 [16384], replicated
- w_input_grad: float32 [128, 384], replicated
- w_hidden_grad: float32 [128, 384], replicated
- b_input_grad: float32 [384], replicated
- b_hidden_grad: float32 [384], replicated
Inputs may be any that keep to these rules, and one draw needn't show every extreme that they name: `source_index`: atom numbers within the edge's group: an edge of group g reads rows g * 1024 + index of the state arrays. Source and target of an edge lie in the same molecule; each device's 64 rows of a group hold whole molecules, runs of consecutive atom numbers taken cyclically within those rows, one of min(100, 32) atoms and the others of at most 18. Among the 1024 edges of one device in one micro-batch, at most 128 have their target atom among the rows of any one device, and exactly 128 for each device that they reach. `target_index`: same numbering and molecules as source_index; the same bound of 128 edges of one device with target atoms on one device holds for source atoms.
All inputs are finite; a program needn't handle non-finite values.
Results may differ from a plain program's by a relative error of at most 0.015.
Values may be sent and summed in bfloat16 or wider, within the bound.
No kernel may reach another device: no remote copies, remote signals or barrier semaphores. Data moves between devices by JAX's collectives and lax.ppermute only.
A program may use at most 128 MiB of HBM per device.

v0:
```python
import functools

import jax
import jax.numpy as jnp
from jax import lax
from jax.experimental import pallas as pl
from jax.experimental.pallas import tpu as pltpu
from jax.sharding import PartitionSpec as P

F32 = jnp.float32
BF16 = jnp.bfloat16
LANES = 128
PIECE = 4
GROUP = 12
MIB = 1024 * 1024


def dot(first, second, dims=((1,), (0,))):
    return lax.dot_general(first, second, (dims, ((), ())), preferred_element_type=F32)


def dot_nt(first, second):
    return dot(first, second, ((1,), (1,)))


def row_ids(shape):
    return lax.broadcasted_iota(jnp.int32, shape, 0)


def col_ids(shape):
    return lax.broadcasted_iota(jnp.int32, shape, 1)


def full_call(kernel, out_shape, scratch=(), limit=16, **more):
    return pl.pallas_call(
        kernel,
        out_shape=out_shape,
        scratch_shapes=scratch,
        compiler_params=pltpu.CompilerParams(vmem_limit_bytes=limit * MIB),
        **more,
    )


def ranks_of(owner, owners):
    hits = (row_ids((owners, owner.shape[1])) == owner).astype(F32)
    before = (row_ids((LANES, LANES)) < col_ids((LANES, LANES))).astype(BF16)
    seen = jnp.zeros((owners, 1), F32)
    ranks = []
    for start in range(0, owner.shape[1], LANES):
        part = hits[:, start : start + LANES]
        place = dot(part.astype(BF16), before) + seen
        ranks.append(jnp.sum(part * place, axis=0, keepdims=True))
        seen = seen + jnp.sum(part, axis=1, keepdims=True)
    return hits, jnp.concatenate(ranks, axis=1)


def route_kernel(own_rows, src_ref, dst_ref, feat_ref, out_ref):
    owners, rows, cap = out_ref.shape
    batches, feats, edges = feat_ref.shape
    shift = own_rows.bit_length() - 1
    marks = [jnp.zeros((16, cap), F32)] * owners
    for batch in range(batches):
        source, target = src_ref[batch : batch + 1], dst_ref[batch : batch + 1]
        owner = source >> shift
        hits, rank = ranks_of(owner, owners)
        spots = (row_ids((cap, edges)) == rank.astype(jnp.int32)).astype(BF16)
        line = row_ids((16, edges)) - 3 * batch
        first = owner << shift
        extra = jnp.where(line == 0, source - first, jnp.where(line == 1, target - first, 1))
        extra = jnp.where((line >= 0) & (line < 3), extra, 0).astype(F32)
        load = jnp.concatenate([feat_ref[batch].astype(F32), extra], axis=0)
        masked = [(load * hits[part : part + 1]).astype(BF16) for part in range(owners)]
        out = dot_nt(jnp.concatenate(masked, axis=0), spots)
        for part in range(owners):
            tile = out[part * (feats + 16) : (part + 1) * (feats + 16)]
            out_ref[part, batch * feats : (batch + 1) * feats] = tile[:feats].astype(BF16)
            marks[part] = marks[part] + tile[feats:]
    for part in range(owners):
        out_ref[part, batches * feats :] = marks[part].astype(BF16)


def unroute_kernel(own_rows, src_ref, back_ref, out_ref):
    owners, batches, rows, cap = back_ref.shape
    edges = src_ref.shape[1]
    shift = own_rows.bit_length() - 1
    for batch in range(batches):
        hits, rank = ranks_of(src_ref[batch : batch + 1] >> shift, owners)
        spots = (row_ids((cap, edges)) == rank.astype(jnp.int32)).astype(BF16)
        parts = [back_ref[part, batch] for part in range(owners)]
        spread = dot(jnp.concatenate(parts, axis=0), spots)
        total = jnp.zeros((rows, edges), F32)
        for part in range(owners):
            total = total + spread[part * rows : (part + 1) * rows] * hits[part : part + 1]
        out_ref[batch] = total.astype(BF16)


def edge_piece(batches, order_ref, edge_ref, piece, batch):
    some = [edge_ref[order_ref[batch, PIECE * piece + k]] for k in range(PIECE)]
    block = jnp.concatenate(some, axis=1)
    feats, marks = block[batch * 16 : (batch + 1) * 16], block[batches * 16 :].astype(F32)
    source = marks[3 * batch : 3 * batch + 1].astype(jnp.int32)
    target = marks[3 * batch + 1 : 3 * batch + 2].astype(jnp.int32)
    held = marks[3 * batch + 2 : 3 * batch + 3]
    code = ((target >> 3) & 3) * 128 + (target >> 5) * 64 + source
    code = jnp.where(held > 0.5, code, -1)
    pairs = (row_ids((512, block.shape[1])) == code).astype(BF16)
    low = row_ids((8, block.shape[1])) == (target & 7)
    return feats, held, pairs, low


def order_blocks(batches, edge_ref, order_ref):
    blocks = edge_ref.shape[0]
    for batch in range(batches):
        front, back = jnp.int32(0), jnp.int32(blocks - 1)
        row = 3 * batch + 2
        for block in range(blocks):
            marks = edge_ref[block, batches * 16 :].astype(F32)
            held = jnp.max(marks[row : row + 1]) > 0.5
            order_ref[batch, jnp.where(held, front, back)] = jnp.int32(block)
            step = held.astype(jnp.int32)
            front, back = front + step, back - (1 - step)
        order_ref[batch, blocks] = front


def first_layer(w_in_ref, b_in_ref):
    bias = jnp.broadcast_to(b_in_ref[...].reshape(1, -1), (8, b_in_ref.shape[0]))
    return w_in_ref[...].astype(F32).T.astype(BF16), bias.T[:, :1]


def gates_of(mail_low, level, w_x, w_h, b_x, b_h):
    width = level.shape[1]
    from_mail = dot(mail_low, w_x[...]) + b_x[...].reshape(1, -1)
    from_state = dot(level, w_h[...]) + b_h[...].reshape(1, -1)
    reset = jax.nn.sigmoid(from_mail[:, :width] + from_state[:, :width])
    update = jax.nn.sigmoid(from_mail[:, width : 2 * width] + from_state[:, width : 2 * width])
    state_part = from_state[:, 2 * width :]
    candidate = jnp.tanh(from_mail[:, 2 * width :] + reset * state_part)
    return reset, update, candidate, state_part


def doubled(level):
    blank = jnp.zeros_like(level)
    return jnp.concatenate(
        [jnp.concatenate([level, blank], axis=1), jnp.concatenate([blank, level], axis=1)], axis=0
    )


def bias_blocks(bias_ref, tail_ref):
    tail_ref[...] = jnp.zeros_like(tail_ref)
    high = bias_ref[...].astype(BF16)
    tail_ref[0] = high
    tail_ref[1] = (bias_ref[...] - high.astype(F32)).astype(BF16)


def turned(tile):
    size = tile.shape[1]
    eye = (row_ids((size, size)) == col_ids((size, size))).astype(F32).astype(BF16)
    return dot_nt(eye, tile).astype(BF16)


def weights_of(w_ref, tail_ref, number):
    units = w_ref.shape[0]
    blocks = []
    for unit in range(number * GROUP, (number + 1) * GROUP):
        blocks.append(w_ref[unit] if unit < units else tail_ref[unit - units])
    return jnp.concatenate(blocks, axis=1)


def pulled_rows(pulled, half):
    rows = []
    for start in range(0, pulled.shape[1], LANES):
        tile = pulled[:, start : start + LANES]
        rows.append(jnp.concatenate([tile[:half], tile[half:]], axis=1))
    return jnp.concatenate(rows, axis=0)


def main_kernel(
    where_ref,
    edge_ref,
    state_ref,
    cot_ref,
    w_in_ref,
    b_in_ref,
    w_far,
    bias_ref,
    w_x,
    w_h,
    b_x,
    b_h,
    new_ref,
    kept_first,
    kept_last,
    given_first,
    given_last,
    g_far,
    level_ref,
    dm_ref,
    base_ref,
    order_ref,
    rows_ref,
    hid_ref,
    acc_ref,
    g_ref,
    p_ref,
    w_ref,
    tail_ref,
    sum_ref,
    sum_sems,
    sems,
):
    fetch = pltpu.make_async_copy(w_far, w_ref, sems.at[0])
    fetch.start()
    blocks = edge_ref.shape[0]
    batches = g_ref.shape[0]
    hidden_units = hid_ref.shape[0]
    units = acc_ref.shape[0] // 8
    own = state_ref.shape[0] // batches
    half = own // 2
    span = GROUP * half
    wide = GROUP * LANES
    chunks = units // GROUP
    order_blocks(batches, edge_ref, order_ref)
    bias_blocks(bias_ref, tail_ref)
    w_in, b_in = first_layer(w_in_ref, b_in_ref)

    for batch in range(batches):
        acc_ref[...] = jnp.zeros_like(acc_ref)

        def add_piece(piece, carry):
            feats, held, pairs, low = edge_piece(batches, order_ref, edge_ref, piece, batch)
            pre = dot(w_in, feats) + b_in
            hid_ref[...] = (pre * jax.nn.sigmoid(pre)).astype(BF16).astype(F32)
            ones = jnp.where(low, 1.0, 0.0)
            parts = []
            for unit in range(0, hidden_units, 2):
                two = [jnp.where(low, hid_ref[unit + k : unit + k + 1], 0.0) for k in range(2)]
                parts.append(jnp.concatenate(two, axis=0).astype(BF16))
            parts.append(jnp.concatenate([ones, ones], axis=0).astype(BF16))
            parts.append(jnp.zeros((8 * (units - hidden_units - 2), pre.shape[1]), BF16))
            acc_ref[...] += dot_nt(jnp.concatenate(parts, axis=0), pairs)
            return carry

        lax.fori_loop(0, (order_ref[batch, blocks] + PIECE - 1) // PIECE, add_piece, 0)

        def place(step, carry):
            for four in range(3):
                rows = []
                for k in range(4):
                    for part in range(4):
                        start = pl.multiple_of(step * 96 + four * 32 + k * 8, 8)
                        rows.append(acc_ref[pl.ds(start, 8), part * LANES : (part + 1) * LANES])
                at = pl.ds(pl.multiple_of((step * 3 + four) * LANES, LANES), LANES)
                g_ref[batch, at, :] = jnp.concatenate(rows, axis=0).astype(BF16)
            return carry

        lax.fori_loop(0, units // 12, place, 0)

    def forward(step, level):
        two = [doubled(level[batch * own : (batch + 1) * own]) for batch in range(batches)]
        mail = jnp.zeros((batches * own, LANES), F32)
        base = step * batches * own
        for number in range(chunks):
            for batch in range(batches):
                out = dot(g_ref[batch, number * span : (number + 1) * span, :], two[batch])
                out = out.astype(BF16)
                for unit in range(GROUP):
                    lane = number * wide + unit * LANES
                    for part in range(2):
                        row = base + batch * own + part * half
                        p_ref[row : row + half, lane : lane + LANES] = out[
                            unit * half : (unit + 1) * half, part * LANES : (part + 1) * LANES
                        ]
            rows = p_ref[base : base + batches * own, number * wide : (number + 1) * wide]
            mail = mail + dot_nt(rows, weights_of(w_ref, tail_ref, number))
        return mail

    def backward(d_mail):
        sums = [jnp.zeros((LANES, 2 * LANES), F32) for batch in range(batches)]
        for number in range(chunks):
            pulled = dot(d_mail, weights_of(w_ref, tail_ref, number)).astype(BF16)
            at = slice(number * span, (number + 1) * span)
            for batch in range(batches):
                tall = pulled_rows(pulled[batch * own : (batch + 1) * own], half)
                sums[batch] = sums[batch] + dot(turned(g_ref[batch, at, :]), tall)
        return jnp.concatenate([one[:own, :LANES] + one[own:, LANES:] for one in sums], axis=0)

    weights = (w_x, w_h, b_x, b_h)
    level_zero = state_ref[...]
    state_zero = level_zero.astype(F32)
    leave = pltpu.make_async_copy(g_ref, g_far, sems.at[1])
    leave.start()
    fetch.wait()
    mail_zero = forward(0, level_zero).astype(BF16)
    gates_zero = gates_of(mail_zero, level_zero, *weights)
    state_one = (1.0 - gates_zero[1]) * gates_zero[2] + gates_zero[1] * state_zero
    level_one = state_one.astype(BF16)
    mail_one = forward(1, level_one).astype(BF16)
    gates_one = gates_of(mail_one, level_one, *weights)
    new_ref[...] = ((1.0 - gates_one[1]) * gates_one[2] + gates_one[1] * state_one).astype(BF16)

    def gru_back(d_next, gates, current):
        reset, update, candidate, state_part = gates
        d_cand = d_next * (1.0 - update) * (1.0 - candidate * candidate)
        d_reset = d_cand * state_part * reset * (1.0 - reset)
        d_update = d_next * (current - candidate) * update * (1.0 - update)
        dg_mail = jnp.concatenate([d_reset, d_update, d_cand], axis=1).astype(BF16)
        dg_state = jnp.concatenate([d_reset, d_update, d_cand * reset], axis=1).astype(BF16)
        d_mail = dot_nt(dg_mail, w_x[...]).astype(BF16)
        d_current = d_next * update + dot_nt(dg_state, w_h[...])
        return dg_mail, dg_state, d_mail, d_current

    dgm_one, dgs_one, dm_one, d_state = gru_back(cot_ref[...].astype(F32), gates_one, state_one)
    d_state = d_state + backward(dm_one)
    dgm_zero, dgs_zero, dm_zero, d_state = gru_back(d_state, gates_zero, state_zero)
    base_ref[...] = d_state
    level_ref[...] = jnp.concatenate([level_zero, level_one], axis=1)
    dm_ref[...] = jnp.concatenate([dm_zero, dm_one], axis=1)

    def both(first, second):
        return jnp.concatenate([first.astype(F32), second.astype(F32)], axis=0)

    dms = both(dm_zero, dm_one).T
    mails, levels = both(mail_zero, mail_one), both(level_zero, level_one)
    dgm, dgs = both(dgm_zero, dgm_one), both(dgs_zero, dgs_one)
    width = dgm.shape[1]
    rows_ref[...] = jnp.zeros_like(rows_ref)
    for k, one in enumerate((dgm, dgs)):
        total = jnp.sum(one, axis=0, keepdims=True)
        for part in range(3):
            row = 24 + 3 * k + part
            rows_ref[row : row + 1, :] = total[:, part * LANES : (part + 1) * LANES]
    small = jnp.concatenate(
        [
            dot(dms.astype(BF16), p_ref[:, hidden_units * LANES : (hidden_units + 1) * LANES]),
            dot(mails.T.astype(BF16), dgm.astype(BF16)),
            dot(levels.T.astype(BF16), dgs.astype(BF16)),
            jnp.zeros((2 * own, LANES), F32),
        ],
        axis=1,
    )

    def sorted_rows(value):
        rows = value.shape[0] // 2
        upper, lower = value[:rows], value[rows:]
        halves = [jnp.where(where_ref[0] == k, upper, lower) for k in range(2)]
        parts = []
        for k, one in enumerate(halves):
            first, second = one[: rows // 2], one[rows // 2 :]
            parts += [jnp.where(where_ref[1 + k] == side, second, first) for side in range(2)]
        return jnp.concatenate(parts, axis=0).astype(BF16)

    dms, small = sorted_rows(dms), sorted_rows(small)
    rows_in, groups, tall, wide_out = kept_first.shape
    taken = wide_out - 2 * LANES
    moves = []
    for group in range(groups):
        out = dot(dms, p_ref[:, group * taken : (group + 1) * taken]).astype(BF16)
        extra = small[:, group * 2 * LANES : (group + 1) * 2 * LANES]
        for k, ref in enumerate((given_first, kept_first, given_last, kept_last)):
            for row in range(rows_in):
                at = ((2, 0, 3, 1)[k] * rows_in + row) * tall
                sum_ref[k, row, group, :, :taken] = out[at : at + tall]
                sum_ref[k, row, group, :, taken:] = extra[at : at + tall]
                moves.append(
                    pltpu.make_async_copy(
                        sum_ref.at[k, row, group], ref.at[row, group], sum_sems.at[k, row, group]
                    )
                )
                moves[-1].start()
    for move in moves:
        move.wait()
    leave.wait()


def edge_kernel(
    batch,
    order_ref,
    edge_ref,
    g_far,
    level_ref,
    dm_ref,
    base_ref,
    w_in_ref,
    b_in_ref,
    w_far,
    bias_ref,
    before_ref,
    feat_before,
    grad_ref,
    feat_ref,
    win_ref,
    tail_ref,
    dg_ref,
    w_ref,
    g_ref,
    sems,
):
    blocks = edge_ref.shape[0]
    batches = order_ref.shape[0]
    hidden_units = w_in_ref.shape[1]
    chunks = (hidden_units + tail_ref.shape[0]) // GROUP
    own, width = grad_ref.shape
    half = own // 2
    fetches = []
    for number in range(chunks):
        some = pl.ds(number * GROUP, min(GROUP, hidden_units - number * GROUP))
        rows = pl.ds(number * GROUP * half, GROUP * half)
        fetches += [
            pltpu.make_async_copy(w_far.at[some], w_ref.at[some], sems.at[number, 0]),
            pltpu.make_async_copy(
                g_far.at[batch, rows], g_ref.at[rows], sems.at[number, 1]
            ),
        ]
    for fetch in fetches:
        fetch.start()
    mine = slice(batch * own, (batch + 1) * own)
    bias_blocks(bias_ref, tail_ref)

    pulls = [dm_ref[mine, step * width : (step + 1) * width] for step in range(2)]
    levels = [doubled(level_ref[mine, step * width : (step + 1) * width]) for step in range(2)]
    levels = jnp.concatenate(levels, axis=1)
    total = jnp.zeros((2 * own, 2 * width), F32)
    both = jnp.concatenate(pulls, axis=0)
    for number in range(chunks):
        fetches[2 * number].wait()
        fetches[2 * number + 1].wait()
        pulled = dot(both, weights_of(w_ref, tail_ref, number)).astype(BF16)
        talls = [pulled_rows(pulled[k * own : (k + 1) * own], half) for k in range(2)]
        at = slice(number * GROUP * half, (number + 1) * GROUP * half)
        total = total + dot(turned(g_ref[at, :]), talls[0])
        d_pair = dot_nt(jnp.concatenate(talls, axis=1), levels)
        for unit in range(0, GROUP, 2):
            row = (number * GROUP + unit) * 8
            for part in range(half // 8):
                pair = [
                    d_pair[(unit + k) * half + part * 8 : (unit + k) * half + part * 8 + 8]
                    for k in range(2)
                ]
                dg_ref[row : row + 16, part * LANES : (part + 1) * LANES] = jnp.concatenate(
                    pair, axis=0
                ).astype(BF16)
    grad = base_ref[mine] + total[:own, :width] + total[own:, width:]
    grad_ref[...] = grad.astype(BF16)

    w_in, b_in = first_layer(w_in_ref, b_in_ref)
    fold = (col_ids((hidden_units, 8 * hidden_units)) >> 3) == row_ids(
        (hidden_units, 8 * hidden_units)
    )
    fold = fold.astype(F32).astype(BF16)
    feat_ref[...] = jnp.zeros_like(feat_ref)
    if batch > 0:
        feat_ref[:, : batch * 16] = feat_before[...]

    def one_piece(piece, sums):
        feats, held, pairs, low = edge_piece(batches, order_ref, edge_ref, piece, batch)
        pre = dot(w_in, feats) + b_in
        sig = jax.nn.sigmoid(pre)
        spread = dot(dg_ref[: 8 * hidden_units], pairs)
        spread = spread.reshape(hidden_units, 8, pre.shape[1])
        spread = jnp.where(low[None], spread, 0.0).reshape(8 * hidden_units, pre.shape[1])
        d_hidden = dot(fold, spread.astype(BF16))
        d_pre = (d_hidden * sig * (1.0 + pre * (1.0 - sig))).astype(BF16)
        out = dot(w_in_ref[...], d_pre).astype(BF16)
        for k in range(PIECE):
            at = order_ref[batch, PIECE * piece + k]
            feat_ref[at, batch * 16 :] = out[:, k * LANES : (k + 1) * LANES]
        ones = jnp.where(row_ids((16, pre.shape[1])) == 0, held, 0.0).astype(BF16)
        return sums + dot_nt(jnp.concatenate([feats, ones], axis=0), d_pre)

    win_ref[...] = lax.fori_loop(
        0, (order_ref[batch, blocks] + PIECE - 1) // PIECE, one_piece, before_ref[...]
    )


def add_kernel(first_ref, second_ref, out_ref):
    out_ref[...] = (first_ref[...].astype(F32) + second_ref[...].astype(F32)).astype(BF16)


def copy_kernel(in_ref, out_ref):
    out_ref[...] = in_ref[...]


def rows_kernel(first_ref, second_ref, out_ref, rows_ref):
    parts, tall, wide = first_ref.shape
    main = wide // LANES - 2
    for part in range(parts):
        total = first_ref[part].astype(F32) + second_ref[part].astype(F32)
        for block in range(main):
            rows_ref[pl.ds(block, tall, stride=main), :] = total[
                :, block * LANES : (block + 1) * LANES
            ]
        for k in range(2):
            start = tall * (main + k)
            rows_ref[start : start + tall, :] = total[:, (main + k) * LANES : (main + k + 1) * LANES]
        out_ref[part] = rows_ref[...].astype(BF16)


def rows_of(first, second):
    parts, tall, wide = first.shape
    shape = (tall * (wide // LANES), LANES)
    return full_call(
        rows_kernel,
        jax.ShapeDtypeStruct((parts,) + shape, BF16),
        (pltpu.VMEM(shape, F32),),
        cost_estimate=cost(1),
    )(first, second)


def place_kernel(tall, count, carried, *refs):
    at_ref, pieces = refs[0], refs[1 : 1 + count]
    outs = refs[1 + count + carried : 6 + count + carried]
    big_ref, little_ref, sems = refs[6 + count + carried :]
    d_w, d_bias, d_x, d_h, d_rest = outs
    waits = []
    slot = 0
    for k, piece in enumerate(pieces):
        chunks, rows_in, lanes = piece.shape
        main = rows_in // tall - 2
        for chunk in range(chunks):
            code = at_ref[k] ^ chunk
            line, part = code >> 2, code & 3
            at = pl.ds(pl.multiple_of(line * tall, 8), tall)
            rows = piece[chunk].astype(F32)
            for row in range(tall):
                big_ref[slot, :, row * lanes : (row + 1) * lanes] = rows[row * main : (row + 1) * main]
            copy = pltpu.make_async_copy(
                big_ref.at[slot],
                d_w.at[
                    pl.ds(pl.multiple_of(part * main, 8), main),
                    pl.ds(pl.multiple_of(line * (tall * lanes), LANES), tall * lanes),
                ],
                sems.at[slot, 0],
            )
            copy.start()
            waits.append(copy)

            for side in range(2):
                start = tall * (main + side)
                little_ref[slot, side] = rows[start : start + tall]

                def move(target, lane):
                    lane = jnp.maximum(lane, 0) * lanes
                    to = pl.ds(pl.multiple_of(jnp.minimum(lane, target.shape[1] - lanes), LANES), lanes)
                    return pltpu.make_async_copy(
                        little_ref.at[slot, side], target.at[at, to], sems.at[slot, 1 + side]
                    )

                block = 2 * part + side
                to_x, to_h = move(d_x, block - 1), move(d_h, block - 4)
                alone = move((d_bias, d_rest)[side], 0)
                lone = block == 7 * side
                pl.when(lone)(alone.start)
                pl.when((block > 0) & (block < 4))(to_x.start)
                pl.when((block > 3) & (block < 7))(to_h.start)
                waits.append(alone)
            slot += 1
    for copy in waits:
        copy.wait()


def cost(micros):
    return pl.CostEstimate(
        flops=int(micros * 1e9), bytes_accessed=int(micros * 3e6), transcendentals=0
    )


def place_pieces(tall, at, pieces, shapes, before=()):
    count = len(pieces)
    chunks, rows_in, lanes = pieces[0].shape
    slots = count * chunks
    vmem = pl.BlockSpec(memory_space=pltpu.VMEM)
    hbm = pl.BlockSpec(memory_space=pl.ANY)
    return pl.pallas_call(
        functools.partial(place_kernel, tall, count, len(before)),
        out_shape=shapes,
        in_specs=[pl.BlockSpec(memory_space=pltpu.SMEM)] + [vmem] * count + [hbm] * len(before),
        out_specs=[hbm] * len(shapes),
        scratch_shapes=(
            pltpu.VMEM((slots, rows_in // tall - 2, tall * lanes), F32),
            pltpu.VMEM((slots, 2, tall, lanes), F32),
            pltpu.SemaphoreType.DMA((slots, 3)),
        ),
        input_output_aliases={1 + count + k: k for k in range(len(before))},
        cost_estimate=cost(0.1),
        compiler_params=pltpu.CompilerParams(vmem_limit_bytes=16 * MIB),
    )(at, *pieces, *before)


def body(
    states,
    edge_feats,
    source_index,
    target_index,
    w_edge_in,
    b_edge_in,
    w_edge_out,
    b_edge_out,
    w_input,
    w_hidden,
    b_input,
    b_hidden,
    cotangent,
):
    batches, own, width = states.shape
    edges = source_index.shape[1]
    owners = lax.axis_size("edge")
    cap = max(2, 2 * edges // owners)
    feat_count, units = w_edge_in.shape

    sent = full_call(
        functools.partial(route_kernel, own),
        jax.ShapeDtypeStruct((owners, batches * feat_count + 16, cap), BF16),
        limit=60,
    )(source_index, target_index, edge_feats)
    edge_data = lax.all_to_all(sent, "edge", 0, 0, tiled=True)
    merge = max(1, LANES // cap)
    if merge > 1:
        edge_data = edge_data.reshape(owners // merge, merge, -1, cap).transpose(0, 2, 1, 3)
        edge_data = edge_data.reshape(owners // merge, -1, merge * cap)

    w_mats = w_edge_out.reshape(units, width, width)
    padded = (units + 2 + GROUP - 1) // GROUP * GROUP

    tall = width // 8
    pairs = own // 2
    blocks = edge_data.shape[0]
    core = lax.axis_index("graph")
    spot = lax.axis_index("edge")
    orders = ((0, 1, 2, 3), (2, 0, 1, 3))

    def bit(side, step):
        first, second = [(spot >> orders[k][step]) & 1 for k in range(2)]
        return jnp.where(side == 0, first, second)

    where = jnp.stack([core, bit(core, 0), bit(1 - core, 0)])
    smem = pl.BlockSpec(memory_space=pltpu.SMEM)
    vmem = pl.BlockSpec(memory_space=pltpu.VMEM)
    far = pl.BlockSpec(memory_space=pltpu.HBM)
    bias = b_edge_out.reshape(width, width)
    quarter = jax.ShapeDtypeStruct((2, 4, tall, (units // 4 + 2) * width), BF16)
    new_states, *sums, g_pairs, levels, d_mails, base, order, first = full_call(
        main_kernel,
        (
            jax.ShapeDtypeStruct((batches * own, width), BF16),
            *[quarter] * 4,
            jax.ShapeDtypeStruct((batches, padded * pairs, LANES), BF16),
            jax.ShapeDtypeStruct((batches * own, 2 * width), BF16),
            jax.ShapeDtypeStruct((batches * own, 2 * width), BF16),
            jax.ShapeDtypeStruct((batches * own, width), F32),
            jax.ShapeDtypeStruct((batches, blocks + 1), jnp.int32),
            jax.ShapeDtypeStruct((32, width), F32),
        ),
        (
            pltpu.VMEM((units, PIECE * LANES), F32),
            pltpu.VMEM((padded * 8, 512), F32),
            pltpu.VMEM((batches, padded * pairs, LANES), BF16),
            pltpu.VMEM((2 * batches * own, padded * width), BF16),
            pltpu.VMEM((units, width, width), BF16),
            pltpu.VMEM((padded - units, width, width), BF16),
            pltpu.VMEM((4,) + quarter.shape, BF16),
            pltpu.SemaphoreType.DMA((4,) + quarter.shape[:2]),
            pltpu.SemaphoreType.DMA((2,)),
        ),
        limit=60,
        in_specs=[smem] + [vmem] * 5 + [far] + [vmem] * 5,
        out_specs=[vmem] + [far] * 5 + [vmem] * 3 + [smem, vmem],
    )(
        where,
        edge_data,
        states.reshape(batches * own, width),
        cotangent.reshape(batches * own, width),
        w_edge_in,
        b_edge_in,
        w_mats,
        bias,
        w_input,
        w_hidden,
        b_input,
        b_hidden,
    )

    cores = lax.axis_size("graph")

    def to_core(value):
        return lax.ppermute(value, "graph", [(0, 1), (1, 0)])

    def swap(value, masks):
        moves = []
        for side in range(cores):
            first = side * owners
            moves += [(first + k, first + (k ^ masks[side])) for k in range(owners)]
        return lax.ppermute(value, ("graph", "edge"), moves)

    def swap_step(value, step):
        return swap(value, [1 << orders[side][step] for side in range(cores)])

    def pick(value, number):
        return lax.dynamic_index_in_dim(value, number, 0, False)

    def added(terms):
        return sum(one.astype(F32) for one in terms)

    def after(value, *others):
        return lax.optimization_barrier((value, *others))[0]

    def edge_grads(batch, pairs_in, first, feats):
        return full_call(
            functools.partial(edge_kernel, batch),
            (
                jax.ShapeDtypeStruct((own, width), BF16),
                jax.ShapeDtypeStruct((blocks, (batch + 1) * feat_count, LANES), BF16),
                jax.ShapeDtypeStruct((32, units), F32),
            ),
            (
                pltpu.VMEM((padded - units, width, width), BF16),
                pltpu.VMEM((padded * 8, 512), BF16),
                pltpu.VMEM((units, width, width), BF16),
                pltpu.VMEM((padded * pairs, LANES), BF16),
                pltpu.SemaphoreType.DMA((padded // GROUP, 2)),
            ),
            limit=60,
            in_specs=[smem, vmem, far] + [vmem] * 5 + [far] + [vmem] * 3,
            cost_estimate=cost(9),
        )(
            order, edge_data, pairs_in, levels, d_mails, base,
            w_edge_in, b_edge_in, w_mats, bias, first, feats,
        )

    def both(big, small, step):
        return lax.optimization_barrier((swap_step(big, step), swap_step(small, step)))

    kept_first, kept_last, given_first, given_last = sums
    got_first, got_last = to_core(given_first), to_core(given_last)
    kept_first = full_call(
        copy_kernel, jax.ShapeDtypeStruct(kept_first.shape, BF16), cost_estimate=cost(1)
    )(kept_first)
    give = full_call(
        add_kernel, jax.ShapeDtypeStruct(kept_first.shape, BF16), cost_estimate=cost(1)
    )(kept_first, got_first)
    terms = [kept_last, got_last]
    state_grad, d_feats = [], b_edge_in
    for step in range(3):
        if step > 0:
            number = bit(core, step)
            give = added([pick(one, 1 - number) for one in terms]).astype(BF16)
            terms = [pick(one, number) for one in terms]
        if step == 2:
            got, small = both(give, first, step)
            first = first + small
        else:
            got = swap_step(give, step)
        if step < batches:
            grad, d_feats, first = edge_grads(step, after(g_pairs, give), first, d_feats)
            got = after(got, first)
            state_grad.append(grad)
        terms.append(got)
        if step == 0:
            terms = [one.reshape((2, 2, 2) + one.shape[2:]) for one in terms]
    total = added(terms).astype(BF16)
    for extra in range(3, owners.bit_length() - 1):
        masks = [1 << extra] * cores
        got, small = swap(total, masks), swap(first, masks)
        if extra < owners.bit_length() - 2:
            first = first + small
        if extra < owners.bit_length() - 2:
            total = added([total, got]).astype(BF16)
    held = rows_of(total, got)

    got, small = lax.optimization_barrier((swap_step(held, 2), small))
    first = first + small
    held = jnp.concatenate([held, got], axis=0)
    across = swap_step(held, 0)
    back = d_feats
    if merge > 1:
        back = back.reshape(blocks, -1, merge, cap).transpose(0, 2, 1, 3)
    back = after(back.reshape(owners, -1, cap), held)
    back = lax.all_to_all(back, "edge", 0, 0, tiled=True)

    near, more = both(held, first, 1)
    first = first + more
    last, more = swap_step(near, 0), swap_step(first, 0)
    near = after(near, back)

    feat_grad = full_call(
        functools.partial(unroute_kernel, own),
        jax.ShapeDtypeStruct((batches, feat_count, edges), BF16),
        cost_estimate=cost(0.1),
    )(source_index, back.reshape(owners, batches, feat_count, cap))

    shapes = tuple(
        jax.ShapeDtypeStruct(shape, F32)
        for shape in (
            (units, width * width),
            (width, width),
            (width, 3 * width),
            (width, 3 * width),
            (width, width),
        )
    )
    outs = ()
    for wave in (((held, 0),), ((near, 4), (across, 8)), ((last, 12),)):
        at, pieces = [], []
        extra = (more, feat_grad) if wave[0][0] is last else ()
        ready = lax.optimization_barrier((outs, tuple(piece for piece, _ in wave), extra))
        outs, wave, extra = ready[0], zip(ready[1], [flips for _, flips in wave]), ready[2]
        for piece, flips in wave:
            for side, one in ((core, piece), (1 - core, to_core(piece))):
                code = side
                for step in range(3):
                    code = code * 2 + bit(side, step)
                at.append((code * 2) ^ flips)
                pieces.append(one)
        outs = place_pieces(tall, jnp.stack(at), pieces, shapes, outs)
    more, feat_grad = extra
    first = first + more
    first_sum = first + to_core(first)
    d_w, d_bias, d_x, d_h, _ = outs
    return (
        new_states.reshape(batches, own, width),
        jnp.stack(state_grad),
        feat_grad,
        first_sum[:feat_count],
        first_sum[feat_count],
        d_w,
        d_bias.reshape(-1),
        d_x,
        d_h,
        first_sum[24:27].reshape(-1),
        first_sum[27:30].reshape(-1),
    )


def solution(mesh):
    spread = ("graph", "edge")
    rows = P(None, spread, None)
    edges = P(None, spread)
    feats = P(None, None, spread)
    in_specs = (rows, feats, edges, edges) + (P(),) * 8 + (rows,)
    out_specs = (rows, rows, feats) + (P(),) * 8
    return jax.shard_map(
        body,
        mesh=mesh,
        in_specs=in_specs,
        out_specs=out_specs,
        check_vma=False,
    )
```

profile of v0, /device:TPU:0, one launch (start us, length us, event | category | flops | bytes accessed | tf_op | source)
XLA Modules:
  0.0 136.8 jit_solution(7622359324604921290)
XLA Ops:
  0.6 3.0 %shard_map.212 = bf16[16,48,128]{2,1,0:T(8,128)(2,1)} custom-call(s32[2,1024]{1,0:T(2,128)} %src_ref.3, s32[2,1024]{1,0:T(2,128)} %dst_ref.1, bf16[2,16,1024]{2,1,0:T(8,128)(2,1)} %feat_ref.1), custom_call_target="tpu_custom_call" | custom-call | tf_op jit(solution)/shard_map/pallas_call | solution.py:610
  3.7 8.3 %all-to-all-start = ((bf16[16,48,128]{2,1,0:T(8,128)(2,1)}), bf16[16,48,128]{2,1,0:T(8,128)(2,1)S(1)}, u32[]{:S(2)}, u32[]{:S(2)}) async-start(bf16[16,48,128]{2,1,0:T(8,128)(2,1)} %shard_map.212), calls=%async_computation | async-start | bytes 393216 | tf_op jit(solution)/shard_map/all_to_all | solution.py:615
  12.0 5.4 %copy.34 = bf16[16,8,128,128]{3,2,1,0:T(8,128)(2,1)} copy(bf16[16,8,128,128]{3,1,2,0:T(8,128)(2,1)} %bitcast.46) | data formatting | bytes 8388608
  18.1 2.6 %all-to-all-done.edge_ref = bf16[16,48,128]{2,1,0:T(8,128)(2,1)S(1)} async-done(((bf16[16,48,128]{2,1,0:T(8,128)(2,1)}), bf16[16,48,128]{2,1,0:T(8,128)(2,1)S(1)}, u32[]{:S(2)}, u32[]{:S(2)}) %all-to-all-start) | async-done | bytes 196640 | tf_op jit(solution)/shard_map/all_to_all | solution.py:615
  21.3 19.2 %shard_map.213 = (bf16[128,128]{1,0:T(8,128)(2,1)}, bf16[2,4,16,4352]{3,2,1,0:T(8,128)(2,1)}, bf16[2,4,16,4352]{3,2,1,0:T(8,128)(2,1)}, bf16[2,4,16,4352]{3,2,1,...) custom-call(s32[3]{0:T(128)} %pad_add_fusion.where_ref, ...), custom_call_target="tpu_custom_call" | custom-call | tf_op jit(solution)/shard_map/pallas_call | solution.py:641
  41.9 1.6 %collective-permute-done.second_ref = bf16[2,4,16,4352]{3,2,1,0:T(8,128)(2,1)S(1)} collective-permute-done((bf16[2,4,16,4352]{3,2,1,0:T(8,128)(2,1)}, bf16[2,4,16,4352]{3,2,1,0:T(8,128)(2,1)S(1)}, u32[]{:S(2)}, u32[]{:S(2)}) %collective-permute-start) | collective-permute-done | bytes 1114144 | tf_op jit(solution)/shard_map/ppermute | solution.py:685
  43.8 1.9 %collective-permute-start.2 = (bf16[2,4,16,4352]{3,2,1,0:T(8,128)(2,1)S(1)}, bf16[2,4,16,4352]{3,2,1,0:T(8,128)(2,1)S(1)}, u32[]{:S(2)}, u32[]{:S(2)}) collective-permute-start(bf16[2,4,16,4352]{3,2,1,0:T(8,128)(2,1)S(1)} %shard_map.215), channel_id=1, source_target_pairs={{0,1},{1,0},{2,3},{3,2},{4,5},{5,4},{6,7},{7,6},{8,9},{9,8},{10,11... | collective-permute-start | bytes 3342344 | tf_op jit(solution)/shard_map/ppermute | solution.py:692
  46.4 12.7 %shard_map.216 = (bf16[64,128]{1,0:T(8,128)(2,1)}, bf16[16,16,128]{2,1,0:T(8,128)(2,1)}, f32[32,128]{1,0:T(8,128)}) custom-call(s32[2,17]{1,0:T(2,128)} %get-tuple-element.70.order_ref, bf16[16,48,128]{2,1,0:T(8,128)(2,1)} %copy-done.3, bf16[2,4224,128]{2,1,0:T(8,128)(2,1)} %get-tuple-element.84.g_far, bf16[128,256]{1,0:T(8,128)(2,1)} %get-tuple-element.75.level_ref, ...), custom_call_target="tpu_custom_call" | custom-call | flops 8999999488 | bytes 27000000 | tf_op jit(solution)/shard_map/pallas_call | solution.py:707
  61.6 10.3 %shard_map.217 = (bf16[64,128]{1,0:T(8,128)(2,1)}, bf16[16,32,128]{2,1,0:T(8,128)(2,1)}, f32[32,128]{1,0:T(8,128)}) custom-call(s32[2,17]{1,0:T(2,128)} %get-tuple-element.70.order_ref, bf16[16,48,128]{2,1,0:T(8,128)(2,1)} %copy-done.3, bf16[2,4224,128]{2,1,0:T(8,128)(2,1)} %get-tuple-element.84.g_far, bf16[128,256]{1,0:T(8,128)(2,1)} %get-tuple-element.75.level_ref, ...), custom_call_target="tpu_custom_call" | custom-call | flops 8999999488 | bytes 27000000 | tf_op jit(solution)/shard_map/pallas_call | solution.py:707
  73.0 4.1 %collective-permute-start.4 = (bf16[2,16,4352]{2,1,0:T(8,128)(2,1)S(1)}, bf16[2,16,4352]{2,1,0:T(8,128)(2,1)S(1)}, u32[]{:S(2)}, u32[]{:S(2)}) collective-permute-start(bf16[2,16,4352]{2,1,0:T(8,128)(2,1)S(1)} %fusion.1), channel_id=1, source_target_pairs={{0,4},{1,5},{2,6},{3,7},{4,0},{5,1},{6,2},{7,3},{8,12},{9,13},{10,... | collective-permute-start | bytes 835592 | tf_op jit(solution)/shard_map/ppermute | solution.py:692
  77.2 4.6 %collective-permute-done.5 = f32[32,128]{1,0:T(8,128)S(1)} collective-permute-done((f32[32,128]{1,0:T(8,128)S(1)}, f32[32,128]{1,0:T(8,128)S(1)}, u32[]{:S(2)}, u32[]{:S(2)}) %collective-permute-start.5) | collective-permute-done | bytes 16416 | tf_op jit(solution)/shard_map/ppermute | solution.py:692
  83.8 12.9 %collective-permute-done.6.second_ref = bf16[2,16,4352]{2,1,0:T(8,128)(2,1)S(1)} collective-permute-done((bf16[2,16,4352]{2,1,0:T(8,128)(2,1)S(1)}, bf16[2,16,4352]{2,1,0:T(8,128)(2,1)S(1)}, u32[]{:S(2)}, u32[]{:S(2)}) %collective-permute-start.6) | collective-permute-done | bytes 278560 | tf_op jit(solution)/shard_map/ppermute | solution.py:692
  97.2 2.9 %collective-permute-start.8 = (f32[32,128]{1,0:T(8,128)S(1)}, f32[32,128]{1,0:T(8,128)S(1)}, u32[]{:S(2)}, u32[]{:S(2)}) collective-permute-start(f32[32,128]{1,0:T(8,128)S(1)} %add.165), channel_id=1, source_target_pairs={{0,8},{1,9},{2,10},{3,11},{4,12},{5,13},{6,14},{7,15},{8,0},{9,1},... | collective-permute-start | bytes 49160 | tf_op jit(solution)/shard_map/ppermute | solution.py:692
  100.1 1.9 %collective-permute-done.8 = f32[32,128]{1,0:T(8,128)S(1)} collective-permute-done((f32[32,128]{1,0:T(8,128)S(1)}, f32[32,128]{1,0:T(8,128)S(1)}, u32[]{:S(2)}, u32[]{:S(2)}) %collective-permute-start.8) | collective-permute-done | bytes 16416 | tf_op jit(solution)/shard_map/ppermute | solution.py:692
  102.0 2.1 %collective-permute-done.7 = bf16[2,544,128]{2,1,0:T(8,128)(2,1)S(1)} collective-permute-done((bf16[2,544,128]{2,1,0:T(8,128)(2,1)S(1)}, bf16[2,544,128]{2,1,0:T(8,128)(2,1)S(1)}, u32[]{:S(2)}, u32[]{:S(2)}) %collective-permute-start.7) | collective-permute-done | bytes 278560 | tf_op jit(solution)/shard_map/ppermute | solution.py:692
  104.8 1.7 %collective-permute-start.12 = (bf16[4,544,128]{2,1,0:T(8,128)(2,1)S(1)}, bf16[4,544,128]{2,1,0:T(8,128)(2,1)S(1)}, u32[]{:S(2)}, u32[]{:S(2)}) collective-permute-start(bf16[4,544,128]{2,1,0:T(8,128)(2,1)S(1)} %pad_maximum_fusion.refs_1_), channel_id=1, source_target_pairs={{0,1},{1,0},{2,3},{3,2},{4,5},{5,4},{6,7},{7,6},{8,9},{9,8},{10,11... | collective-permute-start | bytes 1671176 | tf_op jit(solution)/shard_map/ppermute | solution.py:692
  106.5 4.4 %all-to-all-start.1 = ((bf16[16,32,128]{2,1,0:T(8,128)(2,1)}), bf16[16,32,128]{2,1,0:T(8,128)(2,1)S(1)}, u32[]{:S(2)}, u32[]{:S(2)}) async-start(bf16[16,32,128]{2,1,0:T(8,128)(2,1)} %get-tuple-element.100), calls=%async_computation.1 | async-start | bytes 262144 | tf_op jit(solution)/shard_map/all_to_all | solution.py:777
  110.9 2.0 %collective-permute-start.11 = (f32[32,128]{1,0:T(8,128)S(1)}, f32[32,128]{1,0:T(8,128)S(1)}, u32[]{:S(2)}, u32[]{:S(2)}) collective-permute-start(f32[32,128]{1,0:T(8,128)S(1)} %add.166), channel_id=1, source_target_pairs={{0,2},{1,3},{2,0},{3,1},{4,6},{5,7},{6,4},{7,5},{8,10},{9,11},{10,... | collective-permute-start | bytes 49160 | tf_op jit(solution)/shard_map/ppermute | solution.py:692
  113.0 1.9 %collective-permute-done.11 = f32[32,128]{1,0:T(8,128)S(1)} collective-permute-done((f32[32,128]{1,0:T(8,128)S(1)}, f32[32,128]{1,0:T(8,128)S(1)}, u32[]{:S(2)}, u32[]{:S(2)}) %collective-permute-start.11) | collective-permute-done | bytes 16416 | tf_op jit(solution)/shard_map/ppermute | solution.py:692
  114.9 4.2 %all-to-all-done.1 = bf16[16,32,128]{2,1,0:T(8,128)(2,1)S(1)} async-done(((bf16[16,32,128]{2,1,0:T(8,128)(2,1)}), bf16[16,32,128]{2,1,0:T(8,128)(2,1)S(1)}, u32[]{:S(2)}, u32[]{:S(2)}) %all-to-all-start.1) | async-done | bytes 131104 | tf_op jit(solution)/shard_map/all_to_all | solution.py:777
  119.1 2.1 %shard_map.219 = (f32[128,16384]{1,0:T(8,128)}, f32[128,128]{1,0:T(8,128)}, f32[128,384]{1,0:T(8,128)}, f32[128,384]{1,0:T(8,128)}, f32[128,128]{1,0:T(8,128)S(1)}) custom-call(s32[2]{0:T(128)S(1)} %pad_add_fusion.2.refs_0_, bf16[4,544,128]{2,1,0:T(8,128)(2,1)S(1)} %pad_maximum_fusion.refs_1_, bf16[4,544,128]{2,1,0:T(8,128)(2,1)S(1)} %collective-permute-done.9.refs_2_), custom_call_target="tpu_custom_call" | custom-call | flops 100000000 | bytes 300000 | tf_op jit(solution)/shard_map/pallas_call | solution.py:573
  125.4 3.1 %shard_map.220 = (f32[128,16384]{1,0:T(8,128)}, f32[128,128]{1,0:T(8,128)}, f32[128,384]{1,0:T(8,128)}, f32[128,384]{1,0:T(8,128)}, f32[128,128]{1,0:T(8,128)S(1)}) custom-call(s32[4]{0:T(128)S(1)} %pad_add_fusion.1.refs_0_, ...), custom_call_target="tpu_custom_call", output_to_operand_aliasing={{0}: (5, {}), {1}: (6, {}), {2}: (7, {}), {3}: (8, {}), {4}... | custom-call | flops 100000000 | bytes 300000 | tf_op jit(solution)/shard_map/pallas_call | solution.py:573
  128.5 3.0 %collective-permute-done.16 = f32[32,128]{1,0:T(8,128)S(1)} collective-permute-done((f32[32,128]{1,0:T(8,128)S(1)}, f32[32,128]{1,0:T(8,128)S(1)}, u32[]{:S(2)}, u32[]{:S(2)}) %collective-permute-start.16) | collective-permute-done | bytes 16416 | tf_op jit(solution)/shard_map/ppermute | solution.py:692
  134.5 2.1 %shard_map.222 = (f32[128,16384]{1,0:T(8,128)}, f32[128,128]{1,0:T(8,128)}, f32[128,384]{1,0:T(8,128)}, f32[128,384]{1,0:T(8,128)}, f32[128,128]{1,0:T(8,128)S(1)}) custom-call(s32[2]{0:T(128)S(1)} %pad_add_fusion.3.refs_0_, ...), custom_call_target="tpu_custom_call", output_to_operand_aliasing={{0}: (3, {}), {1}: (4, {}), {2}: (5, {}), {3}: (6, {}), {4}... | custom-call | flops 100000000 | bytes 300000 | tf_op jit(solution)/shard_map/pallas_call | solution.py:573
  (61 shorter events, 17.6 us)
Async XLA Ops:
  3.7 17.0 %all-to-all-start = ((bf16[16,48,128]{2,1,0:T(8,128)(2,1)}), bf16[16,48,128]{2,1,0:T(8,128)(2,1)S(1)}, u32[]{:S(2)}, u32[]{:S(2)}) async-start(bf16[16,48,128]{2,1,0:T(8,128)(2,1)} %shard_map.212), calls=%async_computation | async-start | bytes 393216 | tf_op jit(solution)/shard_map/all_to_all | solution.py:615
  40.5 3.0 %collective-permute-start = (bf16[2,4,16,4352]{3,2,1,0:T(8,128)(2,1)}, bf16[2,4,16,4352]{3,2,1,0:T(8,128)(2,1)S(1)}, u32[]{:S(2)}, u32[]{:S(2)}) collective-permute-start(bf16[2,4,16,4352]{3,2,1,0:T(8,128)(2,1)} %get-tuple-element.73), channel_id=1, source_target_pairs={{0,16},{16,0},{1,17},{17,1},{2,18},{18,2},{3,19},{19,3},{4,20},{20... | collective-permute-start | bytes 3342344 | tf_op jit(solution)/shard_map/ppermute | solution.py:685
  43.8 15.6 %collective-permute-start.2 = (bf16[2,4,16,4352]{3,2,1,0:T(8,128)(2,1)S(1)}, bf16[2,4,16,4352]{3,2,1,0:T(8,128)(2,1)S(1)}, u32[]{:S(2)}, u32[]{:S(2)}) collective-permute-start(bf16[2,4,16,4352]{3,2,1,0:T(8,128)(2,1)S(1)} %shard_map.215), channel_id=1, source_target_pairs={{0,1},{1,0},{2,3},{3,2},{4,5},{5,4},{6,7},{7,6},{8,9},{9,8},{10,11... | collective-permute-start | bytes 3342344 | tf_op jit(solution)/shard_map/ppermute | solution.py:692
  45.7 13.7 %collective-permute-start.1 = (bf16[2,4,16,4352]{3,2,1,0:T(8,128)(2,1)}, bf16[2,4,16,4352]{3,2,1,0:T(8,128)(2,1)}, u32[]{:S(2)}, u32[]{:S(2)}) collective-permute-start(bf16[2,4,16,4352]{3,2,1,0:T(8,128)(2,1)} %get-tuple-element.81), channel_id=1, source_target_pairs={{0,16},{16,0},{1,17},{17,1},{2,18},{18,2},{3,19},{19,3},{4,20},{20... | collective-permute-start | bytes 3342344 | tf_op jit(solution)/shard_map/ppermute | solution.py:685
  46.4 12.9 %copy-start.2 = (bf16[2,4,16,4352]{3,2,1,0:T(8,128)(2,1)S(1)}, bf16[2,4,16,4352]{3,2,1,0:T(8,128)(2,1)}, u32[]{:S(2)}) copy-start(bf16[2,4,16,4352]{3,2,1,0:T(8,128)(2,1)} %get-tuple-element.80) | copy-start | bytes 3342340
  60.6 11.2 %collective-permute-start.3 = (bf16[2,2,16,4352]{3,2,1,0:T(8,128)(2,1)S(1)}, bf16[2,2,16,4352]{3,2,1,0:T(8,128)(2,1)S(1)}, u32[]{:S(2)}, u32[]{:S(2)}) collective-permute-start(bf16[2,2,16,4352]{3,2,1,0:T(8,128)(2,1)S(1)} %fusion), channel_id=1, source_target_pairs={{0,2},{1,3},{2,0},{3,1},{4,6},{5,7},{6,4},{7,5},{8,10},{9,11},{10,... | collective-permute-start | bytes 1671176 | tf_op jit(solution)/shard_map/ppermute | solution.py:692
  73.0 8.8 %collective-permute-start.4 = (bf16[2,16,4352]{2,1,0:T(8,128)(2,1)S(1)}, bf16[2,16,4352]{2,1,0:T(8,128)(2,1)S(1)}, u32[]{:S(2)}, u32[]{:S(2)}) collective-permute-start(bf16[2,16,4352]{2,1,0:T(8,128)(2,1)S(1)} %fusion.1), channel_id=1, source_target_pairs={{0,4},{1,5},{2,6},{3,7},{4,0},{5,1},{6,2},{7,3},{8,12},{9,13},{10,... | collective-permute-start | bytes 835592 | tf_op jit(solution)/shard_map/ppermute | solution.py:692
  77.1 4.7 %collective-permute-start.5 = (f32[32,128]{1,0:T(8,128)S(1)}, f32[32,128]{1,0:T(8,128)S(1)}, u32[]{:S(2)}, u32[]{:S(2)}) collective-permute-start(f32[32,128]{1,0:T(8,128)S(1)} %copy-done.4), channel_id=1, source_target_pairs={{0,4},{1,5},{2,6},{3,7},{4,0},{5,1},{6,2},{7,3},{8,12},{9,13},{10,... | collective-permute-start | bytes 49160 | tf_op jit(solution)/shard_map/ppermute | solution.py:692
  82.9 13.8 %collective-permute-start.6 = (bf16[2,16,4352]{2,1,0:T(8,128)(2,1)S(1)}, bf16[2,16,4352]{2,1,0:T(8,128)(2,1)S(1)}, u32[]{:S(2)}, u32[]{:S(2)}) collective-permute-start(bf16[2,16,4352]{2,1,0:T(8,128)(2,1)S(1)} %fusion.3.first_ref), channel_id=1, source_target_pairs={{0,8},{1,9},{2,10},{3,11},{4,12},{5,13},{6,14},{7,15},{8,0},{9,1},... | collective-permute-start | bytes 835592 | tf_op jit(solution)/shard_map/ppermute | solution.py:692
  97.1 7.0 %collective-permute-start.7 = (bf16[2,544,128]{2,1,0:T(8,128)(2,1)S(1)}, bf16[2,544,128]{2,1,0:T(8,128)(2,1)S(1)}, u32[]{:S(2)}, u32[]{:S(2)}) collective-permute-start(bf16[2,544,128]{2,1,0:T(8,128)(2,1)S(1)} %shard_map.218), channel_id=1, source_target_pairs={{0,4},{1,5},{2,6},{3,7},{4,0},{5,1},{6,2},{7,3},{8,12},{9,13},{10,... | collective-permute-start | bytes 835592 | tf_op jit(solution)/shard_map/ppermute | solution.py:692
  97.2 26.8 %copy-start = (s32[2,1024]{1,0:T(2,128)S(1)}, s32[2,1024]{1,0:T(2,128)}, u32[]{:S(2)}) copy-start(s32[2,1024]{1,0:T(2,128)} %src_ref.3) | copy-start | bytes 24580
  97.2 4.8 %collective-permute-start.8 = (f32[32,128]{1,0:T(8,128)S(1)}, f32[32,128]{1,0:T(8,128)S(1)}, u32[]{:S(2)}, u32[]{:S(2)}) collective-permute-start(f32[32,128]{1,0:T(8,128)S(1)} %add.165), channel_id=1, source_target_pairs={{0,8},{1,9},{2,10},{3,11},{4,12},{5,13},{6,14},{7,15},{8,0},{9,1},... | collective-permute-start | bytes 49160 | tf_op jit(solution)/shard_map/ppermute | solution.py:692
  104.1 10.8 %collective-permute-start.10 = (bf16[4,544,128]{2,1,0:T(8,128)(2,1)S(1)}, bf16[4,544,128]{2,1,0:T(8,128)(2,1)S(1)}, u32[]{:S(2)}, u32[]{:S(2)}) collective-permute-start(bf16[4,544,128]{2,1,0:T(8,128)(2,1)S(1)} %pad_maximum_fusion.refs_1_), channel_id=1, source_target_pairs={{0,2},{1,3},{2,0},{3,1},{4,6},{5,7},{6,4},{7,5},{8,10},{9,11},{10,... | collective-permute-start | bytes 1671176 | tf_op jit(solution)/shard_map/ppermute | solution.py:692
  104.8 14.3 %collective-permute-start.9 = (bf16[4,544,128]{2,1,0:T(8,128)(2,1)S(1)}, bf16[4,544,128]{2,1,0:T(8,128)(2,1)S(1)}, u32[]{:S(2)}, u32[]{:S(2)}) collective-permute-start(bf16[4,544,128]{2,1,0:T(8,128)(2,1)S(1)} %pad_maximum_fusion.refs_1_), channel_id=1, source_target_pairs={{0,16},{16,0},{1,17},{17,1},{2,18},{18,2},{3,19},{19,3},{4,20},{20... | collective-permute-start | bytes 1671176 | tf_op jit(solution)/shard_map/ppermute | solution.py:685
  104.8 16.5 %collective-permute-start.12 = (bf16[4,544,128]{2,1,0:T(8,128)(2,1)S(1)}, bf16[4,544,128]{2,1,0:T(8,128)(2,1)S(1)}, u32[]{:S(2)}, u32[]{:S(2)}) collective-permute-start(bf16[4,544,128]{2,1,0:T(8,128)(2,1)S(1)} %pad_maximum_fusion.refs_1_), channel_id=1, source_target_pairs={{0,1},{1,0},{2,3},{3,2},{4,5},{5,4},{6,7},{7,6},{8,9},{9,8},{10,11... | collective-permute-start | bytes 1671176 | tf_op jit(solution)/shard_map/ppermute | solution.py:692
  106.5 12.6 %all-to-all-start.1 = ((bf16[16,32,128]{2,1,0:T(8,128)(2,1)}), bf16[16,32,128]{2,1,0:T(8,128)(2,1)S(1)}, u32[]{:S(2)}, u32[]{:S(2)}) async-start(bf16[16,32,128]{2,1,0:T(8,128)(2,1)} %get-tuple-element.100), calls=%async_computation.1 | async-start | bytes 262144 | tf_op jit(solution)/shard_map/all_to_all | solution.py:777
  110.9 4.0 %collective-permute-start.11 = (f32[32,128]{1,0:T(8,128)S(1)}, f32[32,128]{1,0:T(8,128)S(1)}, u32[]{:S(2)}, u32[]{:S(2)}) collective-permute-start(f32[32,128]{1,0:T(8,128)S(1)} %add.166), channel_id=1, source_target_pairs={{0,2},{1,3},{2,0},{3,1},{4,6},{5,7},{6,4},{7,5},{8,10},{9,11},{10,... | collective-permute-start | bytes 49160 | tf_op jit(solution)/shard_map/ppermute | solution.py:692
  121.2 4.2 %collective-permute-start.13 = (bf16[4,544,128]{2,1,0:T(8,128)(2,1)S(1)}, bf16[4,544,128]{2,1,0:T(8,128)(2,1)S(1)}, u32[]{:S(2)}, u32[]{:S(2)}) collective-permute-start(bf16[4,544,128]{2,1,0:T(8,128)(2,1)S(1)} %collective-permute-done.10.refs_1_), channel_id=1, source_target_pairs={{0,16},{16,0},{1,17},{17,1},{2,18},{18,2},{3,19},{19,3},{4,20},{20... | collective-permute-start | bytes 1671176 | tf_op jit(solution)/shard_map/ppermute | solution.py:685
  121.3 4.1 %collective-permute-start.14 = (bf16[4,544,128]{2,1,0:T(8,128)(2,1)S(1)}, bf16[4,544,128]{2,1,0:T(8,128)(2,1)S(1)}, u32[]{:S(2)}, u32[]{:S(2)}) collective-permute-start(bf16[4,544,128]{2,1,0:T(8,128)(2,1)S(1)} %collective-permute-done.12.refs_3_), channel_id=1, source_target_pairs={{0,16},{16,0},{1,17},{17,1},{2,18},{18,2},{3,19},{19,3},{4,20},{20... | collective-permute-start | bytes 1671176 | tf_op jit(solution)/shard_map/ppermute | solution.py:685
  121.8 9.7 %collective-permute-start.15 = (bf16[4,544,128]{2,1,0:T(8,128)(2,1)S(1)}, bf16[4,544,128]{2,1,0:T(8,128)(2,1)S(1)}, u32[]{:S(2)}, u32[]{:S(2)}) collective-permute-start(bf16[4,544,128]{2,1,0:T(8,128)(2,1)S(1)} %collective-permute-done.10.refs_1_), channel_id=1, source_target_pairs={{0,1},{1,0},{2,3},{3,2},{4,5},{5,4},{6,7},{7,6},{8,9},{9,8},{10,11... | collective-permute-start | bytes 1671176 | tf_op jit(solution)/shard_map/ppermute | solution.py:692
  122.7 8.9 %collective-permute-start.16 = (f32[32,128]{1,0:T(8,128)S(1)}, f32[32,128]{1,0:T(8,128)S(1)}, u32[]{:S(2)}, u32[]{:S(2)}) collective-permute-start(f32[32,128]{1,0:T(8,128)S(1)} %add.167), channel_id=1, source_target_pairs={{0,1},{1,0},{2,3},{3,2},{4,5},{5,4},{6,7},{7,6},{8,9},{9,8},{10,11... | collective-permute-start | bytes 49160 | tf_op jit(solution)/shard_map/ppermute | solution.py:692
  125.4 6.7 %copy-start.6 = (bf16[64,128]{1,0:T(8,128)(2,1)S(1)}, bf16[64,128]{1,0:T(8,128)(2,1)}, u32[]{:S(2)}) copy-start(bf16[64,128]{1,0:T(8,128)(2,1)} %get-tuple-element.86) | copy-start | bytes 49156
  131.5 1.2 collective-permute-start.17
  131.6 2.9 %collective-permute-start.18 = (bf16[4,544,128]{2,1,0:T(8,128)(2,1)S(1)}, bf16[4,544,128]{2,1,0:T(8,128)(2,1)S(1)}, u32[]{:S(2)}, u32[]{:S(2)}) collective-permute-start(bf16[4,544,128]{2,1,0:T(8,128)(2,1)S(1)} %collective-permute-done.15.refs_1_), channel_id=1, source_target_pairs={{0,16},{16,0},{1,17},{17,1},{2,18},{18,2},{3,19},{19,3},{4,20},{20... | collective-permute-start | bytes 1671176 | tf_op jit(solution)/shard_map/ppermute | solution.py:685
  (4 other events, 13.9 us)
where the time goes:
time: 138 us; the launch traced here: 137 us
  Pallas kernels  54.6 us (40%)
  waiting for transfers between devices  35.1 us (25%)
  starting transfers between devices  31.9 us (23%)
  local copies, waits for them, and re-layouts  9.09 us (7%)
  other arithmetic  5 us (4%)
    ppermute x12, waiting for transfers between devices, swap(): return lax.ppermute(value, ('graph', 'edge'), moves)  26.7 us
    pallas_call x2, Pallas kernels, edge_grads(): full_call(functools.partial(edge_kernel, batch), (jax.ShapeDtypeStruct((o...  23 us
    pallas_call x1, Pallas kernels, body(): full_call(main_kernel, (jax.ShapeDtypeStruct((batches * own, width), BF16...  19.2 us
    ppermute x12, starting transfers between devices, swap(): return lax.ppermute(value, ('graph', 'edge'), moves)  17.2 us
    all_to_all x1, starting transfers between devices, body(): edge_data = lax.all_to_all(sent, 'edge', 0, 0, tiled=True)  8.31 us
    unnamed x15, local copies, waits for them, and re-layouts  7.39 us
    pallas_call x3, Pallas kernels, place_pieces(): pl.pallas_call(functools.partial(place_kernel, tall, count, len(before)),...  7.34 us
    all_to_all x1, starting transfers between devices, body(): back = lax.all_to_all(back, 'edge', 0, 0, tiled=True)  4.41 us
  transfers between devices with their start and end apart: 21, of which 10 were waited for; matrix products, arithmetic and copies ran while one was open for 6% of the time, Pallas kernels for 22%

commit v1 on v0

--- a/solution.py
+++ b/solution.py
@@ -372,84 +372,14 @@
     leave.wait()
 
 
-def edge_kernel(
-    batch,
-    order_ref,
-    edge_ref,
-    g_far,
-    level_ref,
-    dm_ref,
-    base_ref,
-    w_in_ref,
-    b_in_ref,
-    w_far,
-    bias_ref,
-    before_ref,
-    feat_before,
-    grad_ref,
-    feat_ref,
-    win_ref,
-    tail_ref,
-    dg_ref,
-    w_ref,
-    g_ref,
-    sems,
-):
+def edge_sums(batch, batches, order_ref, edge_ref, dg_ref, w_in_ref, b_in_ref, feat_ref, before):
     blocks = edge_ref.shape[0]
-    batches = order_ref.shape[0]
     hidden_units = w_in_ref.shape[1]
-    chunks = (hidden_units + tail_ref.shape[0]) // GROUP
-    own, width = grad_ref.shape
-    half = own // 2
-    fetches = []
-    for number in range(chunks):
-        some = pl.ds(number * GROUP, min(GROUP, hidden_units - number * GROUP))
-        rows = pl.ds(number * GROUP * half, GROUP * half)
-        fetches += [
-            pltpu.make_async_copy(w_far.at[some], w_ref.at[some], sems.at[number, 0]),
-            pltpu.make_async_copy(
-                g_far.at[batch, rows], g_ref.at[rows], sems.at[number, 1]
-            ),
-        ]
-    for fetch in fetches:
-        fetch.start()
-    mine = slice(batch * own, (batch + 1) * own)
-    bias_blocks(bias_ref, tail_ref)
-
-    pulls = [dm_ref[mine, step * width : (step + 1) * width] for step in range(2)]
-    levels = [doubled(level_ref[mine, step * width : (step + 1) * width]) for step in range(2)]
-    levels = jnp.concatenate(levels, axis=1)
-    total = jnp.zeros((2 * own, 2 * width), F32)
-    both = jnp.concatenate(pulls, axis=0)
-    for number in range(chunks):
-        fetches[2 * number].wait()
-        fetches[2 * number + 1].wait()
-        pulled = dot(both, weights_of(w_ref, tail_ref, number)).astype(BF16)
-        talls = [pulled_rows(pulled[k * own : (k + 1) * own], half) for k in range(2)]
-        at = slice(number * GROUP * half, (number + 1) * GROUP * half)
-        total = total + dot(turned(g_ref[at, :]), talls[0])
-        d_pair = dot_nt(jnp.concatenate(talls, axis=1), levels)
-        for unit in range(0, GROUP, 2):
-            row = (number * GROUP + unit) * 8
-            for part in range(half // 8):
-                pair = [
-                    d_pair[(unit + k) * half + part * 8 : (unit + k) * half + part * 8 + 8]
-                    for k in range(2)
-                ]
-                dg_ref[row : row + 16, part * LANES : (part + 1) * LANES] = jnp.concatenate(
-                    pair, axis=0
-                ).astype(BF16)
-    grad = base_ref[mine] + total[:own, :width] + total[own:, width:]
-    grad_ref[...] = grad.astype(BF16)
-
     w_in, b_in = first_layer(w_in_ref, b_in_ref)
     fold = (col_ids((hidden_units, 8 * hidden_units)) >> 3) == row_ids(
         (hidden_units, 8 * hidden_units)
     )
     fold = fold.astype(F32).astype(BF16)
-    feat_ref[...] = jnp.zeros_like(feat_ref)
-    if batch > 0:
-        feat_ref[:, : batch * 16] = feat_before[...]
 
     def one_piece(piece, sums):
         feats, held, pairs, low = edge_piece(batches, order_ref, edge_ref, piece, batch)
@@ -463,12 +393,105 @@
         out = dot(w_in_ref[...], d_pre).astype(BF16)
         for k in range(PIECE):
             at = order_ref[batch, PIECE * piece + k]
-            feat_ref[at, batch * 16 :] = out[:, k * LANES : (k + 1) * LANES]
+            feat_ref[at, batch * 16 : (batch + 1) * 16] = out[:, k * LANES : (k + 1) * LANES]
         ones = jnp.where(row_ids((16, pre.shape[1])) == 0, held, 0.0).astype(BF16)
         return sums + dot_nt(jnp.concatenate([feats, ones], axis=0), d_pre)
 
-    win_ref[...] = lax.fori_loop(
-        0, (order_ref[batch, blocks] + PIECE - 1) // PIECE, one_piece, before_ref[...]
+    return lax.fori_loop(0, (order_ref[batch, blocks] + PIECE - 1) // PIECE, one_piece, before)
+
+
+def back_kernel(
+    order_ref,
+    edge_ref,
+    g_far,
+    level_ref,
+    dm_ref,
+    base_ref,
+    w_in_ref,
+    b_in_ref,
+    w_far,
+    bias_ref,
+    before_ref,
+    grad_ref,
+    feat_ref,
+    dg_ref,
+    win_ref,
+    tail_ref,
+    dg_first,
+    w_ref,
+    g_ref,
+    sems,
+):
+    batches, own, width = grad_ref.shape
+    hidden_units = w_in_ref.shape[1]
+    chunks = (hidden_units + tail_ref.shape[0]) // GROUP
+    half = own // 2
+    fetches = []
+    for number in range(chunks):
+        some = pl.ds(number * GROUP, min(GROUP, hidden_units - number * GROUP))
+        rows = pl.ds(number * GROUP * half, GROUP * half)
+        fetches += [
+            pltpu.make_async_copy(w_far.at[some], w_ref.at[some], sems.at[number, 0]),
+            pltpu.make_async_copy(g_far.at[:, rows], g_ref.at[:, rows], sems.at[number, 1]),
+        ]
+    for fetch in fetches:
+        fetch.start()
+    bias_blocks(bias_ref, tail_ref)
+    feat_ref[...] = jnp.zeros_like(feat_ref)
+
+    pulls, levels = [], []
+    for batch in range(batches):
+        mine = slice(batch * own, (batch + 1) * own)
+        pulls += [dm_ref[mine, step * width : (step + 1) * width] for step in range(2)]
+        both = [doubled(level_ref[mine, step * width : (step + 1) * width]) for step in range(2)]
+        levels.append(jnp.concatenate(both, axis=1))
+    pulls = jnp.concatenate(pulls, axis=0)
+    totals = [jnp.zeros((2 * own, 2 * width), F32) for batch in range(batches)]
+    for number in range(chunks):
+        fetches[2 * number].wait()
+        fetches[2 * number + 1].wait()
+        pulled = dot(pulls, weights_of(w_ref, tail_ref, number)).astype(BF16)
+        at = slice(number * GROUP * half, (number + 1) * GROUP * half)
+        for batch in range(batches):
+            target = dg_ref if batch else dg_first
+            talls = [
+                pulled_rows(pulled[(2 * batch + k) * own : (2 * batch + k + 1) * own], half)
+                for k in range(2)
+            ]
+            totals[batch] = totals[batch] + dot(turned(g_ref[batch, at, :]), talls[0])
+            d_pair = dot_nt(jnp.concatenate(talls, axis=1), levels[batch])
+            for unit in range(0, GROUP, 2):
+                row = (number * GROUP + unit) * 8
+                for part in range(half // 8):
+                    pair = [
+                        d_pair[(unit + k) * half + part * 8 : (unit + k) * half + part * 8 + 8]
+                        for k in range(2)
+                    ]
+                    target[row : row + 16, part * LANES : (part + 1) * LANES] = jnp.concatenate(
+                        pair, axis=0
+                    ).astype(BF16)
+    for batch in range(batches):
+        grad = base_ref[batch * own : (batch + 1) * own] + totals[batch][:own, :width]
+        grad_ref[batch] = (grad + totals[batch][own:, width:]).astype(BF16)
+    win_ref[...] = edge_sums(
+        0, batches, order_ref, edge_ref, dg_first, w_in_ref, b_in_ref, feat_ref, before_ref[...]
+    )
+
+
+def edge_kernel(
+    order_ref, edge_ref, dg_ref, feat_in, w_in_ref, b_in_ref, before_ref, feat_ref, win_ref
+):
+    feat_ref[...] = feat_in[...]
+    win_ref[...] = edge_sums(
+        1,
+        order_ref.shape[0],
+        order_ref,
+        edge_ref,
+        dg_ref,
+        w_in_ref,
+        b_in_ref,
+        feat_ref,
+        before_ref[...],
     )
 
 
@@ -703,31 +726,44 @@
     def after(value, *others):
         return lax.optimization_barrier((value, *others))[0]
 
-    def edge_grads(batch, pairs_in, first, feats):
+    feat_shape = jax.ShapeDtypeStruct((blocks, batches * feat_count, LANES), BF16)
+    win_shape = jax.ShapeDtypeStruct((32, units), F32)
+
+    def first_grads(pairs_in):
         return full_call(
-            functools.partial(edge_kernel, batch),
+            back_kernel,
             (
-                jax.ShapeDtypeStruct((own, width), BF16),
-                jax.ShapeDtypeStruct((blocks, (batch + 1) * feat_count, LANES), BF16),
-                jax.ShapeDtypeStruct((32, units), F32),
+                jax.ShapeDtypeStruct((batches, own, width), BF16),
+                feat_shape,
+                jax.ShapeDtypeStruct((padded * 8, 512), BF16),
+                win_shape,
             ),
             (
                 pltpu.VMEM((padded - units, width, width), BF16),
                 pltpu.VMEM((padded * 8, 512), BF16),
                 pltpu.VMEM((units, width, width), BF16),
-                pltpu.VMEM((padded * pairs, LANES), BF16),
+                pltpu.VMEM((batches, padded * pairs, LANES), BF16),
                 pltpu.SemaphoreType.DMA((padded // GROUP, 2)),
             ),
             limit=60,
-            in_specs=[smem, vmem, far] + [vmem] * 5 + [far] + [vmem] * 3,
-            cost_estimate=cost(9),
+            in_specs=[smem, vmem, far] + [vmem] * 5 + [far] + [vmem] * 2,
+            cost_estimate=cost(12),
         )(
             order, edge_data, pairs_in, levels, d_mails, base,
-            w_edge_in, b_edge_in, w_mats, bias, first, feats,
+            w_edge_in, b_edge_in, w_mats, bias, first,
         )
 
-    def both(big, small, step):
-        return lax.optimization_barrier((swap_step(big, step), swap_step(small, step)))
+    def second_grads(d_pairs, feats, before):
+        return full_call(
+            edge_kernel,
+            (feat_shape, win_shape),
+            in_specs=[smem] + [vmem] * 6,
+            cost_estimate=cost(5),
+        )(order, edge_data, d_pairs, feats, w_edge_in, b_edge_in, before)
+
+    def added_at(big, small, flip):
+        big, more = lax.optimization_barrier((big, swap(small, [flip] * cores)))
+        return big, small + more
 
     kept_first, kept_last, given_first, given_last = sums
     got_first, got_last = to_core(given_first), to_core(given_last)
@@ -738,36 +774,35 @@
         add_kernel, jax.ShapeDtypeStruct(kept_first.shape, BF16), cost_estimate=cost(1)
     )(kept_first, got_first)
     terms = [kept_last, got_last]
-    state_grad, d_feats = [], b_edge_in
     for step in range(3):
         if step > 0:
             number = bit(core, step)
             give = added([pick(one, 1 - number) for one in terms]).astype(BF16)
             terms = [pick(one, number) for one in terms]
+        got = swap_step(give, step)
+        if step == 0:
+            state_grad, d_feats, d_pairs, first = first_grads(after(g_pairs, give))
+            got = after(got, first)
+        if step == 1:
+            d_feats, first = second_grads(after(d_pairs, give), d_feats, first)
+            got = after(got, first)
         if step == 2:
-            got, small = both(give, first, step)
-            first = first + small
-        else:
-            got = swap_step(give, step)
-        if step < batches:
-            grad, d_feats, first = edge_grads(step, after(g_pairs, give), first, d_feats)
-            got = after(got, first)
-            state_grad.append(grad)
+            got, first = added_at(got, first, 4)
         terms.append(got)
         if step == 0:
             terms = [one.reshape((2, 2, 2) + one.shape[2:]) for one in terms]
     total = added(terms).astype(BF16)
     for extra in range(3, owners.bit_length() - 1):
-        masks = [1 << extra] * cores
-        got, small = swap(total, masks), swap(first, masks)
-        if extra < owners.bit_length() - 2:
-            first = first + small
+        got = swap(total, [1 << extra] * cores)
+        if extra > 3:
+            got, first = added_at(got, first, 1 << extra)
         if extra < owners.bit_length() - 2:
             total = added([total, got]).astype(BF16)
+    first = first + swap(first, [1] * cores)
+    got, first = added_at(got, first, 2)
     held = rows_of(total, got)
 
-    got, small = lax.optimization_barrier((swap_step(held, 2), small))
-    first = first + small
+    got, first = added_at(swap_step(held, 2), first, 8)
     held = jnp.concatenate([held, got], axis=0)
     across = swap_step(held, 0)
     back = d_feats
@@ -776,10 +811,17 @@
     back = after(back.reshape(owners, -1, cap), held)
     back = lax.all_to_all(back, "edge", 0, 0, tiled=True)
 
-    near, more = both(held, first, 1)
+    near = swap_step(held, 1)
+    near, more = lax.optimization_barrier((near, to_core(first)))
     first = first + more
-    last, more = swap_step(near, 0), swap_step(first, 0)
+    last = swap_step(near, 0)
     near = after(near, back)
+    small_outs = (
+        first[:feat_count],
+        first[feat_count],
+        first[24:27].reshape(-1),
+        first[27:30].reshape(-1),
+    )
 
     feat_grad = full_call(
         functools.partial(unroute_kernel, own),
@@ -798,35 +840,45 @@
         )
     )
     outs = ()
-    for wave in (((held, 0),), ((near, 4), (across, 8)), ((last, 12),)):
-        at, pieces = [], []
-        extra = (more, feat_grad) if wave[0][0] is last else ()
-        ready = lax.optimization_barrier((outs, tuple(piece for piece, _ in wave), extra))
-        outs, wave, extra = ready[0], zip(ready[1], [flips for _, flips in wave]), ready[2]
-        for piece, flips in wave:
-            for side, one in ((core, piece), (1 - core, to_core(piece))):
-                code = side
-                for step in range(3):
-                    code = code * 2 + bit(side, step)
-                at.append((code * 2) ^ flips)
-                pieces.append(one)
-        outs = place_pieces(tall, jnp.stack(at), pieces, shapes, outs)
-    more, feat_grad = extra
-    first = first + more
-    first_sum = first + to_core(first)
+    def place(outs, pieces):
+        at = []
+        for _, side, flips in pieces:
+            code = side
+            for step in range(3):
+                code = code * 2 + bit(side, step)
+            at.append((code * 2) ^ flips)
+        return place_pieces(tall, jnp.stack(at), [one for one, _, _ in pieces], shapes, outs)
+
+    outs = place((), [(held, core, 0), (to_core(held), 1 - core, 0)])
+    outs, near, across = lax.optimization_barrier((outs, near, across))
+    outs = place(
+        outs,
+        [
+            (near, core, 4),
+            (to_core(near), 1 - core, 4),
+            (across, core, 8),
+            (to_core(across), 1 - core, 8),
+        ],
+    )
+    outs, last, feat_grad, small_outs = lax.optimization_barrier(
+        (outs, last, feat_grad, small_outs)
+    )
+    other = to_core(last)
+    outs = place(outs, [(last, core, 12)])
+    outs = place(outs, [(other, 1 - core, 12)])
     d_w, d_bias, d_x, d_h, _ = outs
     return (
         new_states.reshape(batches, own, width),
-        jnp.stack(state_grad),
+        state_grad,
         feat_grad,
-        first_sum[:feat_count],
-        first_sum[feat_count],
+        small_outs[0],
+        small_outs[1],
         d_w,
         d_bias.reshape(-1),
         d_x,
         d_h,
-        first_sum[24:27].reshape(-1),
-        first_sum[27:30].reshape(-1),
+        small_outs[2],
+        small_outs[3],
     )
 
 

time: 138 us -> 134 us (0.971); the launches traced: 137 us -> 134 us
  starting transfers between devices: 31.9 us -> 24.6 us
  waiting for transfers between devices: 35.1 us -> 37.3 us
    ppermute x12, starting transfers between devices: 17.2 us -> 9.83 us  [swap(): return lax.ppermute(value, ('graph', 'edge'), moves)]
    ppermute x7, waiting for transfers between devices: 1.69 us -> 3.7 us  [to_core(): return lax.ppermute(value, 'graph', [(0, 1), (1, 0)])]
    pallas_call x1, Pallas kernels: 19.2 us -> 20.9 us  [body(): full_call(main_kernel, (jax.ShapeDtypeStruct((batches * own, width), BF16...]
    unnamed x15 -> x25, local copies, waits for them, and re-layouts: 7.39 us -> 8.39 us
    pallas_call x3 -> x4, Pallas kernels: 7.34 us -> 7.43 us  [place_pieces(): pl.pallas_call(functools.partial(place_kernel, tall, count, len(before)),...]
  transfers between devices with their start and end apart: 21 -> 21, of which waited for: 10 -> 13; matrix products, arithmetic and copies ran while one was open for 6% -> 6% of each run, Pallas kernels for 22% -> 22%
where the time goes in v1:
time: 134 us
  Pallas kernels  55.5 us (41%)
  waiting for transfers between devices  37.3 us (28%)
  starting transfers between devices  24.6 us (18%)
  local copies, waits for them, and re-layouts  10.1 us (8%)
  other arithmetic  5.59 us (4%)
    ppermute x12, waiting for transfers between devices, swap(): return lax.ppermute(value, ('graph', 'edge'), moves)  26 us
    pallas_call x1, Pallas kernels, body(): full_call(main_kernel, (jax.ShapeDtypeStruct((batches * own, width), BF16...  20.9 us
    pallas_call x1, Pallas kernels, first_grads(): full_call(back_kernel, (jax.ShapeDtypeStruct((batches, own, width), BF16)...  17.5 us
    ppermute x12, starting transfers between devices, swap(): return lax.ppermute(value, ('graph', 'edge'), moves)  9.83 us
    unnamed x25, local copies, waits for them, and re-layouts  8.39 us
    all_to_all x1, starting transfers between devices, body(): edge_data = lax.all_to_all(sent, 'edge', 0, 0, tiled=True)  8.31 us
    pallas_call x4, Pallas kernels, place_pieces(): pl.pallas_call(functools.partial(place_kernel, tall, count, len(before)),...  7.43 us
    all_to_all x1, starting transfers between devices, body(): back = lax.all_to_all(back, 'edge', 0, 0, tiled=True)  5.09 us
  transfers between devices with their start and end apart: 21, of which 13 were waited for; matrix products, arithmetic and copies ran while one was open for 6% of the time, Pallas kernels for 22%

profile of v1, /device:TPU:0, one launch (start us, length us, event | category | flops | bytes accessed | tf_op | source)
XLA Modules:
  0.0 134.2 jit_solution(12678963580313532514)
XLA Ops:
  0.6 3.0 %shard_map.212 = bf16[16,48,128]{2,1,0:T(8,128)(2,1)} custom-call(s32[2,1024]{1,0:T(2,128)} %src_ref.3, s32[2,1024]{1,0:T(2,128)} %dst_ref.1, bf16[2,16,1024]{2,1,0:T(8,128)(2,1)} %feat_ref.1), custom_call_target="tpu_custom_call" | custom-call | tf_op jit(solution)/shard_map/pallas_call | solution.py:633
  3.7 8.3 %all-to-all-start = ((bf16[16,48,128]{2,1,0:T(8,128)(2,1)}), bf16[16,48,128]{2,1,0:T(8,128)(2,1)S(1)}, u32[]{:S(2)}, u32[]{:S(2)}) async-start(bf16[16,48,128]{2,1,0:T(8,128)(2,1)} %shard_map.212), calls=%async_computation | async-start | bytes 393216 | tf_op jit(solution)/shard_map/all_to_all | solution.py:638
  12.0 5.4 %copy.39 = bf16[16,8,128,128]{3,2,1,0:T(8,128)(2,1)} copy(bf16[16,8,128,128]{3,1,2,0:T(8,128)(2,1)} %bitcast.43) | data formatting | bytes 8388608
  18.1 2.6 %all-to-all-done.edge_ref = bf16[16,48,128]{2,1,0:T(8,128)(2,1)S(1)} async-done(((bf16[16,48,128]{2,1,0:T(8,128)(2,1)}), bf16[16,48,128]{2,1,0:T(8,128)(2,1)S(1)}, u32[]{:S(2)}, u32[]{:S(2)}) %all-to-all-start) | async-done | bytes 196640 | tf_op jit(solution)/shard_map/all_to_all | solution.py:638
  21.3 20.9 %shard_map.213 = (bf16[128,128]{1,0:T(8,128)(2,1)}, bf16[2,4,16,4352]{3,2,1,0:T(8,128)(2,1)}, bf16[2,4,16,4352]{3,2,1,0:T(8,128)(2,1)}, bf16[2,4,16,4352]{3,2,1,...) custom-call(s32[3]{0:T(128)} %pad_add_fusion.where_ref, ...), custom_call_target="tpu_custom_call" | custom-call | tf_op jit(solution)/shard_map/pallas_call | solution.py:664
  44.1 1.8 %collective-permute-done.second_ref = bf16[2,4,16,4352]{3,2,1,0:T(8,128)(2,1)S(1)} collective-permute-done((bf16[2,4,16,4352]{3,2,1,0:T(8,128)(2,1)}, bf16[2,4,16,4352]{3,2,1,0:T(8,128)(2,1)S(1)}, u32[]{:S(2)}, u32[]{:S(2)}) %collective-permute-start) | collective-permute-done | bytes 1114144 | tf_op jit(solution)/shard_map/ppermute | solution.py:708
  46.4 17.5 %shard_map.216 = (bf16[2,64,128]{2,1,0:T(8,128)(2,1)}, bf16[16,32,128]{2,1,0:T(8,128)(2,1)}, bf16[1056,512]{1,0:T(8,128)(2,1)}, f32[32,128]{1,0:T(8,128)}) custom-call(s32[2,17]{1,0:T(2,128)} %get-tuple-element.80.order_ref, bf16[16,48,128]{2,1,0:T(8,128)(2,1)} %copy-done, bf16[2,4224,128]{2,1,0:T(8,128)(2,1)} %get-tuple-element.84.g_far, ...), custom_call_target="tpu_custom_call" | custom-call | flops 12000000000 | bytes 36000000 | tf_op jit(solution)/shard_map/pallas_call | solution.py:733
  64.9 2.4 %fusion = bf16[2,2,16,4352]{3,2,1,0:T(8,128)(2,1)} fusion(bf16[2,2,2,16,4352]{4,3,2,1,0:T(8,128)(2,1)} %bitcast.47, s32[]{:T(128)S(6)} %select_n.81, bf16[2,2,2,16,4352]{4,3,2,1,0:T(8,128)(2,1)} %bitcast.14, bf16[2,2,2,16,4352]{4,3,2,1,0:T(8,128)(2,1)S(1)} %bitcast.44), kind=kLoop, calls=%fused_computation.1 | loop fusion | flops 1671168 | bytes 2228228 | tf_op jit(solution)/shard_map/convert_element_type | solution.py:780
  68.6 4.6 %shard_map.217 = (bf16[16,32,128]{2,1,0:T(8,128)(2,1)}, f32[32,128]{1,0:T(8,128)S(1)}) custom-call(s32[2,17]{1,0:T(2,128)S(1)} %copy-done.6, bf16[16,48,128]{2,1,0:T(8,128)(2,1)S(1)} %copy-done.1, bf16[1056,512]{1,0:T(8,128)(2,1)S(1)} %copy-done.7, bf16[16,32,128]{2,1,0:T(8,128)(2,1)S(1)} %copy-done.8, bf16[16,128]{1,0:T(8,128)(2,1)S(1)} %copy-done.3, ...), custom_call_target="tpu_custom_call" | custom-call | flops 5000000000 | bytes 15000000 | tf_op jit(solution)/shard_map/pallas_call | solution.py:757
  73.2 3.8 %collective-permute-done.3 = bf16[2,2,16,4352]{3,2,1,0:T(8,128)(2,1)S(1)} collective-permute-done((bf16[2,2,16,4352]{3,2,1,0:T(8,128)(2,1)}, bf16[2,2,16,4352]{3,2,1,0:T(8,128)(2,1)S(1)}, u32[]{:S(2)}, u32[]{:S(2)}) %collective-permute-start.3) | collective-permute-done | bytes 557088 | tf_op jit(solution)/shard_map/ppermute | solution.py:715
  78.3 2.0 %collective-permute-start.5 = (f32[32,128]{1,0:T(8,128)S(1)}, f32[32,128]{1,0:T(8,128)S(1)}, u32[]{:S(2)}, u32[]{:S(2)}) collective-permute-start(f32[32,128]{1,0:T(8,128)S(1)} %get-tuple-element.97), channel_id=1, source_target_pairs={{0,4},{1,5},{2,6},{3,7},{4,0},{5,1},{6,2},{7,3},{8,12},{9,13},{10,... | collective-permute-start | bytes 49160 | tf_op jit(solution)/shard_map/ppermute | solution.py:715
  80.3 4.7 %collective-permute-done.5 = f32[32,128]{1,0:T(8,128)S(1)} collective-permute-done((f32[32,128]{1,0:T(8,128)S(1)}, f32[32,128]{1,0:T(8,128)S(1)}, u32[]{:S(2)}, u32[]{:S(2)}) %collective-permute-start.5) | collective-permute-done | bytes 16416 | tf_op jit(solution)/shard_map/ppermute | solution.py:715
  86.3 2.0 %collective-permute-start.7 = (f32[32,128]{1,0:T(8,128)S(1)}, f32[32,128]{1,0:T(8,128)S(1)}, u32[]{:S(2)}, u32[]{:S(2)}) collective-permute-start(f32[32,128]{1,0:T(8,128)S(1)} %add.165), channel_id=1, source_target_pairs={{0,1},{1,0},{2,3},{3,2},{4,5},{5,4},{6,7},{7,6},{8,9},{9,8},{10,11... | collective-permute-start | bytes 49160 | tf_op jit(solution)/shard_map/ppermute | solution.py:715
  88.4 1.8 %collective-permute-done.7 = f32[32,128]{1,0:T(8,128)S(1)} collective-permute-done((f32[32,128]{1,0:T(8,128)S(1)}, f32[32,128]{1,0:T(8,128)S(1)}, u32[]{:S(2)}, u32[]{:S(2)}) %collective-permute-start.7) | collective-permute-done | bytes 16416 | tf_op jit(solution)/shard_map/ppermute | solution.py:715
  90.1 1.9 %collective-permute-start.8 = (f32[32,128]{1,0:T(8,128)S(1)}, f32[32,128]{1,0:T(8,128)S(1)}, u32[]{:S(2)}, u32[]{:S(2)}) collective-permute-start(f32[32,128]{1,0:T(8,128)S(1)} %add.166), channel_id=1, source_target_pairs={{0,2},{1,3},{2,0},{3,1},{4,6},{5,7},{6,4},{7,5},{8,10},{9,11},{10,... | collective-permute-start | bytes 49160 | tf_op jit(solution)/shard_map/ppermute | solution.py:715
  92.1 1.8 %collective-permute-done.8 = f32[32,128]{1,0:T(8,128)S(1)} collective-permute-done((f32[32,128]{1,0:T(8,128)S(1)}, f32[32,128]{1,0:T(8,128)S(1)}, u32[]{:S(2)}, u32[]{:S(2)}) %collective-permute-start.8) | collective-permute-done | bytes 16416 | tf_op jit(solution)/shard_map/ppermute | solution.py:715
  93.9 5.8 %collective-permute-done.6.second_ref = bf16[2,16,4352]{2,1,0:T(8,128)(2,1)S(1)} collective-permute-done((bf16[2,16,4352]{2,1,0:T(8,128)(2,1)S(1)}, bf16[2,16,4352]{2,1,0:T(8,128)(2,1)S(1)}, u32[]{:S(2)}, u32[]{:S(2)}) %collective-permute-start.6) | collective-permute-done | bytes 278560 | tf_op jit(solution)/shard_map/ppermute | solution.py:715
  101.8 3.2 %collective-permute-done.10 = f32[32,128]{1,0:T(8,128)S(1)} collective-permute-done((f32[32,128]{1,0:T(8,128)S(1)}, f32[32,128]{1,0:T(8,128)S(1)}, u32[]{:S(2)}, u32[]{:S(2)}) %collective-permute-start.10) | collective-permute-done | bytes 16416 | tf_op jit(solution)/shard_map/ppermute | solution.py:715
  105.0 2.1 %collective-permute-done.9 = bf16[2,544,128]{2,1,0:T(8,128)(2,1)S(1)} collective-permute-done((bf16[2,544,128]{2,1,0:T(8,128)(2,1)S(1)}, bf16[2,544,128]{2,1,0:T(8,128)(2,1)S(1)}, u32[]{:S(2)}, u32[]{:S(2)}) %collective-permute-start.9) | collective-permute-done | bytes 278560 | tf_op jit(solution)/shard_map/ppermute | solution.py:715
  107.7 5.1 %all-to-all-start.1 = ((bf16[16,32,128]{2,1,0:T(8,128)(2,1)}), bf16[16,32,128]{2,1,0:T(8,128)(2,1)S(1)}, u32[]{:S(2)}, u32[]{:S(2)}) async-start(bf16[16,32,128]{2,1,0:T(8,128)(2,1)} %get-tuple-element.112), calls=%async_computation.1 | async-start | bytes 262144 | tf_op jit(solution)/shard_map/all_to_all | solution.py:812
  114.1 2.8 %collective-permute-done.12.refs_1_ = bf16[4,544,128]{2,1,0:T(8,128)(2,1)S(1)} collective-permute-done((bf16[4,544,128]{2,1,0:T(8,128)(2,1)S(1)}, bf16[4,544,128]{2,1,0:T(8,128)(2,1)S(1)}, u32[]{:S(2)}, u32[]{:S(2)}) %collective-permute-start.12) | collective-permute-done | bytes 557088 | tf_op jit(solution)/shard_map/ppermute | solution.py:715
  116.9 5.0 %all-to-all-done.1 = bf16[16,32,128]{2,1,0:T(8,128)(2,1)S(1)} async-done(((bf16[16,32,128]{2,1,0:T(8,128)(2,1)}), bf16[16,32,128]{2,1,0:T(8,128)(2,1)S(1)}, u32[]{:S(2)}, u32[]{:S(2)}) %all-to-all-start.1) | async-done | bytes 131104 | tf_op jit(solution)/shard_map/all_to_all | solution.py:812
  121.9 2.1 %shard_map.219 = (f32[128,16384]{1,0:T(8,128)}, f32[128,128]{1,0:T(8,128)}, f32[128,384]{1,0:T(8,128)}, f32[128,384]{1,0:T(8,128)}, f32[128,128]{1,0:T(8,128)S(1)}) custom-call(s32[2]{0:T(128)S(1)} %pad_add_fusion.2.refs_0_, bf16[4,544,128]{2,1,0:T(8,128)(2,1)S(1)} %pad_maximum_fusion.refs_1_, bf16[4,544,128]{2,1,0:T(8,128)(2,1)S(1)} %collective-permute-done.11.refs_2_), custom_call_target="tpu_custom_call" | custom-call | flops 100000000 | bytes 300000 | tf_op jit(solution)/shard_map/pallas_call | solution.py:596
  127.8 3.1 %shard_map.220 = (f32[128,16384]{1,0:T(8,128)}, f32[128,128]{1,0:T(8,128)}, f32[128,384]{1,0:T(8,128)}, f32[128,384]{1,0:T(8,128)}, f32[128,128]{1,0:T(8,128)S(1)}) custom-call(s32[4]{0:T(128)S(1)} %pad_add_fusion.1.refs_0_, ...), custom_call_target="tpu_custom_call", output_to_operand_aliasing={{0}: (5, {}), {1}: (6, {}), {2}: (7, {}), {3}: (8, {}), {4}... | custom-call | flops 100000000 | bytes 300000 | tf_op jit(solution)/shard_map/pallas_call | solution.py:596
  (70 shorter events, 19.3 us)
Async XLA Ops:
  3.7 17.0 %all-to-all-start = ((bf16[16,48,128]{2,1,0:T(8,128)(2,1)}), bf16[16,48,128]{2,1,0:T(8,128)(2,1)S(1)}, u32[]{:S(2)}, u32[]{:S(2)}) async-start(bf16[16,48,128]{2,1,0:T(8,128)(2,1)} %shard_map.212), calls=%async_computation | async-start | bytes 393216 | tf_op jit(solution)/shard_map/all_to_all | solution.py:638
  42.2 3.7 %collective-permute-start = (bf16[2,4,16,4352]{3,2,1,0:T(8,128)(2,1)}, bf16[2,4,16,4352]{3,2,1,0:T(8,128)(2,1)S(1)}, u32[]{:S(2)}, u32[]{:S(2)}) collective-permute-start(bf16[2,4,16,4352]{3,2,1,0:T(8,128)(2,1)} %get-tuple-element.83), channel_id=1, source_target_pairs={{0,16},{16,0},{1,17},{17,1},{2,18},{18,2},{3,19},{19,3},{4,20},{20... | collective-permute-start | bytes 3342344 | tf_op jit(solution)/shard_map/ppermute | solution.py:708
  42.3 21.6 %collective-permute-start.1 = (bf16[2,4,16,4352]{3,2,1,0:T(8,128)(2,1)}, bf16[2,4,16,4352]{3,2,1,0:T(8,128)(2,1)}, u32[]{:S(2)}, u32[]{:S(2)}) collective-permute-start(bf16[2,4,16,4352]{3,2,1,0:T(8,128)(2,1)} %get-tuple-element.91), channel_id=1, source_target_pairs={{0,16},{16,0},{1,17},{17,1},{2,18},{18,2},{3,19},{19,3},{4,20},{20... | collective-permute-start | bytes 3342344 | tf_op jit(solution)/shard_map/ppermute | solution.py:708
  46.2 17.6 %collective-permute-start.2 = (bf16[2,4,16,4352]{3,2,1,0:T(8,128)(2,1)S(1)}, bf16[2,4,16,4352]{3,2,1,0:T(8,128)(2,1)S(1)}, u32[]{:S(2)}, u32[]{:S(2)}) collective-permute-start(bf16[2,4,16,4352]{3,2,1,0:T(8,128)(2,1)S(1)} %shard_map.215), channel_id=1, source_target_pairs={{0,1},{1,0},{2,3},{3,2},{4,5},{5,4},{6,7},{7,6},{8,9},{9,8},{10,11... | collective-permute-start | bytes 3342344 | tf_op jit(solution)/shard_map/ppermute | solution.py:715
  46.4 18.5 %copy-start.10 = (bf16[2,4,16,4352]{3,2,1,0:T(8,128)(2,1)S(1)}, bf16[2,4,16,4352]{3,2,1,0:T(8,128)(2,1)}, u32[]{:S(2)}) copy-start(bf16[2,4,16,4352]{3,2,1,0:T(8,128)(2,1)} %get-tuple-element.90) | copy-start | bytes 3342340
  64.9 3.7 %copy-start.4 = (f32[128]{0:T(128)S(1)}, f32[128]{0:T(128)}, u32[]{:S(2)}) copy-start(f32[128]{0:T(128)} %b_in_ref.5) | copy-start | bytes 1540
  67.3 9.7 %collective-permute-start.3 = (bf16[2,2,16,4352]{3,2,1,0:T(8,128)(2,1)}, bf16[2,2,16,4352]{3,2,1,0:T(8,128)(2,1)S(1)}, u32[]{:S(2)}, u32[]{:S(2)}) collective-permute-start(bf16[2,2,16,4352]{3,2,1,0:T(8,128)(2,1)} %fusion), channel_id=1, source_target_pairs={{0,2},{1,3},{2,0},{3,1},{4,6},{5,7},{6,4},{7,5},{8,10},{9,11},{10,... | collective-permute-start | bytes 1671176 | tf_op jit(solution)/shard_map/ppermute | solution.py:715
  78.2 6.8 %collective-permute-start.4 = (bf16[2,16,4352]{2,1,0:T(8,128)(2,1)S(1)}, bf16[2,16,4352]{2,1,0:T(8,128)(2,1)S(1)}, u32[]{:S(2)}, u32[]{:S(2)}) collective-permute-start(bf16[2,16,4352]{2,1,0:T(8,128)(2,1)S(1)} %fusion.1), channel_id=1, source_target_pairs={{0,4},{1,5},{2,6},{3,7},{4,0},{5,1},{6,2},{7,3},{8,12},{9,13},{10,... | collective-permute-start | bytes 835592 | tf_op jit(solution)/shard_map/ppermute | solution.py:715
  78.3 6.7 %collective-permute-start.5 = (f32[32,128]{1,0:T(8,128)S(1)}, f32[32,128]{1,0:T(8,128)S(1)}, u32[]{:S(2)}, u32[]{:S(2)}) collective-permute-start(f32[32,128]{1,0:T(8,128)S(1)} %get-tuple-element.97), channel_id=1, source_target_pairs={{0,4},{1,5},{2,6},{3,7},{4,0},{5,1},{6,2},{7,3},{8,12},{9,13},{10,... | collective-permute-start | bytes 49160 | tf_op jit(solution)/shard_map/ppermute | solution.py:715
  86.2 13.5 %collective-permute-start.6 = (bf16[2,16,4352]{2,1,0:T(8,128)(2,1)S(1)}, bf16[2,16,4352]{2,1,0:T(8,128)(2,1)S(1)}, u32[]{:S(2)}, u32[]{:S(2)}) collective-permute-start(bf16[2,16,4352]{2,1,0:T(8,128)(2,1)S(1)} %fusion.3.first_ref), channel_id=1, source_target_pairs={{0,8},{1,9},{2,10},{3,11},{4,12},{5,13},{6,14},{7,15},{8,0},{9,1},... | collective-permute-start | bytes 835592 | tf_op jit(solution)/shard_map/ppermute | solution.py:715
  86.3 3.8 %collective-permute-start.7 = (f32[32,128]{1,0:T(8,128)S(1)}, f32[32,128]{1,0:T(8,128)S(1)}, u32[]{:S(2)}, u32[]{:S(2)}) collective-permute-start(f32[32,128]{1,0:T(8,128)S(1)} %add.165), channel_id=1, source_target_pairs={{0,1},{1,0},{2,3},{3,2},{4,5},{5,4},{6,7},{7,6},{8,9},{9,8},{10,11... | collective-permute-start | bytes 49160 | tf_op jit(solution)/shard_map/ppermute | solution.py:715
  90.1 3.7 %collective-permute-start.8 = (f32[32,128]{1,0:T(8,128)S(1)}, f32[32,128]{1,0:T(8,128)S(1)}, u32[]{:S(2)}, u32[]{:S(2)}) collective-permute-start(f32[32,128]{1,0:T(8,128)S(1)} %add.166), channel_id=1, source_target_pairs={{0,2},{1,3},{2,0},{3,1},{4,6},{5,7},{6,4},{7,5},{8,10},{9,11},{10,... | collective-permute-start | bytes 49160 | tf_op jit(solution)/shard_map/ppermute | solution.py:715
  100.1 7.0 %collective-permute-start.9 = (bf16[2,544,128]{2,1,0:T(8,128)(2,1)S(1)}, bf16[2,544,128]{2,1,0:T(8,128)(2,1)S(1)}, u32[]{:S(2)}, u32[]{:S(2)}) collective-permute-start(bf16[2,544,128]{2,1,0:T(8,128)(2,1)S(1)} %shard_map.218), channel_id=1, source_target_pairs={{0,4},{1,5},{2,6},{3,7},{4,0},{5,1},{6,2},{7,3},{8,12},{9,13},{10,... | collective-permute-start | bytes 835592 | tf_op jit(solution)/shard_map/ppermute | solution.py:715
  100.2 24.5 %copy-start.2 = (s32[2,1024]{1,0:T(2,128)S(1)}, s32[2,1024]{1,0:T(2,128)}, u32[]{:S(2)}) copy-start(s32[2,1024]{1,0:T(2,128)} %src_ref.3) | copy-start | bytes 24580
  100.2 4.8 %collective-permute-start.10 = (f32[32,128]{1,0:T(8,128)S(1)}, f32[32,128]{1,0:T(8,128)S(1)}, u32[]{:S(2)}, u32[]{:S(2)}) collective-permute-start(f32[32,128]{1,0:T(8,128)S(1)} %add.167), channel_id=1, source_target_pairs={{0,8},{1,9},{2,10},{3,11},{4,12},{5,13},{6,14},{7,15},{8,0},{9,1},... | collective-permute-start | bytes 49160 | tf_op jit(solution)/shard_map/ppermute | solution.py:715
  107.1 9.8 %collective-permute-start.12 = (bf16[4,544,128]{2,1,0:T(8,128)(2,1)S(1)}, bf16[4,544,128]{2,1,0:T(8,128)(2,1)S(1)}, u32[]{:S(2)}, u32[]{:S(2)}) collective-permute-start(bf16[4,544,128]{2,1,0:T(8,128)(2,1)S(1)} %pad_maximum_fusion.refs_1_), channel_id=1, source_target_pairs={{0,2},{1,3},{2,0},{3,1},{4,6},{5,7},{6,4},{7,5},{8,10},{9,11},{10,... | collective-permute-start | bytes 1671176 | tf_op jit(solution)/shard_map/ppermute | solution.py:715
  107.5 14.5 %collective-permute-start.11 = (bf16[4,544,128]{2,1,0:T(8,128)(2,1)S(1)}, bf16[4,544,128]{2,1,0:T(8,128)(2,1)S(1)}, u32[]{:S(2)}, u32[]{:S(2)}) collective-permute-start(bf16[4,544,128]{2,1,0:T(8,128)(2,1)S(1)} %pad_maximum_fusion.refs_1_), channel_id=1, source_target_pairs={{0,16},{16,0},{1,17},{17,1},{2,18},{18,2},{3,19},{19,3},{4,20},{20... | collective-permute-start | bytes 1671176 | tf_op jit(solution)/shard_map/ppermute | solution.py:708
  107.5 16.6 %collective-permute-start.14 = (bf16[4,544,128]{2,1,0:T(8,128)(2,1)S(1)}, bf16[4,544,128]{2,1,0:T(8,128)(2,1)S(1)}, u32[]{:S(2)}, u32[]{:S(2)}) collective-permute-start(bf16[4,544,128]{2,1,0:T(8,128)(2,1)S(1)} %pad_maximum_fusion.refs_1_), channel_id=1, source_target_pairs={{0,1},{1,0},{2,3},{3,2},{4,5},{5,4},{6,7},{7,6},{8,9},{9,8},{10,11... | collective-permute-start | bytes 1671176 | tf_op jit(solution)/shard_map/ppermute | solution.py:715
  107.7 14.2 %all-to-all-start.1 = ((bf16[16,32,128]{2,1,0:T(8,128)(2,1)}), bf16[16,32,128]{2,1,0:T(8,128)(2,1)S(1)}, u32[]{:S(2)}, u32[]{:S(2)}) async-start(bf16[16,32,128]{2,1,0:T(8,128)(2,1)} %get-tuple-element.112), calls=%async_computation.1 | async-start | bytes 262144 | tf_op jit(solution)/shard_map/all_to_all | solution.py:812
  112.9 1.2 collective-permute-start.13
  116.9 14.0 %collective-permute-start.17 = (bf16[4,544,128]{2,1,0:T(8,128)(2,1)S(1)}, bf16[4,544,128]{2,1,0:T(8,128)(2,1)S(1)}, u32[]{:S(2)}, u32[]{:S(2)}) collective-permute-start(bf16[4,544,128]{2,1,0:T(8,128)(2,1)S(1)} %collective-permute-done.12.refs_1_), channel_id=1, source_target_pairs={{0,1},{1,0},{2,3},{3,2},{4,5},{5,4},{6,7},{7,6},{8,9},{9,8},{10,11... | collective-permute-start | bytes 1671176 | tf_op jit(solution)/shard_map/ppermute | solution.py:715
  124.1 3.7 %collective-permute-start.15 = (bf16[4,544,128]{2,1,0:T(8,128)(2,1)S(1)}, bf16[4,544,128]{2,1,0:T(8,128)(2,1)S(1)}, u32[]{:S(2)}, u32[]{:S(2)}) collective-permute-start(bf16[4,544,128]{2,1,0:T(8,128)(2,1)S(1)} %collective-permute-done.12.refs_1_), channel_id=1, source_target_pairs={{0,16},{16,0},{1,17},{17,1},{2,18},{18,2},{3,19},{19,3},{4,20},{20... | collective-permute-start | bytes 1671176 | tf_op jit(solution)/shard_map/ppermute | solution.py:708
  124.1 3.7 %collective-permute-start.16 = (bf16[4,544,128]{2,1,0:T(8,128)(2,1)S(1)}, bf16[4,544,128]{2,1,0:T(8,128)(2,1)S(1)}, u32[]{:S(2)}, u32[]{:S(2)}) collective-permute-start(bf16[4,544,128]{2,1,0:T(8,128)(2,1)S(1)} %collective-permute-done.14.refs_3_), channel_id=1, source_target_pairs={{0,16},{16,0},{1,17},{17,1},{2,18},{18,2},{3,19},{19,3},{4,20},{20... | collective-permute-start | bytes 1671176 | tf_op jit(solution)/shard_map/ppermute | solution.py:708
  130.9 2.0 %collective-permute-start.18 = (bf16[4,544,128]{2,1,0:T(8,128)(2,1)S(1)}, bf16[4,544,128]{2,1,0:T(8,128)(2,1)S(1)}, u32[]{:S(2)}, u32[]{:S(2)}) collective-permute-start(bf16[4,544,128]{2,1,0:T(8,128)(2,1)S(1)} %collective-permute-done.17.refs_1_), channel_id=1, source_target_pairs={{0,16},{16,0},{1,17},{17,1},{2,18},{18,2},{3,19},{19,3},{4,20},{20... | collective-permute-start | bytes 1671176 | tf_op jit(solution)/shard_map/ppermute | solution.py:708
  (9 other events, 25.3 us)

commit v2 on v1

--- a/solution.py
+++ b/solution.py
@@ -385,7 +385,7 @@
         feats, held, pairs, low = edge_piece(batches, order_ref, edge_ref, piece, batch)
         pre = dot(w_in, feats) + b_in
         sig = jax.nn.sigmoid(pre)
-        spread = dot(dg_ref[: 8 * hidden_units], pairs)
+        spread = dot(dg_ref[batch, : 8 * hidden_units], pairs)
         spread = spread.reshape(hidden_units, 8, pre.shape[1])
         spread = jnp.where(low[None], spread, 0.0).reshape(8 * hidden_units, pre.shape[1])
         d_hidden = dot(fold, spread.astype(BF16))
@@ -401,29 +401,21 @@
 
 
 def back_kernel(
-    order_ref,
-    edge_ref,
     g_far,
     level_ref,
     dm_ref,
     base_ref,
-    w_in_ref,
-    b_in_ref,
     w_far,
     bias_ref,
-    before_ref,
     grad_ref,
-    feat_ref,
     dg_ref,
-    win_ref,
     tail_ref,
-    dg_first,
     w_ref,
     g_ref,
     sems,
 ):
     batches, own, width = grad_ref.shape
-    hidden_units = w_in_ref.shape[1]
+    hidden_units = w_ref.shape[0]
     chunks = (hidden_units + tail_ref.shape[0]) // GROUP
     half = own // 2
     fetches = []
@@ -437,7 +429,6 @@
     for fetch in fetches:
         fetch.start()
     bias_blocks(bias_ref, tail_ref)
-    feat_ref[...] = jnp.zeros_like(feat_ref)
 
     pulls, levels = [], []
     for batch in range(batches):
@@ -453,7 +444,6 @@
         pulled = dot(pulls, weights_of(w_ref, tail_ref, number)).astype(BF16)
         at = slice(number * GROUP * half, (number + 1) * GROUP * half)
         for batch in range(batches):
-            target = dg_ref if batch else dg_first
             talls = [
                 pulled_rows(pulled[(2 * batch + k) * own : (2 * batch + k + 1) * own], half)
                 for k in range(2)
@@ -467,32 +457,23 @@
                         d_pair[(unit + k) * half + part * 8 : (unit + k) * half + part * 8 + 8]
                         for k in range(2)
                     ]
-                    target[row : row + 16, part * LANES : (part + 1) * LANES] = jnp.concatenate(
+                    dg_ref[batch, row : row + 16, part * LANES : (part + 1) * LANES] = jnp.concatenate(
                         pair, axis=0
                     ).astype(BF16)
     for batch in range(batches):
         grad = base_ref[batch * own : (batch + 1) * own] + totals[batch][:own, :width]
         grad_ref[batch] = (grad + totals[batch][own:, width:]).astype(BF16)
-    win_ref[...] = edge_sums(
-        0, batches, order_ref, edge_ref, dg_first, w_in_ref, b_in_ref, feat_ref, before_ref[...]
-    )
-
-
-def edge_kernel(
-    order_ref, edge_ref, dg_ref, feat_in, w_in_ref, b_in_ref, before_ref, feat_ref, win_ref
-):
-    feat_ref[...] = feat_in[...]
-    win_ref[...] = edge_sums(
-        1,
-        order_ref.shape[0],
-        order_ref,
-        edge_ref,
-        dg_ref,
-        w_in_ref,
-        b_in_ref,
-        feat_ref,
-        before_ref[...],
-    )
+
+
+def edge_kernel(order_ref, edge_ref, dg_ref, w_in_ref, b_in_ref, before_ref, feat_ref, win_ref):
+    batches = order_ref.shape[0]
+    feat_ref[...] = jnp.zeros_like(feat_ref)
+    sums = before_ref[...]
+    for batch in range(batches):
+        sums = edge_sums(
+            batch, batches, order_ref, edge_ref, dg_ref, w_in_ref, b_in_ref, feat_ref, sums
+        )
+    win_ref[...] = sums
 
 
 def add_kernel(first_ref, second_ref, out_ref):
@@ -726,40 +707,35 @@
     def after(value, *others):
         return lax.optimization_barrier((value, *others))[0]
 
-    feat_shape = jax.ShapeDtypeStruct((blocks, batches * feat_count, LANES), BF16)
-    win_shape = jax.ShapeDtypeStruct((32, units), F32)
-
     def first_grads(pairs_in):
         return full_call(
             back_kernel,
             (
                 jax.ShapeDtypeStruct((batches, own, width), BF16),
-                feat_shape,
-                jax.ShapeDtypeStruct((padded * 8, 512), BF16),
-                win_shape,
+                jax.ShapeDtypeStruct((batches, padded * 8, 512), BF16),
             ),
             (
                 pltpu.VMEM((padded - units, width, width), BF16),
-                pltpu.VMEM((padded * 8, 512), BF16),
                 pltpu.VMEM((units, width, width), BF16),
                 pltpu.VMEM((batches, padded * pairs, LANES), BF16),
                 pltpu.SemaphoreType.DMA((padded // GROUP, 2)),
             ),
             limit=60,
-            in_specs=[smem, vmem, far] + [vmem] * 5 + [far] + [vmem] * 2,
+            in_specs=[far] + [vmem] * 3 + [far, vmem],
             cost_estimate=cost(12),
-        )(
-            order, edge_data, pairs_in, levels, d_mails, base,
-            w_edge_in, b_edge_in, w_mats, bias, first,
-        )
-
-    def second_grads(d_pairs, feats, before):
+        )(pairs_in, levels, d_mails, base, w_mats, bias)
+
+    def second_grads(d_pairs):
         return full_call(
             edge_kernel,
-            (feat_shape, win_shape),
-            in_specs=[smem] + [vmem] * 6,
-            cost_estimate=cost(5),
-        )(order, edge_data, d_pairs, feats, w_edge_in, b_edge_in, before)
+            (
+                jax.ShapeDtypeStruct((blocks, batches * feat_count, LANES), BF16),
+                jax.ShapeDtypeStruct((32, units), F32),
+            ),
+            limit=60,
+            in_specs=[smem] + [vmem] * 5,
+            cost_estimate=cost(9),
+        )(order, edge_data, d_pairs, w_edge_in, b_edge_in, first)
 
     def added_at(big, small, flip):
         big, more = lax.optimization_barrier((big, swap(small, [flip] * cores)))
@@ -781,10 +757,10 @@
             terms = [pick(one, number) for one in terms]
         got = swap_step(give, step)
         if step == 0:
-            state_grad, d_feats, d_pairs, first = first_grads(after(g_pairs, give))
-            got = after(got, first)
+            state_grad, d_pairs = first_grads(after(g_pairs, give))
+            got = after(got, state_grad)
         if step == 1:
-            d_feats, first = second_grads(after(d_pairs, give), d_feats, first)
+            d_feats, first = second_grads(after(d_pairs, give))
             got = after(got, first)
         if step == 2:
             got, first = added_at(got, first, 4)

time: 134 us -> 129 us (0.963)
  Pallas kernels: 55.5 us -> 51 us
  starting transfers between devices: 24.6 us -> 27.6 us
  waiting for transfers between devices: 37.3 us -> 35.4 us
    ppermute x12, starting transfers between devices: 9.83 us -> 14.4 us  [swap(): return lax.ppermute(value, ('graph', 'edge'), moves)]
    pallas_call x1, Pallas kernels: 17.5 us -> 14.4 us  [first_grads(): full_call(back_kernel, (jax.ShapeDtypeStruct((batches, own, width), BF16)...]
    pallas_call x1, Pallas kernels: 20.9 us -> 18.3 us  [body(): full_call(main_kernel, (jax.ShapeDtypeStruct((batches * own, width), BF16...]
    all_to_all x1, starting transfers between devices: 5.09 us -> 3.51 us  [body(): back = lax.all_to_all(back, 'edge', 0, 0, tiled=True)]
    unnamed x25 -> x11, local copies, waits for them, and re-layouts: 8.39 us -> 7.39 us
where the time goes in v2:
time: 129 us
  Pallas kernels  51 us (40%)
  waiting for transfers between devices  35.4 us (27%)
  starting transfers between devices  27.6 us (21%)
  local copies, waits for them, and re-layouts  9.08 us (7%)
  other arithmetic  4.3 us (3%)
    ppermute x12, waiting for transfers between devices, swap(): return lax.ppermute(value, ('graph', 'edge'), moves)  25.7 us
    pallas_call x1, Pallas kernels, body(): full_call(main_kernel, (jax.ShapeDtypeStruct((batches * own, width), BF16...  18.3 us
    ppermute x12, starting transfers between devices, swap(): return lax.ppermute(value, ('graph', 'edge'), moves)  14.4 us
    pallas_call x1, Pallas kernels, first_grads(): full_call(back_kernel, (jax.ShapeDtypeStruct((batches, own, width), BF16)...  14.4 us
    all_to_all x1, starting transfers between devices, body(): edge_data = lax.all_to_all(sent, 'edge', 0, 0, tiled=True)  8.31 us
    pallas_call x4, Pallas kernels, place_pieces(): pl.pallas_call(functools.partial(place_kernel, tall, count, len(before)),...  7.43 us
    unnamed x11, local copies, waits for them, and re-layouts  7.39 us
    pallas_call x1, Pallas kernels, second_grads(): full_call(edge_kernel, (jax.ShapeDtypeStruct((blocks, batches * feat_coun...  5.72 us
  transfers between devices with their start and end apart: 21, of which 13 were waited for; matrix products, arithmetic and copies ran while one was open for 6% of the time, Pallas kernels for 22%

profile of v2, /device:TPU:0, one launch (start us, length us, event | category | flops | bytes accessed | tf_op | source)
XLA Modules:
  0.0 128.5 jit_solution(9493991204972551977)
XLA Ops:
  0.6 3.0 %shard_map.212 = bf16[16,48,128]{2,1,0:T(8,128)(2,1)} custom-call(s32[2,1024]{1,0:T(2,128)} %src_ref.3, s32[2,1024]{1,0:T(2,128)} %dst_ref.1, bf16[2,16,1024]{2,1,0:T(8,128)(2,1)} %feat_ref.1), custom_call_target="tpu_custom_call" | custom-call | tf_op jit(solution)/shard_map/pallas_call | solution.py:614
  3.7 8.3 %all-to-all-start = ((bf16[16,48,128]{2,1,0:T(8,128)(2,1)}), bf16[16,48,128]{2,1,0:T(8,128)(2,1)S(1)}, u32[]{:S(2)}, u32[]{:S(2)}) async-start(bf16[16,48,128]{2,1,0:T(8,128)(2,1)} %shard_map.212), calls=%async_computation | async-start | bytes 393216 | tf_op jit(solution)/shard_map/all_to_all | solution.py:619
  12.0 5.4 %copy.39 = bf16[16,8,128,128]{3,2,1,0:T(8,128)(2,1)} copy(bf16[16,8,128,128]{3,1,2,0:T(8,128)(2,1)} %bitcast.43) | data formatting | bytes 8388608
  18.1 2.6 %all-to-all-done.edge_ref = bf16[16,48,128]{2,1,0:T(8,128)(2,1)S(1)} async-done(((bf16[16,48,128]{2,1,0:T(8,128)(2,1)}), bf16[16,48,128]{2,1,0:T(8,128)(2,1)S(1)}, u32[]{:S(2)}, u32[]{:S(2)}) %all-to-all-start) | async-done | bytes 196640 | tf_op jit(solution)/shard_map/all_to_all | solution.py:619
  21.3 18.3 %shard_map.213 = (bf16[128,128]{1,0:T(8,128)(2,1)}, bf16[2,4,16,4352]{3,2,1,0:T(8,128)(2,1)}, bf16[2,4,16,4352]{3,2,1,0:T(8,128)(2,1)}, bf16[2,4,16,4352]{3,2,1,...) custom-call(s32[3]{0:T(128)} %pad_add_fusion.where_ref, ...), custom_call_target="tpu_custom_call" | custom-call | tf_op jit(solution)/shard_map/pallas_call | solution.py:645
  43.0 2.7 %collective-permute-start.2 = (bf16[2,4,16,4352]{3,2,1,0:T(8,128)(2,1)S(1)}, bf16[2,4,16,4352]{3,2,1,0:T(8,128)(2,1)}, u32[]{:S(2)}, u32[]{:S(2)}) collective-permute-start(bf16[2,4,16,4352]{3,2,1,0:T(8,128)(2,1)S(1)} %shard_map.215), channel_id=1, source_target_pairs={{0,1},{1,0},{2,3},{3,2},{4,5},{5,4},{6,7},{7,6},{8,9},{9,8},{10,11... | collective-permute-start | bytes 3342344 | tf_op jit(solution)/shard_map/ppermute | solution.py:696
  45.7 14.4 %shard_map.216 = (bf16[2,64,128]{2,1,0:T(8,128)(2,1)}, bf16[2,1056,512]{2,1,0:T(8,128)(2,1)}) custom-call(bf16[2,4224,128]{2,1,0:T(8,128)(2,1)} %get-tuple-element.81.g_far, bf16[128,256]{1,0:T(8,128)(2,1)} %get-tuple-element.82.level_ref, bf16[128,256]{1,0:T(8,128)(2,1)} %get-tuple-element.83.dm_ref, f32[128,128]{1,0:T(8,128)} %get-tuple-element.84.base_ref, ...), custom_call_target="tpu_custom_call" | custom-call | flops 12000000000 | bytes 36000000 | tf_op jit(solution)/shard_map/pallas_call | solution.py:711
  62.5 5.7 %shard_map.217 = (bf16[16,32,128]{2,1,0:T(8,128)(2,1)}, f32[32,128]{1,0:T(8,128)}) custom-call(s32[2,17]{1,0:T(2,128)} %get-tuple-element.89.order_ref, bf16[16,48,128]{2,1,0:T(8,128)(2,1)} %copy-done.3, bf16[2,1056,512]{2,1,0:T(8,128)(2,1)} %get-tuple-element.91.dg_ref, bf16[16,128]{1,0:T(8,128)(2,1)} %w_in_ref.3, f32[128]{0:T(128)} %b_in_ref.3, ...), custom_call_target="tpu_custom_call" | custom-call | flops 8999999488 | bytes 27000000 | tf_op jit(solution)/shard_map/pallas_call | solution.py:729
  68.2 2.8 %collective-permute-done.3 = bf16[2,2,16,4352]{3,2,1,0:T(8,128)(2,1)S(1)} collective-permute-done((bf16[2,2,16,4352]{3,2,1,0:T(8,128)(2,1)S(1)}, bf16[2,2,16,4352]{3,2,1,0:T(8,128)(2,1)S(1)}, u32[]{:S(2)}, u32[]{:S(2)}) %collective-permute-start.3) | collective-permute-done | bytes 557088 | tf_op jit(solution)/shard_map/ppermute | solution.py:696
  72.1 1.5 %collective-permute-start.4 = (bf16[2,16,4352]{2,1,0:T(8,128)(2,1)S(1)}, bf16[2,16,4352]{2,1,0:T(8,128)(2,1)S(1)}, u32[]{:S(2)}, u32[]{:S(2)}) collective-permute-start(bf16[2,16,4352]{2,1,0:T(8,128)(2,1)S(1)} %fusion.1), channel_id=1, source_target_pairs={{0,4},{1,5},{2,6},{3,7},{4,0},{5,1},{6,2},{7,3},{8,12},{9,13},{10,... | collective-permute-start | bytes 835592 | tf_op jit(solution)/shard_map/ppermute | solution.py:696
  74.2 4.7 %collective-permute-done.5 = f32[32,128]{1,0:T(8,128)S(1)} collective-permute-done((f32[32,128]{1,0:T(8,128)S(1)}, f32[32,128]{1,0:T(8,128)S(1)}, u32[]{:S(2)}, u32[]{:S(2)}) %collective-permute-start.5) | collective-permute-done | bytes 16416 | tf_op jit(solution)/shard_map/ppermute | solution.py:696
  81.9 3.0 %collective-permute-done.7 = f32[32,128]{1,0:T(8,128)S(1)} collective-permute-done((f32[32,128]{1,0:T(8,128)S(1)}, f32[32,128]{1,0:T(8,128)S(1)}, u32[]{:S(2)}, u32[]{:S(2)}) %collective-permute-start.7) | collective-permute-done | bytes 16416 | tf_op jit(solution)/shard_map/ppermute | solution.py:696
  85.0 1.6 %collective-permute-start.8 = (f32[32,128]{1,0:T(8,128)S(1)}, f32[32,128]{1,0:T(8,128)S(1)}, u32[]{:S(2)}, u32[]{:S(2)}) collective-permute-start(f32[32,128]{1,0:T(8,128)S(1)} %add.166), channel_id=1, source_target_pairs={{0,2},{1,3},{2,0},{3,1},{4,6},{5,7},{6,4},{7,5},{8,10},{9,11},{10,... | collective-permute-start | bytes 49160 | tf_op jit(solution)/shard_map/ppermute | solution.py:696
  86.6 2.1 %collective-permute-done.8 = f32[32,128]{1,0:T(8,128)S(1)} collective-permute-done((f32[32,128]{1,0:T(8,128)S(1)}, f32[32,128]{1,0:T(8,128)S(1)}, u32[]{:S(2)}, u32[]{:S(2)}) %collective-permute-start.8) | collective-permute-done | bytes 16416 | tf_op jit(solution)/shard_map/ppermute | solution.py:696
  88.7 5.1 %collective-permute-done.6.second_ref = bf16[2,16,4352]{2,1,0:T(8,128)(2,1)S(1)} collective-permute-done((bf16[2,16,4352]{2,1,0:T(8,128)(2,1)S(1)}, bf16[2,16,4352]{2,1,0:T(8,128)(2,1)S(1)}, u32[]{:S(2)}, u32[]{:S(2)}) %collective-permute-start.6) | collective-permute-done | bytes 278560 | tf_op jit(solution)/shard_map/ppermute | solution.py:696
  94.3 1.6 %collective-permute-start.10 = (f32[32,128]{1,0:T(8,128)S(1)}, f32[32,128]{1,0:T(8,128)S(1)}, u32[]{:S(2)}, u32[]{:S(2)}) collective-permute-start(f32[32,128]{1,0:T(8,128)S(1)} %add.167), channel_id=1, source_target_pairs={{0,8},{1,9},{2,10},{3,11},{4,12},{5,13},{6,14},{7,15},{8,0},{9,1},... | collective-permute-start | bytes 49160 | tf_op jit(solution)/shard_map/ppermute | solution.py:696
  95.9 3.2 %collective-permute-done.10 = f32[32,128]{1,0:T(8,128)S(1)} collective-permute-done((f32[32,128]{1,0:T(8,128)S(1)}, f32[32,128]{1,0:T(8,128)S(1)}, u32[]{:S(2)}, u32[]{:S(2)}) %collective-permute-start.10) | collective-permute-done | bytes 16416 | tf_op jit(solution)/shard_map/ppermute | solution.py:696
  99.0 2.1 %collective-permute-done.9 = bf16[2,544,128]{2,1,0:T(8,128)(2,1)S(1)} collective-permute-done((bf16[2,544,128]{2,1,0:T(8,128)(2,1)S(1)}, bf16[2,544,128]{2,1,0:T(8,128)(2,1)S(1)}, u32[]{:S(2)}, u32[]{:S(2)}) %collective-permute-start.9) | collective-permute-done | bytes 278560 | tf_op jit(solution)/shard_map/ppermute | solution.py:696
  103.5 3.5 %all-to-all-start.1 = ((bf16[16,32,128]{2,1,0:T(8,128)(2,1)}), bf16[16,32,128]{2,1,0:T(8,128)(2,1)S(1)}, u32[]{:S(2)}, u32[]{:S(2)}) async-start(bf16[16,32,128]{2,1,0:T(8,128)(2,1)} %get-tuple-element.108), calls=%async_computation.1 | async-start | bytes 262144 | tf_op jit(solution)/shard_map/all_to_all | solution.py:788
  108.3 2.6 %collective-permute-done.12.refs_1_ = bf16[4,544,128]{2,1,0:T(8,128)(2,1)S(1)} collective-permute-done((bf16[4,544,128]{2,1,0:T(8,128)(2,1)S(1)}, bf16[4,544,128]{2,1,0:T(8,128)(2,1)S(1)}, u32[]{:S(2)}, u32[]{:S(2)}) %collective-permute-start.12) | collective-permute-done | bytes 557088 | tf_op jit(solution)/shard_map/ppermute | solution.py:696
  112.0 4.2 %all-to-all-done.1 = bf16[16,32,128]{2,1,0:T(8,128)(2,1)S(1)} async-done(((bf16[16,32,128]{2,1,0:T(8,128)(2,1)}), bf16[16,32,128]{2,1,0:T(8,128)(2,1)S(1)}, u32[]{:S(2)}, u32[]{:S(2)}) %all-to-all-start.1) | async-done | bytes 131104 | tf_op jit(solution)/shard_map/all_to_all | solution.py:788
  116.2 2.1 %shard_map.219 = (f32[128,16384]{1,0:T(8,128)}, f32[128,128]{1,0:T(8,128)}, f32[128,384]{1,0:T(8,128)}, f32[128,384]{1,0:T(8,128)}, f32[128,128]{1,0:T(8,128)S(1)}) custom-call(s32[2]{0:T(128)S(1)} %pad_add_fusion.2.refs_0_, bf16[4,544,128]{2,1,0:T(8,128)(2,1)S(1)} %pad_maximum_fusion.refs_1_, bf16[4,544,128]{2,1,0:T(8,128)(2,1)S(1)} %collective-permute-done.11.refs_2_), custom_call_target="tpu_custom_call" | custom-call | flops 100000000 | bytes 300000 | tf_op jit(solution)/shard_map/pallas_call | solution.py:577
  119.0 1.4 %shard_map.221 = bf16[2,16,1024]{2,1,0:T(8,128)(2,1)} custom-call(s32[2,1024]{1,0:T(2,128)S(1)} %copy-done, bf16[16,2,16,128]{3,2,1,0:T(8,128)(2,1)S(1)} %bitcast.40), custom_call_target="tpu_custom_call" | custom-call | flops 100000000 | bytes 300000 | tf_op jit(solution)/shard_map/pallas_call | solution.py:802
  122.1 3.1 %shard_map.220 = (f32[128,16384]{1,0:T(8,128)}, f32[128,128]{1,0:T(8,128)}, f32[128,384]{1,0:T(8,128)}, f32[128,384]{1,0:T(8,128)}, f32[128,128]{1,0:T(8,128)S(1)}) custom-call(s32[4]{0:T(128)S(1)} %pad_add_fusion.1.refs_0_, ...), custom_call_target="tpu_custom_call", output_to_operand_aliasing={{0}: (5, {}), {1}: (6, {}), {2}: (7, {}), {3}: (8, {}), {4}... | custom-call | flops 100000000 | bytes 300000 | tf_op jit(solution)/shard_map/pallas_call | solution.py:577
  (56 shorter events, 22.2 us)
Async XLA Ops:
  3.7 17.0 %all-to-all-start = ((bf16[16,48,128]{2,1,0:T(8,128)(2,1)}), bf16[16,48,128]{2,1,0:T(8,128)(2,1)S(1)}, u32[]{:S(2)}, u32[]{:S(2)}) async-start(bf16[16,48,128]{2,1,0:T(8,128)(2,1)} %shard_map.212), calls=%async_computation | async-start | bytes 393216 | tf_op jit(solution)/shard_map/all_to_all | solution.py:619
  39.7 3.0 %collective-permute-start = (bf16[2,4,16,4352]{3,2,1,0:T(8,128)(2,1)}, bf16[2,4,16,4352]{3,2,1,0:T(8,128)(2,1)S(1)}, u32[]{:S(2)}, u32[]{:S(2)}) collective-permute-start(bf16[2,4,16,4352]{3,2,1,0:T(8,128)(2,1)} %get-tuple-element.80), channel_id=1, source_target_pairs={{0,16},{16,0},{1,17},{17,1},{2,18},{18,2},{3,19},{19,3},{4,20},{20... | collective-permute-start | bytes 3342344 | tf_op jit(solution)/shard_map/ppermute | solution.py:689
  39.8 20.3 %collective-permute-start.1 = (bf16[2,4,16,4352]{3,2,1,0:T(8,128)(2,1)}, bf16[2,4,16,4352]{3,2,1,0:T(8,128)(2,1)S(1)}, u32[]{:S(2)}, u32[]{:S(2)}) collective-permute-start(bf16[2,4,16,4352]{3,2,1,0:T(8,128)(2,1)} %get-tuple-element.87), channel_id=1, source_target_pairs={{0,16},{16,0},{1,17},{17,1},{2,18},{18,2},{3,19},{19,3},{4,20},{20... | collective-permute-start | bytes 3342344 | tf_op jit(solution)/shard_map/ppermute | solution.py:689
  43.0 17.1 %collective-permute-start.2 = (bf16[2,4,16,4352]{3,2,1,0:T(8,128)(2,1)S(1)}, bf16[2,4,16,4352]{3,2,1,0:T(8,128)(2,1)}, u32[]{:S(2)}, u32[]{:S(2)}) collective-permute-start(bf16[2,4,16,4352]{3,2,1,0:T(8,128)(2,1)S(1)} %shard_map.215), channel_id=1, source_target_pairs={{0,1},{1,0},{2,3},{3,2},{4,5},{5,4},{6,7},{7,6},{8,9},{9,8},{10,11... | collective-permute-start | bytes 3342344 | tf_op jit(solution)/shard_map/ppermute | solution.py:696
  45.7 14.4 %copy-start.2 = (bf16[2,4,16,4352]{3,2,1,0:T(8,128)(2,1)S(1)}, bf16[2,4,16,4352]{3,2,1,0:T(8,128)(2,1)}, u32[]{:S(2)}) copy-start(bf16[2,4,16,4352]{3,2,1,0:T(8,128)(2,1)} %get-tuple-element.86) | copy-start | bytes 3342340
  61.4 9.6 %collective-permute-start.3 = (bf16[2,2,16,4352]{3,2,1,0:T(8,128)(2,1)S(1)}, bf16[2,2,16,4352]{3,2,1,0:T(8,128)(2,1)S(1)}, u32[]{:S(2)}, u32[]{:S(2)}) collective-permute-start(bf16[2,2,16,4352]{3,2,1,0:T(8,128)(2,1)S(1)} %fusion), channel_id=1, source_target_pairs={{0,2},{1,3},{2,0},{3,1},{4,6},{5,7},{6,4},{7,5},{8,10},{9,11},{10,... | collective-permute-start | bytes 1671176 | tf_op jit(solution)/shard_map/ppermute | solution.py:696
  68.2 5.4 %copy-start.4 = (f32[32,128]{1,0:T(8,128)S(1)}, f32[32,128]{1,0:T(8,128)}, u32[]{:S(2)}) copy-start(f32[32,128]{1,0:T(8,128)} %get-tuple-element.93) | copy-start | bytes 49156
  72.1 6.8 %collective-permute-start.4 = (bf16[2,16,4352]{2,1,0:T(8,128)(2,1)S(1)}, bf16[2,16,4352]{2,1,0:T(8,128)(2,1)S(1)}, u32[]{:S(2)}, u32[]{:S(2)}) collective-permute-start(bf16[2,16,4352]{2,1,0:T(8,128)(2,1)S(1)} %fusion.1), channel_id=1, source_target_pairs={{0,4},{1,5},{2,6},{3,7},{4,0},{5,1},{6,2},{7,3},{8,12},{9,13},{10,... | collective-permute-start | bytes 835592 | tf_op jit(solution)/shard_map/ppermute | solution.py:696
  73.6 5.3 %collective-permute-start.5 = (f32[32,128]{1,0:T(8,128)S(1)}, f32[32,128]{1,0:T(8,128)S(1)}, u32[]{:S(2)}, u32[]{:S(2)}) collective-permute-start(f32[32,128]{1,0:T(8,128)S(1)} %copy-done.4), channel_id=1, source_target_pairs={{0,4},{1,5},{2,6},{3,7},{4,0},{5,1},{6,2},{7,3},{8,12},{9,13},{10,... | collective-permute-start | bytes 49160 | tf_op jit(solution)/shard_map/ppermute | solution.py:696
  80.0 13.8 %collective-permute-start.6 = (bf16[2,16,4352]{2,1,0:T(8,128)(2,1)S(1)}, bf16[2,16,4352]{2,1,0:T(8,128)(2,1)S(1)}, u32[]{:S(2)}, u32[]{:S(2)}) collective-permute-start(bf16[2,16,4352]{2,1,0:T(8,128)(2,1)S(1)} %fusion.3.first_ref), channel_id=1, source_target_pairs={{0,8},{1,9},{2,10},{3,11},{4,12},{5,13},{6,14},{7,15},{8,0},{9,1},... | collective-permute-start | bytes 835592 | tf_op jit(solution)/shard_map/ppermute | solution.py:696
  81.2 3.7 %collective-permute-start.7 = (f32[32,128]{1,0:T(8,128)S(1)}, f32[32,128]{1,0:T(8,128)S(1)}, u32[]{:S(2)}, u32[]{:S(2)}) collective-permute-start(f32[32,128]{1,0:T(8,128)S(1)} %add.165), channel_id=1, source_target_pairs={{0,1},{1,0},{2,3},{3,2},{4,5},{5,4},{6,7},{7,6},{8,9},{9,8},{10,11... | collective-permute-start | bytes 49160 | tf_op jit(solution)/shard_map/ppermute | solution.py:696
  85.0 3.7 %collective-permute-start.8 = (f32[32,128]{1,0:T(8,128)S(1)}, f32[32,128]{1,0:T(8,128)S(1)}, u32[]{:S(2)}, u32[]{:S(2)}) collective-permute-start(f32[32,128]{1,0:T(8,128)S(1)} %add.166), channel_id=1, source_target_pairs={{0,2},{1,3},{2,0},{3,1},{4,6},{5,7},{6,4},{7,5},{8,10},{9,11},{10,... | collective-permute-start | bytes 49160 | tf_op jit(solution)/shard_map/ppermute | solution.py:696
  94.2 7.0 %collective-permute-start.9 = (bf16[2,544,128]{2,1,0:T(8,128)(2,1)S(1)}, bf16[2,544,128]{2,1,0:T(8,128)(2,1)S(1)}, u32[]{:S(2)}, u32[]{:S(2)}) collective-permute-start(bf16[2,544,128]{2,1,0:T(8,128)(2,1)S(1)} %shard_map.218), channel_id=1, source_target_pairs={{0,4},{1,5},{2,6},{3,7},{4,0},{5,1},{6,2},{7,3},{8,12},{9,13},{10,... | collective-permute-start | bytes 835592 | tf_op jit(solution)/shard_map/ppermute | solution.py:696
  94.3 24.7 %copy-start = (s32[2,1024]{1,0:T(2,128)S(1)}, s32[2,1024]{1,0:T(2,128)}, u32[]{:S(2)}) copy-start(s32[2,1024]{1,0:T(2,128)} %src_ref.3) | copy-start | bytes 24580
  94.3 4.7 %collective-permute-start.10 = (f32[32,128]{1,0:T(8,128)S(1)}, f32[32,128]{1,0:T(8,128)S(1)}, u32[]{:S(2)}, u32[]{:S(2)}) collective-permute-start(f32[32,128]{1,0:T(8,128)S(1)} %add.167), channel_id=1, source_target_pairs={{0,8},{1,9},{2,10},{3,11},{4,12},{5,13},{6,14},{7,15},{8,0},{9,1},... | collective-permute-start | bytes 49160 | tf_op jit(solution)/shard_map/ppermute | solution.py:696
  101.2 9.7 %collective-permute-start.12 = (bf16[4,544,128]{2,1,0:T(8,128)(2,1)S(1)}, bf16[4,544,128]{2,1,0:T(8,128)(2,1)S(1)}, u32[]{:S(2)}, u32[]{:S(2)}) collective-permute-start(bf16[4,544,128]{2,1,0:T(8,128)(2,1)S(1)} %pad_maximum_fusion.refs_1_), channel_id=1, source_target_pairs={{0,2},{1,3},{2,0},{3,1},{4,6},{5,7},{6,4},{7,5},{8,10},{9,11},{10,... | collective-permute-start | bytes 1671176 | tf_op jit(solution)/shard_map/ppermute | solution.py:696
  102.5 13.7 %collective-permute-start.11 = (bf16[4,544,128]{2,1,0:T(8,128)(2,1)S(1)}, bf16[4,544,128]{2,1,0:T(8,128)(2,1)S(1)}, u32[]{:S(2)}, u32[]{:S(2)}) collective-permute-start(bf16[4,544,128]{2,1,0:T(8,128)(2,1)S(1)} %pad_maximum_fusion.refs_1_), channel_id=1, source_target_pairs={{0,16},{16,0},{1,17},{17,1},{2,18},{18,2},{3,19},{19,3},{4,20},{20... | collective-permute-start | bytes 1671176 | tf_op jit(solution)/shard_map/ppermute | solution.py:689
  102.5 15.8 %collective-permute-start.14 = (bf16[4,544,128]{2,1,0:T(8,128)(2,1)S(1)}, bf16[4,544,128]{2,1,0:T(8,128)(2,1)S(1)}, u32[]{:S(2)}, u32[]{:S(2)}) collective-permute-start(bf16[4,544,128]{2,1,0:T(8,128)(2,1)S(1)} %pad_maximum_fusion.refs_1_), channel_id=1, source_target_pairs={{0,1},{1,0},{2,3},{3,2},{4,5},{5,4},{6,7},{7,6},{8,9},{9,8},{10,11... | collective-permute-start | bytes 1671176 | tf_op jit(solution)/shard_map/ppermute | solution.py:696
  103.5 12.7 %all-to-all-start.1 = ((bf16[16,32,128]{2,1,0:T(8,128)(2,1)}), bf16[16,32,128]{2,1,0:T(8,128)(2,1)S(1)}, u32[]{:S(2)}, u32[]{:S(2)}) async-start(bf16[16,32,128]{2,1,0:T(8,128)(2,1)} %get-tuple-element.108), calls=%async_computation.1 | async-start | bytes 262144 | tf_op jit(solution)/shard_map/all_to_all | solution.py:788
  107.0 1.2 collective-permute-start.13
  110.9 14.3 %collective-permute-start.17 = (bf16[4,544,128]{2,1,0:T(8,128)(2,1)S(1)}, bf16[4,544,128]{2,1,0:T(8,128)(2,1)S(1)}, u32[]{:S(2)}, u32[]{:S(2)}) collective-permute-start(bf16[4,544,128]{2,1,0:T(8,128)(2,1)S(1)} %collective-permute-done.12.refs_1_), channel_id=1, source_target_pairs={{0,1},{1,0},{2,3},{3,2},{4,5},{5,4},{6,7},{7,6},{8,9},{9,8},{10,11... | collective-permute-start | bytes 1671176 | tf_op jit(solution)/shard_map/ppermute | solution.py:696
  118.3 3.8 %collective-permute-start.15 = (bf16[4,544,128]{2,1,0:T(8,128)(2,1)S(1)}, bf16[4,544,128]{2,1,0:T(8,128)(2,1)S(1)}, u32[]{:S(2)}, u32[]{:S(2)}) collective-permute-start(bf16[4,544,128]{2,1,0:T(8,128)(2,1)S(1)} %collective-permute-done.12.refs_1_), channel_id=1, source_target_pairs={{0,16},{16,0},{1,17},{17,1},{2,18},{18,2},{3,19},{19,3},{4,20},{20... | collective-permute-start | bytes 1671176 | tf_op jit(solution)/shard_map/ppermute | solution.py:689
  118.4 3.7 %collective-permute-start.16 = (bf16[4,544,128]{2,1,0:T(8,128)(2,1)S(1)}, bf16[4,544,128]{2,1,0:T(8,128)(2,1)S(1)}, u32[]{:S(2)}, u32[]{:S(2)}) collective-permute-start(bf16[4,544,128]{2,1,0:T(8,128)(2,1)S(1)} %collective-permute-done.14.refs_3_), channel_id=1, source_target_pairs={{0,16},{16,0},{1,17},{17,1},{2,18},{18,2},{3,19},{19,3},{4,20},{20... | collective-permute-start | bytes 1671176 | tf_op jit(solution)/shard_map/ppermute | solution.py:689
  125.2 2.0 %collective-permute-start.18 = (bf16[4,544,128]{2,1,0:T(8,128)(2,1)S(1)}, bf16[4,544,128]{2,1,0:T(8,128)(2,1)S(1)}, u32[]{:S(2)}, u32[]{:S(2)}) collective-permute-start(bf16[4,544,128]{2,1,0:T(8,128)(2,1)S(1)} %collective-permute-done.17.refs_1_), channel_id=1, source_target_pairs={{0,16},{16,0},{1,17},{17,1},{2,18},{18,2},{3,19},{19,3},{4,20},{20... | collective-permute-start | bytes 1671176 | tf_op jit(solution)/shard_map/ppermute | solution.py:689
  (2 other events, 1.9 us)

commit v3 on v2

--- a/solution.py
+++ b/solution.py
@@ -762,8 +762,6 @@
         if step == 1:
             d_feats, first = second_grads(after(d_pairs, give))
             got = after(got, first)
-        if step == 2:
-            got, first = added_at(got, first, 4)
         terms.append(got)
         if step == 0:
             terms = [one.reshape((2, 2, 2) + one.shape[2:]) for one in terms]
@@ -774,6 +772,8 @@
             got, first = added_at(got, first, 1 << extra)
         if extra < owners.bit_length() - 2:
             total = added([total, got]).astype(BF16)
+    first = after(first, total)
+    first = first + swap(first, [4] * cores)
     first = first + swap(first, [1] * cores)
     got, first = added_at(got, first, 2)
     held = rows_of(total, got)

time: 129 us -> 130 us (level)
  starting transfers between devices: 27.6 us -> 30.5 us
  waiting for transfers between devices: 35.4 us -> 33.3 us
    ppermute x12, waiting for transfers between devices: 25.7 us -> 22.9 us  [swap(): return lax.ppermute(value, ('graph', 'edge'), moves)]
    all_to_all x1, starting transfers between devices: 3.51 us -> 5.51 us  [body(): back = lax.all_to_all(back, 'edge', 0, 0, tiled=True)]
  transfers between devices with their start and end apart: 21 -> 21, of which waited for: 13 -> 12; matrix products, arithmetic and copies ran while one was open for 6% -> 6% of each run, Pallas kernels for 22% -> 22%
where the time goes in v3:
time: 130 us; the launch traced here: 129 us
  Pallas kernels  51 us (39%)
  waiting for transfers between devices  33.3 us (26%)
  starting transfers between devices  30.5 us (23%)
  local copies, waits for them, and re-layouts  9.08 us (7%)
  other arithmetic  4.3 us (3%)
    ppermute x12, waiting for transfers between devices, swap(): return lax.ppermute(value, ('graph', 'edge'), moves)  22.9 us
    pallas_call x1, Pallas kernels, body(): full_call(main_kernel, (jax.ShapeDtypeStruct((batches * own, width), BF16...  18.3 us
    ppermute x12, starting transfers between devices, swap(): return lax.ppermute(value, ('graph', 'edge'), moves)  15.2 us
    pallas_call x1, Pallas kernels, first_grads(): full_call(back_kernel, (jax.ShapeDtypeStruct((batches, own, width), BF16)...  14.4 us
    all_to_all x1, starting transfers between devices, body(): edge_data = lax.all_to_all(sent, 'edge', 0, 0, tiled=True)  8.31 us
    pallas_call x4, Pallas kernels, place_pieces(): pl.pallas_call(functools.partial(place_kernel, tall, count, len(before)),...  7.43 us
    unnamed x11, local copies, waits for them, and re-layouts  7.39 us
    pallas_call x1, Pallas kernels, second_grads(): full_call(edge_kernel, (jax.ShapeDtypeStruct((blocks, batches * feat_coun...  5.72 us
  transfers between devices with their start and end apart: 21, of which 12 were waited for; matrix products, arithmetic and copies ran while one was open for 6% of the time, Pallas kernels for 22%

profile of v3, /device:TPU:0, one launch (start us, length us, event | category | flops | bytes accessed | tf_op | source)
XLA Modules:
  0.0 129.2 jit_solution(987359614811383846)
XLA Ops:
  0.6 3.0 %shard_map.212 = bf16[16,48,128]{2,1,0:T(8,128)(2,1)} custom-call(s32[2,1024]{1,0:T(2,128)} %src_ref.3, s32[2,1024]{1,0:T(2,128)} %dst_ref.1, bf16[2,16,1024]{2,1,0:T(8,128)(2,1)} %feat_ref.1), custom_call_target="tpu_custom_call" | custom-call | tf_op jit(solution)/shard_map/pallas_call | solution.py:614
  3.7 8.3 %all-to-all-start = ((bf16[16,48,128]{2,1,0:T(8,128)(2,1)}), bf16[16,48,128]{2,1,0:T(8,128)(2,1)S(1)}, u32[]{:S(2)}, u32[]{:S(2)}) async-start(bf16[16,48,128]{2,1,0:T(8,128)(2,1)} %shard_map.212), calls=%async_computation | async-start | bytes 393216 | tf_op jit(solution)/shard_map/all_to_all | solution.py:619
  12.0 5.4 %copy.39 = bf16[16,8,128,128]{3,2,1,0:T(8,128)(2,1)} copy(bf16[16,8,128,128]{3,1,2,0:T(8,128)(2,1)} %bitcast.43) | data formatting | bytes 8388608
  18.1 2.6 %all-to-all-done.edge_ref = bf16[16,48,128]{2,1,0:T(8,128)(2,1)S(1)} async-done(((bf16[16,48,128]{2,1,0:T(8,128)(2,1)}), bf16[16,48,128]{2,1,0:T(8,128)(2,1)S(1)}, u32[]{:S(2)}, u32[]{:S(2)}) %all-to-all-start) | async-done | bytes 196640 | tf_op jit(solution)/shard_map/all_to_all | solution.py:619
  21.3 18.3 %shard_map.213 = (bf16[128,128]{1,0:T(8,128)(2,1)}, bf16[2,4,16,4352]{3,2,1,0:T(8,128)(2,1)}, bf16[2,4,16,4352]{3,2,1,0:T(8,128)(2,1)}, bf16[2,4,16,4352]{3,2,1,...) custom-call(s32[3]{0:T(128)} %pad_add_fusion.where_ref, ...), custom_call_target="tpu_custom_call" | custom-call | tf_op jit(solution)/shard_map/pallas_call | solution.py:645
  43.0 2.7 %collective-permute-start.2 = (bf16[2,4,16,4352]{3,2,1,0:T(8,128)(2,1)S(1)}, bf16[2,4,16,4352]{3,2,1,0:T(8,128)(2,1)}, u32[]{:S(2)}, u32[]{:S(2)}) collective-permute-start(bf16[2,4,16,4352]{3,2,1,0:T(8,128)(2,1)S(1)} %shard_map.215), channel_id=1, source_target_pairs={{0,1},{1,0},{2,3},{3,2},{4,5},{5,4},{6,7},{7,6},{8,9},{9,8},{10,11... | collective-permute-start | bytes 3342344 | tf_op jit(solution)/shard_map/ppermute | solution.py:696
  45.7 14.4 %shard_map.216 = (bf16[2,64,128]{2,1,0:T(8,128)(2,1)}, bf16[2,1056,512]{2,1,0:T(8,128)(2,1)}) custom-call(bf16[2,4224,128]{2,1,0:T(8,128)(2,1)} %get-tuple-element.80.g_far, bf16[128,256]{1,0:T(8,128)(2,1)} %get-tuple-element.81.level_ref, bf16[128,256]{1,0:T(8,128)(2,1)} %get-tuple-element.82.dm_ref, f32[128,128]{1,0:T(8,128)} %get-tuple-element.83.base_ref, ...), custom_call_target="tpu_custom_call" | custom-call | flops 12000000000 | bytes 36000000 | tf_op jit(solution)/shard_map/pallas_call | solution.py:711
  61.9 5.7 %shard_map.217 = (bf16[16,32,128]{2,1,0:T(8,128)(2,1)}, f32[32,128]{1,0:T(8,128)}) custom-call(s32[2,17]{1,0:T(2,128)} %get-tuple-element.88.order_ref, bf16[16,48,128]{2,1,0:T(8,128)(2,1)} %copy-done.3, bf16[2,1056,512]{2,1,0:T(8,128)(2,1)} %get-tuple-element.90.dg_ref, bf16[16,128]{1,0:T(8,128)(2,1)} %w_in_ref.3, f32[128]{0:T(128)} %b_in_ref.3, ...), custom_call_target="tpu_custom_call" | custom-call | flops 8999999488 | bytes 27000000 | tf_op jit(solution)/shard_map/pallas_call | solution.py:729
  67.6 3.3 %collective-permute-done.3 = bf16[2,2,16,4352]{3,2,1,0:T(8,128)(2,1)S(1)} collective-permute-done((bf16[2,2,16,4352]{3,2,1,0:T(8,128)(2,1)S(1)}, bf16[2,2,16,4352]{3,2,1,0:T(8,128)(2,1)S(1)}, u32[]{:S(2)}, u32[]{:S(2)}) %collective-permute-start.3) | collective-permute-done | bytes 557088 | tf_op jit(solution)/shard_map/ppermute | solution.py:696
  72.1 1.3 collective-permute-start.4
  73.4 5.3 %collective-permute-done.4 = bf16[2,16,4352]{2,1,0:T(8,128)(2,1)S(1)} collective-permute-done((bf16[2,16,4352]{2,1,0:T(8,128)(2,1)S(1)}, bf16[2,16,4352]{2,1,0:T(8,128)(2,1)S(1)}, u32[]{:S(2)}, u32[]{:S(2)}) %collective-permute-start.4) | collective-permute-done | bytes 278560 | tf_op jit(solution)/shard_map/ppermute | solution.py:696
  79.8 1.9 %collective-permute-start.5 = (bf16[2,16,4352]{2,1,0:T(8,128)(2,1)S(1)}, bf16[2,16,4352]{2,1,0:T(8,128)(2,1)S(1)}, u32[]{:S(2)}, u32[]{:S(2)}) collective-permute-start(bf16[2,16,4352]{2,1,0:T(8,128)(2,1)S(1)} %fusion.3.first_ref), channel_id=1, source_target_pairs={{0,8},{1,9},{2,10},{3,11},{4,12},{5,13},{6,14},{7,15},{8,0},{9,1},... | collective-permute-start | bytes 835592 | tf_op jit(solution)/shard_map/ppermute | solution.py:696
  82.1 3.9 %collective-permute-done.6 = f32[32,128]{1,0:T(8,128)S(1)} collective-permute-done((f32[32,128]{1,0:T(8,128)S(1)}, f32[32,128]{1,0:T(8,128)S(1)}, u32[]{:S(2)}, u32[]{:S(2)}) %collective-permute-start.6) | collective-permute-done | bytes 16416 | tf_op jit(solution)/shard_map/ppermute | solution.py:696
  86.9 2.8 %collective-permute-done.7 = f32[32,128]{1,0:T(8,128)S(1)} collective-permute-done((f32[32,128]{1,0:T(8,128)S(1)}, f32[32,128]{1,0:T(8,128)S(1)}, u32[]{:S(2)}, u32[]{:S(2)}) %collective-permute-start.7) | collective-permute-done | bytes 16416 | tf_op jit(solution)/shard_map/ppermute | solution.py:696
  89.8 1.6 %collective-permute-start.8 = (f32[32,128]{1,0:T(8,128)S(1)}, f32[32,128]{1,0:T(8,128)S(1)}, u32[]{:S(2)}, u32[]{:S(2)}) collective-permute-start(f32[32,128]{1,0:T(8,128)S(1)} %add.166), channel_id=1, source_target_pairs={{0,2},{1,3},{2,0},{3,1},{4,6},{5,7},{6,4},{7,5},{8,10},{9,11},{10,... | collective-permute-start | bytes 49160 | tf_op jit(solution)/shard_map/ppermute | solution.py:696
  91.3 2.1 %collective-permute-done.8 = f32[32,128]{1,0:T(8,128)S(1)} collective-permute-done((f32[32,128]{1,0:T(8,128)S(1)}, f32[32,128]{1,0:T(8,128)S(1)}, u32[]{:S(2)}, u32[]{:S(2)}) %collective-permute-start.8) | collective-permute-done | bytes 16416 | tf_op jit(solution)/shard_map/ppermute | solution.py:696
  93.9 2.7 %collective-permute-start.9 = (bf16[2,544,128]{2,1,0:T(8,128)(2,1)S(1)}, bf16[2,544,128]{2,1,0:T(8,128)(2,1)S(1)}, u32[]{:S(2)}, u32[]{:S(2)}) collective-permute-start(bf16[2,544,128]{2,1,0:T(8,128)(2,1)S(1)} %shard_map.218), channel_id=1, source_target_pairs={{0,4},{1,5},{2,6},{3,7},{4,0},{5,1},{6,2},{7,3},{8,12},{9,13},{10,... | collective-permute-start | bytes 835592 | tf_op jit(solution)/shard_map/ppermute | solution.py:696
  96.9 4.4 %collective-permute-done.10 = f32[32,128]{1,0:T(8,128)S(1)} collective-permute-done((f32[32,128]{1,0:T(8,128)S(1)}, f32[32,128]{1,0:T(8,128)S(1)}, u32[]{:S(2)}, u32[]{:S(2)}) %collective-permute-start.10) | collective-permute-done | bytes 16416 | tf_op jit(solution)/shard_map/ppermute | solution.py:696
  101.4 1.6 %collective-permute-start.12 = (bf16[4,544,128]{2,1,0:T(8,128)(2,1)S(1)}, bf16[4,544,128]{2,1,0:T(8,128)(2,1)S(1)}, u32[]{:S(2)}, u32[]{:S(2)}) collective-permute-start(bf16[4,544,128]{2,1,0:T(8,128)(2,1)S(1)} %pad_maximum_fusion.refs_1_), channel_id=1, source_target_pairs={{0,2},{1,3},{2,0},{3,1},{4,6},{5,7},{6,4},{7,5},{8,10},{9,11},{10,... | collective-permute-start | bytes 1671176 | tf_op jit(solution)/shard_map/ppermute | solution.py:696
  103.3 5.5 %all-to-all-start.1 = ((bf16[16,32,128]{2,1,0:T(8,128)(2,1)}), bf16[16,32,128]{2,1,0:T(8,128)(2,1)S(1)}, u32[]{:S(2)}, u32[]{:S(2)}) async-start(bf16[16,32,128]{2,1,0:T(8,128)(2,1)} %get-tuple-element.106), calls=%async_computation.1 | async-start | bytes 262144 | tf_op jit(solution)/shard_map/all_to_all | solution.py:788
  112.0 5.0 %all-to-all-done.1 = bf16[16,32,128]{2,1,0:T(8,128)(2,1)S(1)} async-done(((bf16[16,32,128]{2,1,0:T(8,128)(2,1)}), bf16[16,32,128]{2,1,0:T(8,128)(2,1)S(1)}, u32[]{:S(2)}, u32[]{:S(2)}) %all-to-all-start.1) | async-done | bytes 131104 | tf_op jit(solution)/shard_map/all_to_all | solution.py:788
  116.9 2.1 %shard_map.219 = (f32[128,16384]{1,0:T(8,128)}, f32[128,128]{1,0:T(8,128)}, f32[128,384]{1,0:T(8,128)}, f32[128,384]{1,0:T(8,128)}, f32[128,128]{1,0:T(8,128)S(1)}) custom-call(s32[2]{0:T(128)S(1)} %pad_add_fusion.2.refs_0_, bf16[4,544,128]{2,1,0:T(8,128)(2,1)S(1)} %pad_maximum_fusion.refs_1_, bf16[4,544,128]{2,1,0:T(8,128)(2,1)S(1)} %collective-permute-done.11.refs_2_), custom_call_target="tpu_custom_call" | custom-call | flops 100000000 | bytes 300000 | tf_op jit(solution)/shard_map/pallas_call | solution.py:577
  119.7 1.4 %shard_map.221 = bf16[2,16,1024]{2,1,0:T(8,128)(2,1)} custom-call(s32[2,1024]{1,0:T(2,128)S(1)} %copy-done, bf16[16,2,16,128]{3,2,1,0:T(8,128)(2,1)S(1)} %bitcast.40), custom_call_target="tpu_custom_call" | custom-call | flops 100000000 | bytes 300000 | tf_op jit(solution)/shard_map/pallas_call | solution.py:802
  122.8 3.1 %shard_map.220 = (f32[128,16384]{1,0:T(8,128)}, f32[128,128]{1,0:T(8,128)}, f32[128,384]{1,0:T(8,128)}, f32[128,384]{1,0:T(8,128)}, f32[128,128]{1,0:T(8,128)S(1)}) custom-call(s32[4]{0:T(128)S(1)} %pad_add_fusion.1.refs_0_, ...), custom_call_target="tpu_custom_call", output_to_operand_aliasing={{0}: (5, {}), {1}: (6, {}), {2}: (7, {}), {3}: (8, {}), {4}... | custom-call | flops 100000000 | bytes 300000 | tf_op jit(solution)/shard_map/pallas_call | solution.py:577
  (56 shorter events, 19.5 us)
Async XLA Ops:
  3.7 17.0 %all-to-all-start = ((bf16[16,48,128]{2,1,0:T(8,128)(2,1)}), bf16[16,48,128]{2,1,0:T(8,128)(2,1)S(1)}, u32[]{:S(2)}, u32[]{:S(2)}) async-start(bf16[16,48,128]{2,1,0:T(8,128)(2,1)} %shard_map.212), calls=%async_computation | async-start | bytes 393216 | tf_op jit(solution)/shard_map/all_to_all | solution.py:619
  39.7 3.0 %collective-permute-start = (bf16[2,4,16,4352]{3,2,1,0:T(8,128)(2,1)}, bf16[2,4,16,4352]{3,2,1,0:T(8,128)(2,1)S(1)}, u32[]{:S(2)}, u32[]{:S(2)}) collective-permute-start(bf16[2,4,16,4352]{3,2,1,0:T(8,128)(2,1)} %get-tuple-element.79), channel_id=1, source_target_pairs={{0,16},{16,0},{1,17},{17,1},{2,18},{18,2},{3,19},{19,3},{4,20},{20... | collective-permute-start | bytes 3342344 | tf_op jit(solution)/shard_map/ppermute | solution.py:689
  39.8 20.3 %collective-permute-start.1 = (bf16[2,4,16,4352]{3,2,1,0:T(8,128)(2,1)}, bf16[2,4,16,4352]{3,2,1,0:T(8,128)(2,1)S(1)}, u32[]{:S(2)}, u32[]{:S(2)}) collective-permute-start(bf16[2,4,16,4352]{3,2,1,0:T(8,128)(2,1)} %get-tuple-element.86), channel_id=1, source_target_pairs={{0,16},{16,0},{1,17},{17,1},{2,18},{18,2},{3,19},{19,3},{4,20},{20... | collective-permute-start | bytes 3342344 | tf_op jit(solution)/shard_map/ppermute | solution.py:689
  43.0 17.1 %collective-permute-start.2 = (bf16[2,4,16,4352]{3,2,1,0:T(8,128)(2,1)S(1)}, bf16[2,4,16,4352]{3,2,1,0:T(8,128)(2,1)}, u32[]{:S(2)}, u32[]{:S(2)}) collective-permute-start(bf16[2,4,16,4352]{3,2,1,0:T(8,128)(2,1)S(1)} %shard_map.215), channel_id=1, source_target_pairs={{0,1},{1,0},{2,3},{3,2},{4,5},{5,4},{6,7},{7,6},{8,9},{9,8},{10,11... | collective-permute-start | bytes 3342344 | tf_op jit(solution)/shard_map/ppermute | solution.py:696
  45.7 14.4 %copy-start.2 = (bf16[2,4,16,4352]{3,2,1,0:T(8,128)(2,1)S(1)}, bf16[2,4,16,4352]{3,2,1,0:T(8,128)(2,1)}, u32[]{:S(2)}) copy-start(bf16[2,4,16,4352]{3,2,1,0:T(8,128)(2,1)} %get-tuple-element.85) | copy-start | bytes 3342340
  61.4 9.6 %collective-permute-start.3 = (bf16[2,2,16,4352]{3,2,1,0:T(8,128)(2,1)S(1)}, bf16[2,2,16,4352]{3,2,1,0:T(8,128)(2,1)S(1)}, u32[]{:S(2)}, u32[]{:S(2)}) collective-permute-start(bf16[2,2,16,4352]{3,2,1,0:T(8,128)(2,1)S(1)} %fusion), channel_id=1, source_target_pairs={{0,2},{1,3},{2,0},{3,1},{4,6},{5,7},{6,4},{7,5},{8,10},{9,11},{10,... | collective-permute-start | bytes 1671176 | tf_op jit(solution)/shard_map/ppermute | solution.py:696
  72.1 9.7 %copy-start.4 = (f32[32,128]{1,0:T(8,128)S(1)}, f32[32,128]{1,0:T(8,128)}, u32[]{:S(2)}) copy-start(f32[32,128]{1,0:T(8,128)} %get-tuple-element.94) | copy-start | bytes 49156
  72.1 6.6 %collective-permute-start.4 = (bf16[2,16,4352]{2,1,0:T(8,128)(2,1)S(1)}, bf16[2,16,4352]{2,1,0:T(8,128)(2,1)S(1)}, u32[]{:S(2)}, u32[]{:S(2)}) collective-permute-start(bf16[2,16,4352]{2,1,0:T(8,128)(2,1)S(1)} %fusion.1), channel_id=1, source_target_pairs={{0,4},{1,5},{2,6},{3,7},{4,0},{5,1},{6,2},{7,3},{8,12},{9,13},{10,... | collective-permute-start | bytes 835592 | tf_op jit(solution)/shard_map/ppermute | solution.py:696
  79.8 13.7 %collective-permute-start.5 = (bf16[2,16,4352]{2,1,0:T(8,128)(2,1)S(1)}, bf16[2,16,4352]{2,1,0:T(8,128)(2,1)S(1)}, u32[]{:S(2)}, u32[]{:S(2)}) collective-permute-start(bf16[2,16,4352]{2,1,0:T(8,128)(2,1)S(1)} %fusion.3.first_ref), channel_id=1, source_target_pairs={{0,8},{1,9},{2,10},{3,11},{4,12},{5,13},{6,14},{7,15},{8,0},{9,1},... | collective-permute-start | bytes 835592 | tf_op jit(solution)/shard_map/ppermute | solution.py:696
  81.8 4.2 %collective-permute-start.6 = (f32[32,128]{1,0:T(8,128)S(1)}, f32[32,128]{1,0:T(8,128)S(1)}, u32[]{:S(2)}, u32[]{:S(2)}) collective-permute-start(f32[32,128]{1,0:T(8,128)S(1)} %copy-done.4), channel_id=1, source_target_pairs={{0,4},{1,5},{2,6},{3,7},{4,0},{5,1},{6,2},{7,3},{8,12},{9,13},{10,... | collective-permute-start | bytes 49160 | tf_op jit(solution)/shard_map/ppermute | solution.py:696
  86.0 3.7 %collective-permute-start.7 = (f32[32,128]{1,0:T(8,128)S(1)}, f32[32,128]{1,0:T(8,128)S(1)}, u32[]{:S(2)}, u32[]{:S(2)}) collective-permute-start(f32[32,128]{1,0:T(8,128)S(1)} %add.165), channel_id=1, source_target_pairs={{0,1},{1,0},{2,3},{3,2},{4,5},{5,4},{6,7},{7,6},{8,9},{9,8},{10,11... | collective-permute-start | bytes 49160 | tf_op jit(solution)/shard_map/ppermute | solution.py:696
  89.8 3.7 %collective-permute-start.8 = (f32[32,128]{1,0:T(8,128)S(1)}, f32[32,128]{1,0:T(8,128)S(1)}, u32[]{:S(2)}, u32[]{:S(2)}) collective-permute-start(f32[32,128]{1,0:T(8,128)S(1)} %add.166), channel_id=1, source_target_pairs={{0,2},{1,3},{2,0},{3,1},{4,6},{5,7},{6,4},{7,5},{8,10},{9,11},{10,... | collective-permute-start | bytes 49160 | tf_op jit(solution)/shard_map/ppermute | solution.py:696
  93.9 7.4 %collective-permute-start.9 = (bf16[2,544,128]{2,1,0:T(8,128)(2,1)S(1)}, bf16[2,544,128]{2,1,0:T(8,128)(2,1)S(1)}, u32[]{:S(2)}, u32[]{:S(2)}) collective-permute-start(bf16[2,544,128]{2,1,0:T(8,128)(2,1)S(1)} %shard_map.218), channel_id=1, source_target_pairs={{0,4},{1,5},{2,6},{3,7},{4,0},{5,1},{6,2},{7,3},{8,12},{9,13},{10,... | collective-permute-start | bytes 835592 | tf_op jit(solution)/shard_map/ppermute | solution.py:696
  96.6 23.2 %copy-start = (s32[2,1024]{1,0:T(2,128)S(1)}, s32[2,1024]{1,0:T(2,128)}, u32[]{:S(2)}) copy-start(s32[2,1024]{1,0:T(2,128)} %src_ref.3) | copy-start | bytes 24580
  96.6 4.7 %collective-permute-start.10 = (f32[32,128]{1,0:T(8,128)S(1)}, f32[32,128]{1,0:T(8,128)S(1)}, u32[]{:S(2)}, u32[]{:S(2)}) collective-permute-start(f32[32,128]{1,0:T(8,128)S(1)} %add.167), channel_id=1, source_target_pairs={{0,8},{1,9},{2,10},{3,11},{4,12},{5,13},{6,14},{7,15},{8,0},{9,1},... | collective-permute-start | bytes 49160 | tf_op jit(solution)/shard_map/ppermute | solution.py:696
  101.4 9.6 %collective-permute-start.12 = (bf16[4,544,128]{2,1,0:T(8,128)(2,1)S(1)}, bf16[4,544,128]{2,1,0:T(8,128)(2,1)S(1)}, u32[]{:S(2)}, u32[]{:S(2)}) collective-permute-start(bf16[4,544,128]{2,1,0:T(8,128)(2,1)S(1)} %pad_maximum_fusion.refs_1_), channel_id=1, source_target_pairs={{0,2},{1,3},{2,0},{3,1},{4,6},{5,7},{6,4},{7,5},{8,10},{9,11},{10,... | collective-permute-start | bytes 1671176 | tf_op jit(solution)/shard_map/ppermute | solution.py:696
  103.0 13.9 %collective-permute-start.11 = (bf16[4,544,128]{2,1,0:T(8,128)(2,1)S(1)}, bf16[4,544,128]{2,1,0:T(8,128)(2,1)S(1)}, u32[]{:S(2)}, u32[]{:S(2)}) collective-permute-start(bf16[4,544,128]{2,1,0:T(8,128)(2,1)S(1)} %pad_maximum_fusion.refs_1_), channel_id=1, source_target_pairs={{0,16},{16,0},{1,17},{17,1},{2,18},{18,2},{3,19},{19,3},{4,20},{20... | collective-permute-start | bytes 1671176 | tf_op jit(solution)/shard_map/ppermute | solution.py:689
  103.0 16.1 %collective-permute-start.14 = (bf16[4,544,128]{2,1,0:T(8,128)(2,1)S(1)}, bf16[4,544,128]{2,1,0:T(8,128)(2,1)S(1)}, u32[]{:S(2)}, u32[]{:S(2)}) collective-permute-start(bf16[4,544,128]{2,1,0:T(8,128)(2,1)S(1)} %pad_maximum_fusion.refs_1_), channel_id=1, source_target_pairs={{0,1},{1,0},{2,3},{3,2},{4,5},{5,4},{6,7},{7,6},{8,9},{9,8},{10,11... | collective-permute-start | bytes 1671176 | tf_op jit(solution)/shard_map/ppermute | solution.py:696
  103.3 13.7 %all-to-all-start.1 = ((bf16[16,32,128]{2,1,0:T(8,128)(2,1)}), bf16[16,32,128]{2,1,0:T(8,128)(2,1)S(1)}, u32[]{:S(2)}, u32[]{:S(2)}) async-start(bf16[16,32,128]{2,1,0:T(8,128)(2,1)} %get-tuple-element.106), calls=%async_computation.1 | async-start | bytes 262144 | tf_op jit(solution)/shard_map/all_to_all | solution.py:788
  108.8 1.2 collective-permute-start.13
  111.0 14.9 %collective-permute-start.17 = (bf16[4,544,128]{2,1,0:T(8,128)(2,1)S(1)}, bf16[4,544,128]{2,1,0:T(8,128)(2,1)S(1)}, u32[]{:S(2)}, u32[]{:S(2)}) collective-permute-start(bf16[4,544,128]{2,1,0:T(8,128)(2,1)S(1)} %collective-permute-done.12.refs_1_), channel_id=1, source_target_pairs={{0,1},{1,0},{2,3},{3,2},{4,5},{5,4},{6,7},{7,6},{8,9},{9,8},{10,11... | collective-permute-start | bytes 1671176 | tf_op jit(solution)/shard_map/ppermute | solution.py:696
  119.1 3.7 %collective-permute-start.15 = (bf16[4,544,128]{2,1,0:T(8,128)(2,1)S(1)}, bf16[4,544,128]{2,1,0:T(8,128)(2,1)S(1)}, u32[]{:S(2)}, u32[]{:S(2)}) collective-permute-start(bf16[4,544,128]{2,1,0:T(8,128)(2,1)S(1)} %collective-permute-done.12.refs_1_), channel_id=1, source_target_pairs={{0,16},{16,0},{1,17},{17,1},{2,18},{18,2},{3,19},{19,3},{4,20},{20... | collective-permute-start | bytes 1671176 | tf_op jit(solution)/shard_map/ppermute | solution.py:689
  119.2 3.7 %collective-permute-start.16 = (bf16[4,544,128]{2,1,0:T(8,128)(2,1)S(1)}, bf16[4,544,128]{2,1,0:T(8,128)(2,1)S(1)}, u32[]{:S(2)}, u32[]{:S(2)}) collective-permute-start(bf16[4,544,128]{2,1,0:T(8,128)(2,1)S(1)} %collective-permute-done.14.refs_3_), channel_id=1, source_target_pairs={{0,16},{16,0},{1,17},{17,1},{2,18},{18,2},{3,19},{19,3},{4,20},{20... | collective-permute-start | bytes 1671176 | tf_op jit(solution)/shard_map/ppermute | solution.py:689
  125.9 2.0 %collective-permute-start.18 = (bf16[4,544,128]{2,1,0:T(8,128)(2,1)S(1)}, bf16[4,544,128]{2,1,0:T(8,128)(2,1)S(1)}, u32[]{:S(2)}, u32[]{:S(2)}) collective-permute-start(bf16[4,544,128]{2,1,0:T(8,128)(2,1)S(1)} %collective-permute-done.17.refs_1_), channel_id=1, source_target_pairs={{0,16},{16,0},{1,17},{17,1},{2,18},{18,2},{3,19},{19,3},{4,20},{20... | collective-permute-start | bytes 1671176 | tf_op jit(solution)/shard_map/ppermute | solution.py:689
  (2 other events, 1.9 us)

commit v4 on v2

--- a/solution.py
+++ b/solution.py
@@ -11,7 +11,7 @@
 BF16 = jnp.bfloat16
 LANES = 128
 PIECE = 4
-GROUP = 12
+GROUP = 22
 MIB = 1024 * 1024
 
 

time: 129 us -> 128 us (level)
  waiting for transfers between devices: 35.4 us -> 31.3 us
  starting transfers between devices: 27.6 us -> 30.5 us
    ppermute x12, waiting for transfers between devices: 25.7 us -> 22.1 us  [swap(): return lax.ppermute(value, ('graph', 'edge'), moves)]
    pallas_call x1, Pallas kernels: 14.4 us -> 12.4 us  [first_grads(): full_call(back_kernel, (jax.ShapeDtypeStruct((batches, own, width), BF16)...]
    ppermute x12, starting transfers between devices: 14.4 us -> 16.4 us  [swap(): return lax.ppermute(value, ('graph', 'edge'), moves)]
  transfers between devices with their start and end apart: 21 -> 21, of which waited for: 13 -> 14; matrix products, arithmetic and copies ran while one was open for 6% -> 6% of each run, Pallas kernels for 22% -> 21%
where the time goes in v4:
time: 128 us; the launch traced here: 127 us
  Pallas kernels  51 us (40%)
  waiting for transfers between devices  31.3 us (24%)
  starting transfers between devices  30.5 us (24%)
  local copies, waits for them, and re-layouts  9.08 us (7%)
  other arithmetic  4.3 us (3%)
    ppermute x12, waiting for transfers between devices, swap(): return lax.ppermute(value, ('graph', 'edge'), moves)  22.1 us
    pallas_call x1, Pallas kernels, body(): full_call(main_kernel, (jax.ShapeDtypeStruct((batches * own, width), BF16...  19.3 us
    ppermute x12, starting transfers between devices, swap(): return lax.ppermute(value, ('graph', 'edge'), moves)  16.4 us
    pallas_call x1, Pallas kernels, first_grads(): full_call(back_kernel, (jax.ShapeDtypeStruct((batches, own, width), BF16)...  12.4 us
    all_to_all x1, starting transfers between devices, body(): edge_data = lax.all_to_all(sent, 'edge', 0, 0, tiled=True)  8.31 us
    pallas_call x4, Pallas kernels, place_pieces(): pl.pallas_call(functools.partial(place_kernel, tall, count, len(before)),...  7.43 us
    unnamed x11, local copies, waits for them, and re-layouts  7.39 us
    pallas_call x1, Pallas kernels, second_grads(): full_call(edge_kernel, (jax.ShapeDtypeStruct((blocks, batches * feat_coun...  6.79 us
  transfers between devices with their start and end apart: 21, of which 14 were waited for; matrix products, arithmetic and copies ran while one was open for 6% of the time, Pallas kernels for 21%

profile of v4, /device:TPU:0, one launch (start us, length us, event | category | flops | bytes accessed | tf_op | source)
XLA Modules:
  0.0 127.4 jit_solution(12678636877500576702)
XLA Ops:
  0.6 3.0 %shard_map.212 = bf16[16,48,128]{2,1,0:T(8,128)(2,1)} custom-call(s32[2,1024]{1,0:T(2,128)} %src_ref.3, s32[2,1024]{1,0:T(2,128)} %dst_ref.1, bf16[2,16,1024]{2,1,0:T(8,128)(2,1)} %feat_ref.1), custom_call_target="tpu_custom_call" | custom-call | tf_op jit(solution)/shard_map/pallas_call | solution.py:614
  3.7 8.3 %all-to-all-start = ((bf16[16,48,128]{2,1,0:T(8,128)(2,1)}), bf16[16,48,128]{2,1,0:T(8,128)(2,1)S(1)}, u32[]{:S(2)}, u32[]{:S(2)}) async-start(bf16[16,48,128]{2,1,0:T(8,128)(2,1)} %shard_map.212), calls=%async_computation | async-start | bytes 393216 | tf_op jit(solution)/shard_map/all_to_all | solution.py:619
  12.0 5.4 %copy.39 = bf16[16,8,128,128]{3,2,1,0:T(8,128)(2,1)} copy(bf16[16,8,128,128]{3,1,2,0:T(8,128)(2,1)} %bitcast.43) | data formatting | bytes 8388608
  18.1 2.6 %all-to-all-done.edge_ref = bf16[16,48,128]{2,1,0:T(8,128)(2,1)S(1)} async-done(((bf16[16,48,128]{2,1,0:T(8,128)(2,1)}), bf16[16,48,128]{2,1,0:T(8,128)(2,1)S(1)}, u32[]{:S(2)}, u32[]{:S(2)}) %all-to-all-start) | async-done | bytes 196640 | tf_op jit(solution)/shard_map/all_to_all | solution.py:619
  21.3 19.3 %shard_map.213 = (bf16[128,128]{1,0:T(8,128)(2,1)}, bf16[2,4,16,4352]{3,2,1,0:T(8,128)(2,1)}, bf16[2,4,16,4352]{3,2,1,0:T(8,128)(2,1)}, bf16[2,4,16,4352]{3,2,1,...) custom-call(s32[3]{0:T(128)} %pad_add_fusion.where_ref, ...), custom_call_target="tpu_custom_call" | custom-call | tf_op jit(solution)/shard_map/pallas_call | solution.py:645
  43.9 1.9 %collective-permute-start.2 = (bf16[2,4,16,4352]{3,2,1,0:T(8,128)(2,1)S(1)}, bf16[2,4,16,4352]{3,2,1,0:T(8,128)(2,1)}, u32[]{:S(2)}, u32[]{:S(2)}) collective-permute-start(bf16[2,4,16,4352]{3,2,1,0:T(8,128)(2,1)S(1)} %shard_map.215), channel_id=1, source_target_pairs={{0,1},{1,0},{2,3},{3,2},{4,5},{5,4},{6,7},{7,6},{8,9},{9,8},{10,11... | collective-permute-start | bytes 3342344 | tf_op jit(solution)/shard_map/ppermute | solution.py:696
  45.8 12.4 %shard_map.216 = (bf16[2,64,128]{2,1,0:T(8,128)(2,1)}, bf16[2,1056,512]{2,1,0:T(8,128)(2,1)}) custom-call(bf16[2,4224,128]{2,1,0:T(8,128)(2,1)} %get-tuple-element.81.g_far, bf16[128,256]{1,0:T(8,128)(2,1)} %get-tuple-element.82.level_ref, bf16[128,256]{1,0:T(8,128)(2,1)} %get-tuple-element.83.dm_ref, f32[128,128]{1,0:T(8,128)} %get-tuple-element.84.base_ref, ...), custom_call_target="tpu_custom_call" | custom-call | flops 12000000000 | bytes 36000000 | tf_op jit(solution)/shard_map/pallas_call | solution.py:711
  61.7 6.8 %shard_map.217 = (bf16[16,32,128]{2,1,0:T(8,128)(2,1)}, f32[32,128]{1,0:T(8,128)}) custom-call(s32[2,17]{1,0:T(2,128)} %get-tuple-element.89.order_ref, bf16[16,48,128]{2,1,0:T(8,128)(2,1)} %copy-done.3, bf16[2,1056,512]{2,1,0:T(8,128)(2,1)} %get-tuple-element.91.dg_ref, bf16[16,128]{1,0:T(8,128)(2,1)} %w_in_ref.3, f32[128]{0:T(128)} %b_in_ref.3, ...), custom_call_target="tpu_custom_call" | custom-call | flops 8999999488 | bytes 27000000 | tf_op jit(solution)/shard_map/pallas_call | solution.py:729
  68.5 1.9 %collective-permute-done.3 = bf16[2,2,16,4352]{3,2,1,0:T(8,128)(2,1)S(1)} collective-permute-done((bf16[2,2,16,4352]{3,2,1,0:T(8,128)(2,1)S(1)}, bf16[2,2,16,4352]{3,2,1,0:T(8,128)(2,1)S(1)}, u32[]{:S(2)}, u32[]{:S(2)}) %collective-permute-start.3) | collective-permute-done | bytes 557088 | tf_op jit(solution)/shard_map/ppermute | solution.py:696
  71.6 1.9 %collective-permute-start.4 = (bf16[2,16,4352]{2,1,0:T(8,128)(2,1)S(1)}, bf16[2,16,4352]{2,1,0:T(8,128)(2,1)S(1)}, u32[]{:S(2)}, u32[]{:S(2)}) collective-permute-start(bf16[2,16,4352]{2,1,0:T(8,128)(2,1)S(1)} %fusion.1), channel_id=1, source_target_pairs={{0,4},{1,5},{2,6},{3,7},{4,0},{5,1},{6,2},{7,3},{8,12},{9,13},{10,... | collective-permute-start | bytes 835592 | tf_op jit(solution)/shard_map/ppermute | solution.py:696
  73.7 4.7 %collective-permute-done.5 = f32[32,128]{1,0:T(8,128)S(1)} collective-permute-done((f32[32,128]{1,0:T(8,128)S(1)}, f32[32,128]{1,0:T(8,128)S(1)}, u32[]{:S(2)}, u32[]{:S(2)}) %collective-permute-start.5) | collective-permute-done | bytes 16416 | tf_op jit(solution)/shard_map/ppermute | solution.py:696
  80.9 2.0 %collective-permute-start.7 = (f32[32,128]{1,0:T(8,128)S(1)}, f32[32,128]{1,0:T(8,128)S(1)}, u32[]{:S(2)}, u32[]{:S(2)}) collective-permute-start(f32[32,128]{1,0:T(8,128)S(1)} %add.165), channel_id=1, source_target_pairs={{0,1},{1,0},{2,3},{3,2},{4,5},{5,4},{6,7},{7,6},{8,9},{9,8},{10,11... | collective-permute-start | bytes 49160 | tf_op jit(solution)/shard_map/ppermute | solution.py:696
  83.0 1.7 %collective-permute-done.7 = f32[32,128]{1,0:T(8,128)S(1)} collective-permute-done((f32[32,128]{1,0:T(8,128)S(1)}, f32[32,128]{1,0:T(8,128)S(1)}, u32[]{:S(2)}, u32[]{:S(2)}) %collective-permute-start.7) | collective-permute-done | bytes 16416 | tf_op jit(solution)/shard_map/ppermute | solution.py:696
  84.7 2.0 %collective-permute-start.8 = (f32[32,128]{1,0:T(8,128)S(1)}, f32[32,128]{1,0:T(8,128)S(1)}, u32[]{:S(2)}, u32[]{:S(2)}) collective-permute-start(f32[32,128]{1,0:T(8,128)S(1)} %add.166), channel_id=1, source_target_pairs={{0,2},{1,3},{2,0},{3,1},{4,6},{5,7},{6,4},{7,5},{8,10},{9,11},{10,... | collective-permute-start | bytes 49160 | tf_op jit(solution)/shard_map/ppermute | solution.py:696
  86.7 1.7 %collective-permute-done.8 = f32[32,128]{1,0:T(8,128)S(1)} collective-permute-done((f32[32,128]{1,0:T(8,128)S(1)}, f32[32,128]{1,0:T(8,128)S(1)}, u32[]{:S(2)}, u32[]{:S(2)}) %collective-permute-start.8) | collective-permute-done | bytes 16416 | tf_op jit(solution)/shard_map/ppermute | solution.py:696
  88.4 4.7 %collective-permute-done.6.second_ref = bf16[2,16,4352]{2,1,0:T(8,128)(2,1)S(1)} collective-permute-done((bf16[2,16,4352]{2,1,0:T(8,128)(2,1)S(1)}, bf16[2,16,4352]{2,1,0:T(8,128)(2,1)S(1)}, u32[]{:S(2)}, u32[]{:S(2)}) %collective-permute-start.6) | collective-permute-done | bytes 278560 | tf_op jit(solution)/shard_map/ppermute | solution.py:696
  93.6 2.4 %collective-permute-start.10 = (f32[32,128]{1,0:T(8,128)S(1)}, f32[32,128]{1,0:T(8,128)S(1)}, u32[]{:S(2)}, u32[]{:S(2)}) collective-permute-start(f32[32,128]{1,0:T(8,128)S(1)} %add.167), channel_id=1, source_target_pairs={{0,8},{1,9},{2,10},{3,11},{4,12},{5,13},{6,14},{7,15},{8,0},{9,1},... | collective-permute-start | bytes 49160 | tf_op jit(solution)/shard_map/ppermute | solution.py:696
  96.0 2.4 %collective-permute-done.10 = f32[32,128]{1,0:T(8,128)S(1)} collective-permute-done((f32[32,128]{1,0:T(8,128)S(1)}, f32[32,128]{1,0:T(8,128)S(1)}, u32[]{:S(2)}, u32[]{:S(2)}) %collective-permute-start.10) | collective-permute-done | bytes 16416 | tf_op jit(solution)/shard_map/ppermute | solution.py:696
  98.4 1.9 %collective-permute-done.9 = bf16[2,544,128]{2,1,0:T(8,128)(2,1)S(1)} collective-permute-done((bf16[2,544,128]{2,1,0:T(8,128)(2,1)S(1)}, bf16[2,544,128]{2,1,0:T(8,128)(2,1)S(1)}, u32[]{:S(2)}, u32[]{:S(2)}) %collective-permute-start.9) | collective-permute-done | bytes 278560 | tf_op jit(solution)/shard_map/ppermute | solution.py:696
  101.0 1.6 %collective-permute-start.14 = (bf16[4,544,128]{2,1,0:T(8,128)(2,1)S(1)}, bf16[4,544,128]{2,1,0:T(8,128)(2,1)S(1)}, u32[]{:S(2)}, u32[]{:S(2)}) collective-permute-start(bf16[4,544,128]{2,1,0:T(8,128)(2,1)S(1)} %pad_maximum_fusion.refs_1_), channel_id=1, source_target_pairs={{0,1},{1,0},{2,3},{3,2},{4,5},{5,4},{6,7},{7,6},{8,9},{9,8},{10,11... | collective-permute-start | bytes 1671176 | tf_op jit(solution)/shard_map/ppermute | solution.py:696
  102.6 4.5 %all-to-all-start.1 = ((bf16[16,32,128]{2,1,0:T(8,128)(2,1)}), bf16[16,32,128]{2,1,0:T(8,128)(2,1)S(1)}, u32[]{:S(2)}, u32[]{:S(2)}) async-start(bf16[16,32,128]{2,1,0:T(8,128)(2,1)} %get-tuple-element.108), calls=%async_computation.1 | async-start | bytes 262144 | tf_op jit(solution)/shard_map/all_to_all | solution.py:788
  111.4 3.7 %all-to-all-done.1 = bf16[16,32,128]{2,1,0:T(8,128)(2,1)S(1)} async-done(((bf16[16,32,128]{2,1,0:T(8,128)(2,1)}), bf16[16,32,128]{2,1,0:T(8,128)(2,1)S(1)}, u32[]{:S(2)}, u32[]{:S(2)}) %all-to-all-start.1) | async-done | bytes 131104 | tf_op jit(solution)/shard_map/all_to_all | solution.py:788
  115.0 2.1 %shard_map.219 = (f32[128,16384]{1,0:T(8,128)}, f32[128,128]{1,0:T(8,128)}, f32[128,384]{1,0:T(8,128)}, f32[128,384]{1,0:T(8,128)}, f32[128,128]{1,0:T(8,128)S(1)}) custom-call(s32[2]{0:T(128)S(1)} %pad_add_fusion.2.refs_0_, bf16[4,544,128]{2,1,0:T(8,128)(2,1)S(1)} %pad_maximum_fusion.refs_1_, bf16[4,544,128]{2,1,0:T(8,128)(2,1)S(1)} %collective-permute-done.11.refs_2_), custom_call_target="tpu_custom_call" | custom-call | flops 100000000 | bytes 300000 | tf_op jit(solution)/shard_map/pallas_call | solution.py:577
  120.9 3.1 %shard_map.220 = (f32[128,16384]{1,0:T(8,128)}, f32[128,128]{1,0:T(8,128)}, f32[128,384]{1,0:T(8,128)}, f32[128,384]{1,0:T(8,128)}, f32[128,128]{1,0:T(8,128)S(1)}) custom-call(s32[4]{0:T(128)S(1)} %pad_add_fusion.1.refs_0_, ...), custom_call_target="tpu_custom_call", output_to_operand_aliasing={{0}: (5, {}), {1}: (6, {}), {2}: (7, {}), {3}: (8, {}), {4}... | custom-call | flops 100000000 | bytes 300000 | tf_op jit(solution)/shard_map/pallas_call | solution.py:577
  (56 shorter events, 24.2 us)
Async XLA Ops:
  3.7 17.0 %all-to-all-start = ((bf16[16,48,128]{2,1,0:T(8,128)(2,1)}), bf16[16,48,128]{2,1,0:T(8,128)(2,1)S(1)}, u32[]{:S(2)}, u32[]{:S(2)}) async-start(bf16[16,48,128]{2,1,0:T(8,128)(2,1)} %shard_map.212), calls=%async_computation | async-start | bytes 393216 | tf_op jit(solution)/shard_map/all_to_all | solution.py:619
  40.6 3.0 %collective-permute-start = (bf16[2,4,16,4352]{3,2,1,0:T(8,128)(2,1)}, bf16[2,4,16,4352]{3,2,1,0:T(8,128)(2,1)S(1)}, u32[]{:S(2)}, u32[]{:S(2)}) collective-permute-start(bf16[2,4,16,4352]{3,2,1,0:T(8,128)(2,1)} %get-tuple-element.80), channel_id=1, source_target_pairs={{0,16},{16,0},{1,17},{17,1},{2,18},{18,2},{3,19},{19,3},{4,20},{20... | collective-permute-start | bytes 3342344 | tf_op jit(solution)/shard_map/ppermute | solution.py:689
  40.7 18.9 %collective-permute-start.1 = (bf16[2,4,16,4352]{3,2,1,0:T(8,128)(2,1)}, bf16[2,4,16,4352]{3,2,1,0:T(8,128)(2,1)S(1)}, u32[]{:S(2)}, u32[]{:S(2)}) collective-permute-start(bf16[2,4,16,4352]{3,2,1,0:T(8,128)(2,1)} %get-tuple-element.87), channel_id=1, source_target_pairs={{0,16},{16,0},{1,17},{17,1},{2,18},{18,2},{3,19},{19,3},{4,20},{20... | collective-permute-start | bytes 3342344 | tf_op jit(solution)/shard_map/ppermute | solution.py:689
  43.9 15.7 %collective-permute-start.2 = (bf16[2,4,16,4352]{3,2,1,0:T(8,128)(2,1)S(1)}, bf16[2,4,16,4352]{3,2,1,0:T(8,128)(2,1)}, u32[]{:S(2)}, u32[]{:S(2)}) collective-permute-start(bf16[2,4,16,4352]{3,2,1,0:T(8,128)(2,1)S(1)} %shard_map.215), channel_id=1, source_target_pairs={{0,1},{1,0},{2,3},{3,2},{4,5},{5,4},{6,7},{7,6},{8,9},{9,8},{10,11... | collective-permute-start | bytes 3342344 | tf_op jit(solution)/shard_map/ppermute | solution.py:696
  45.8 13.8 %copy-start.2 = (bf16[2,4,16,4352]{3,2,1,0:T(8,128)(2,1)S(1)}, bf16[2,4,16,4352]{3,2,1,0:T(8,128)(2,1)}, u32[]{:S(2)}) copy-start(bf16[2,4,16,4352]{3,2,1,0:T(8,128)(2,1)} %get-tuple-element.86) | copy-start | bytes 3342340
  60.9 9.6 %collective-permute-start.3 = (bf16[2,2,16,4352]{3,2,1,0:T(8,128)(2,1)S(1)}, bf16[2,2,16,4352]{3,2,1,0:T(8,128)(2,1)S(1)}, u32[]{:S(2)}, u32[]{:S(2)}) collective-permute-start(bf16[2,2,16,4352]{3,2,1,0:T(8,128)(2,1)S(1)} %fusion), channel_id=1, source_target_pairs={{0,2},{1,3},{2,0},{3,1},{4,6},{5,7},{6,4},{7,5},{8,10},{9,11},{10,... | collective-permute-start | bytes 1671176 | tf_op jit(solution)/shard_map/ppermute | solution.py:696
  68.5 4.9 %copy-start.4 = (f32[32,128]{1,0:T(8,128)S(1)}, f32[32,128]{1,0:T(8,128)}, u32[]{:S(2)}) copy-start(f32[32,128]{1,0:T(8,128)} %get-tuple-element.93) | copy-start | bytes 49156
  71.6 6.8 %collective-permute-start.4 = (bf16[2,16,4352]{2,1,0:T(8,128)(2,1)S(1)}, bf16[2,16,4352]{2,1,0:T(8,128)(2,1)S(1)}, u32[]{:S(2)}, u32[]{:S(2)}) collective-permute-start(bf16[2,16,4352]{2,1,0:T(8,128)(2,1)S(1)} %fusion.1), channel_id=1, source_target_pairs={{0,4},{1,5},{2,6},{3,7},{4,0},{5,1},{6,2},{7,3},{8,12},{9,13},{10,... | collective-permute-start | bytes 835592 | tf_op jit(solution)/shard_map/ppermute | solution.py:696
  73.4 4.9 %collective-permute-start.5 = (f32[32,128]{1,0:T(8,128)S(1)}, f32[32,128]{1,0:T(8,128)S(1)}, u32[]{:S(2)}, u32[]{:S(2)}) collective-permute-start(f32[32,128]{1,0:T(8,128)S(1)} %copy-done.4), channel_id=1, source_target_pairs={{0,4},{1,5},{2,6},{3,7},{4,0},{5,1},{6,2},{7,3},{8,12},{9,13},{10,... | collective-permute-start | bytes 49160 | tf_op jit(solution)/shard_map/ppermute | solution.py:696
  79.5 13.6 %collective-permute-start.6 = (bf16[2,16,4352]{2,1,0:T(8,128)(2,1)S(1)}, bf16[2,16,4352]{2,1,0:T(8,128)(2,1)S(1)}, u32[]{:S(2)}, u32[]{:S(2)}) collective-permute-start(bf16[2,16,4352]{2,1,0:T(8,128)(2,1)S(1)} %fusion.3.first_ref), channel_id=1, source_target_pairs={{0,8},{1,9},{2,10},{3,11},{4,12},{5,13},{6,14},{7,15},{8,0},{9,1},... | collective-permute-start | bytes 835592 | tf_op jit(solution)/shard_map/ppermute | solution.py:696
  80.9 3.7 %collective-permute-start.7 = (f32[32,128]{1,0:T(8,128)S(1)}, f32[32,128]{1,0:T(8,128)S(1)}, u32[]{:S(2)}, u32[]{:S(2)}) collective-permute-start(f32[32,128]{1,0:T(8,128)S(1)} %add.165), channel_id=1, source_target_pairs={{0,1},{1,0},{2,3},{3,2},{4,5},{5,4},{6,7},{7,6},{8,9},{9,8},{10,11... | collective-permute-start | bytes 49160 | tf_op jit(solution)/shard_map/ppermute | solution.py:696
  84.7 3.7 %collective-permute-start.8 = (f32[32,128]{1,0:T(8,128)S(1)}, f32[32,128]{1,0:T(8,128)S(1)}, u32[]{:S(2)}, u32[]{:S(2)}) collective-permute-start(f32[32,128]{1,0:T(8,128)S(1)} %add.166), channel_id=1, source_target_pairs={{0,2},{1,3},{2,0},{3,1},{4,6},{5,7},{6,4},{7,5},{8,10},{9,11},{10,... | collective-permute-start | bytes 49160 | tf_op jit(solution)/shard_map/ppermute | solution.py:696
  93.5 6.8 %collective-permute-start.9 = (bf16[2,544,128]{2,1,0:T(8,128)(2,1)S(1)}, bf16[2,544,128]{2,1,0:T(8,128)(2,1)S(1)}, u32[]{:S(2)}, u32[]{:S(2)}) collective-permute-start(bf16[2,544,128]{2,1,0:T(8,128)(2,1)S(1)} %shard_map.218), channel_id=1, source_target_pairs={{0,4},{1,5},{2,6},{3,7},{4,0},{5,1},{6,2},{7,3},{8,12},{9,13},{10,... | collective-permute-start | bytes 835592 | tf_op jit(solution)/shard_map/ppermute | solution.py:696
  93.6 24.3 %copy-start = (s32[2,1024]{1,0:T(2,128)S(1)}, s32[2,1024]{1,0:T(2,128)}, u32[]{:S(2)}) copy-start(s32[2,1024]{1,0:T(2,128)} %src_ref.3) | copy-start | bytes 24580
  93.6 4.8 %collective-permute-start.10 = (f32[32,128]{1,0:T(8,128)S(1)}, f32[32,128]{1,0:T(8,128)S(1)}, u32[]{:S(2)}, u32[]{:S(2)}) collective-permute-start(f32[32,128]{1,0:T(8,128)S(1)} %add.167), channel_id=1, source_target_pairs={{0,8},{1,9},{2,10},{3,11},{4,12},{5,13},{6,14},{7,15},{8,0},{9,1},... | collective-permute-start | bytes 49160 | tf_op jit(solution)/shard_map/ppermute | solution.py:696
  100.3 9.7 %collective-permute-start.12 = (bf16[4,544,128]{2,1,0:T(8,128)(2,1)S(1)}, bf16[4,544,128]{2,1,0:T(8,128)(2,1)S(1)}, u32[]{:S(2)}, u32[]{:S(2)}) collective-permute-start(bf16[4,544,128]{2,1,0:T(8,128)(2,1)S(1)} %pad_maximum_fusion.refs_1_), channel_id=1, source_target_pairs={{0,2},{1,3},{2,0},{3,1},{4,6},{5,7},{6,4},{7,5},{8,10},{9,11},{10,... | collective-permute-start | bytes 1671176 | tf_op jit(solution)/shard_map/ppermute | solution.py:696
  101.0 14.0 %collective-permute-start.11 = (bf16[4,544,128]{2,1,0:T(8,128)(2,1)S(1)}, bf16[4,544,128]{2,1,0:T(8,128)(2,1)S(1)}, u32[]{:S(2)}, u32[]{:S(2)}) collective-permute-start(bf16[4,544,128]{2,1,0:T(8,128)(2,1)S(1)} %pad_maximum_fusion.refs_1_), channel_id=1, source_target_pairs={{0,16},{16,0},{1,17},{17,1},{2,18},{18,2},{3,19},{19,3},{4,20},{20... | collective-permute-start | bytes 1671176 | tf_op jit(solution)/shard_map/ppermute | solution.py:689
  101.0 16.2 %collective-permute-start.14 = (bf16[4,544,128]{2,1,0:T(8,128)(2,1)S(1)}, bf16[4,544,128]{2,1,0:T(8,128)(2,1)S(1)}, u32[]{:S(2)}, u32[]{:S(2)}) collective-permute-start(bf16[4,544,128]{2,1,0:T(8,128)(2,1)S(1)} %pad_maximum_fusion.refs_1_), channel_id=1, source_target_pairs={{0,1},{1,0},{2,3},{3,2},{4,5},{5,4},{6,7},{7,6},{8,9},{9,8},{10,11... | collective-permute-start | bytes 1671176 | tf_op jit(solution)/shard_map/ppermute | solution.py:696
  102.6 12.4 %all-to-all-start.1 = ((bf16[16,32,128]{2,1,0:T(8,128)(2,1)}), bf16[16,32,128]{2,1,0:T(8,128)(2,1)S(1)}, u32[]{:S(2)}, u32[]{:S(2)}) async-start(bf16[16,32,128]{2,1,0:T(8,128)(2,1)} %get-tuple-element.108), calls=%async_computation.1 | async-start | bytes 262144 | tf_op jit(solution)/shard_map/all_to_all | solution.py:788
  107.2 1.2 collective-permute-start.13
  110.0 14.0 %collective-permute-start.17 = (bf16[4,544,128]{2,1,0:T(8,128)(2,1)S(1)}, bf16[4,544,128]{2,1,0:T(8,128)(2,1)S(1)}, u32[]{:S(2)}, u32[]{:S(2)}) collective-permute-start(bf16[4,544,128]{2,1,0:T(8,128)(2,1)S(1)} %collective-permute-done.12.refs_1_), channel_id=1, source_target_pairs={{0,1},{1,0},{2,3},{3,2},{4,5},{5,4},{6,7},{7,6},{8,9},{9,8},{10,11... | collective-permute-start | bytes 1671176 | tf_op jit(solution)/shard_map/ppermute | solution.py:696
  117.2 3.8 %collective-permute-start.15 = (bf16[4,544,128]{2,1,0:T(8,128)(2,1)S(1)}, bf16[4,544,128]{2,1,0:T(8,128)(2,1)S(1)}, u32[]{:S(2)}, u32[]{:S(2)}) collective-permute-start(bf16[4,544,128]{2,1,0:T(8,128)(2,1)S(1)} %collective-permute-done.12.refs_1_), channel_id=1, source_target_pairs={{0,16},{16,0},{1,17},{17,1},{2,18},{18,2},{3,19},{19,3},{4,20},{20... | collective-permute-start | bytes 1671176 | tf_op jit(solution)/shard_map/ppermute | solution.py:689
  117.3 3.7 %collective-permute-start.16 = (bf16[4,544,128]{2,1,0:T(8,128)(2,1)S(1)}, bf16[4,544,128]{2,1,0:T(8,128)(2,1)S(1)}, u32[]{:S(2)}, u32[]{:S(2)}) collective-permute-start(bf16[4,544,128]{2,1,0:T(8,128)(2,1)S(1)} %collective-permute-done.14.refs_3_), channel_id=1, source_target_pairs={{0,16},{16,0},{1,17},{17,1},{2,18},{18,2},{3,19},{19,3},{4,20},{20... | collective-permute-start | bytes 1671176 | tf_op jit(solution)/shard_map/ppermute | solution.py:689
  124.0 2.0 %collective-permute-start.18 = (bf16[4,544,128]{2,1,0:T(8,128)(2,1)S(1)}, bf16[4,544,128]{2,1,0:T(8,128)(2,1)S(1)}, u32[]{:S(2)}, u32[]{:S(2)}) collective-permute-start(bf16[4,544,128]{2,1,0:T(8,128)(2,1)S(1)} %collective-permute-done.17.refs_1_), channel_id=1, source_target_pairs={{0,16},{16,0},{1,17},{17,1},{2,18},{18,2},{3,19},{19,3},{4,20},{20... | collective-permute-start | bytes 1671176 | tf_op jit(solution)/shard_map/ppermute | solution.py:689
  (2 other events, 1.9 us)
